TPU v7x, 32 devices: a whole 2x2x4 slice. The times are simulated.
32 devices in a mesh: days: 2 (over y), chan: 4 (over z), tm: 2 (over x), freq: 2 (over core).
Axes of the slice: x: 2, y: 2, z: 4, core: 2. Of those that a mesh axis runs over, the one named last changes fastest.
Arguments:
- recording: bfloat16 [2048, 2048], P(('days', 'chan', 'freq'), 'tm'), parts along dimension 0, may hold values from -6 to 6
- trailing: bfloat16 [2048, 1024], P(('days', 'chan', 'freq')), parts along dimension 0, may hold values from -6 to 6
- whiten_filter: bfloat16 [1024, 64], P(('chan', 'freq')), may hold values from -0.75 to 0.75
- pair_list: int32 [8, 4], P(('days', 'chan')), parts along dimension 0, may hold values from -1 to 3, as said below
Outputs:
- cross_spectra: float32 [8, 4, 4, 2, 256, 256], P(('days', 'chan'), None, ('tm', 'freq')), parts along dimension 0
There are 2 independent parts, one for each index of `days`. A program takes and returns all parts, laid end to end along the dimension named above; an argument that names none is the same for every part. Nothing has to cross between parts.
Inputs may be any that keep to these rules, and one draw needn't show every extreme that they name: `pair_list`: row a lists in its first slots distinct blocks b with |b - a| <= 3, then -1 in the remaining slots; every row lists at least one block, and some row of every draw fills all 4 slots.
All inputs are finite; a program needn't handle non-finite values.
Results may differ from a plain program's by a relative error of at most 0.0046.
Values may be sent and summed in bfloat16 or wider, within the bound.
No kernel may reach another device: no remote copies, remote signals or barrier semaphores. Data moves between devices by JAX's collectives and lax.ppermute only.
A program may use at most 64 MiB of HBM per device.

v0:
```python
import math

import jax
import jax.numpy as jnp
from jax import lax
from jax.sharding import PartitionSpec as P

FB = 512
REACH = 3
SLOTS = 4


def shifted(block, axis, distance):
    devices = range(lax.axis_size(axis))
    route = [(i - distance, i) for i in devices if i - distance in devices]
    return lax.ppermute(block, axis, route)


def extended(value, sides, width):
    for axis, dim in sides:
        size, length = (lax.axis_size(axis), value.shape[dim])
        up = [(i, (i + 1) % size) for i in range(size - 1)]
        down = [(j, i) for i, j in up]
        last = lax.slice_in_dim(value, length - width, length, axis=dim)
        initial = lax.slice_in_dim(value, 0, width, axis=dim)
        before = lax.ppermute(last, axis, up)
        after = lax.ppermute(initial, axis, down)
        value = jnp.concatenate([before, value, after], axis=dim)
    return value


def fourier_table(first_bin, bin_count, length):
    samples = jnp.arange(length, dtype=jnp.int32)[:, None]
    bin_index = first_bin + jnp.arange(bin_count, dtype=jnp.int32)[None, :]
    phase = samples * bin_index % length
    angle = 2.0 * math.pi / length * phase.astype(jnp.float32)
    taper = 0.5 - 0.5 * jnp.cos(
        2.0 * math.pi / length * jnp.arange(length, dtype=jnp.int32).astype(jnp.float32)
    )
    normaliser = 1.0 / math.sqrt(0.375 * length)
    cosine = (taper[:, None] * jnp.cos(angle) * normaliser).astype(jnp.bfloat16)
    sine_table = (-taper[:, None] * jnp.sin(angle) * normaliser).astype(jnp.bfloat16)
    return (cosine, sine_table)


def local(recording, trailing, whiten_filter, pair_list):
    local_rows, local_span = recording.shape
    hop_size = trailing.shape[1]
    window_size = 2 * hop_size
    segment_count = local_span // hop_size
    following = shifted(recording, "tm", -1)
    is_last = lax.axis_index("tm") == lax.axis_size("tm") - 1
    following = jnp.where(is_last, trailing, following)
    signal = jnp.concatenate([recording, following], axis=1)
    segments = jnp.stack([signal], axis=1)
    stacked_segments = segments.reshape(local_rows * segment_count, window_size)
    bin_step = min(256, FB)
    real_bins = []
    imag_bins = []
    for first_bin in range(0, FB, bin_step):
        cosine, sine_table = fourier_table(first_bin, bin_step, window_size)
        joined = jnp.concatenate([cosine, sine_table], axis=1)
        product = jnp.dot(stacked_segments, joined, preferred_element_type=jnp.float32).astype(
            jnp.bfloat16
        )
        real_bins.append(product[:, :bin_step])
        imag_bins.append(product[:, bin_step:])
    real_spec = jnp.concatenate(real_bins, axis=1)
    imag_spec = jnp.concatenate(imag_bins, axis=1)
    raw_spectra = jnp.stack([real_spec, imag_spec])
    tap_count = whiten_filter.shape[1]
    rim_width = tap_count // 2
    offset = (
        jnp.arange(local_rows + tap_count, dtype=jnp.int32)[None, :]
        - jnp.arange(local_rows, dtype=jnp.int32)[:, None]
    )
    inside = (offset >= 0) & (offset < tap_count)
    picked_weights = jnp.take_along_axis(whiten_filter, jnp.clip(offset, 0, tap_count - 1), axis=1)
    band_matrix = jnp.where(inside, picked_weights, jnp.zeros((), whiten_filter.dtype))
    padded = extended(raw_spectra, ((("chan", "freq"), 1),), rim_width)
    predicted = jnp.einsum("ij,ajk->aik", band_matrix, padded, preferred_element_type=jnp.float32)
    whitened = (raw_spectra.astype(jnp.float32) - predicted).astype(jnp.bfloat16)
    spectra = whitened.reshape(2, local_rows, segment_count, FB)
    tm_count = lax.axis_size("tm")
    freq_count = lax.axis_size("freq")
    pieces = lax.all_to_all(spectra[None], ("tm", "freq"), split_axis=4, concat_axis=0, tiled=True)
    band_width = pieces.shape[-1]
    pieces = pieces.reshape(tm_count, freq_count, 2, local_rows, segment_count, band_width)
    banded = pieces.transpose(2, 1, 3, 0, 4, 5).reshape(
        2, freq_count * local_rows, tm_count * segment_count, band_width
    )
    block_rows = banded.shape[1]
    own_block = banded.reshape(2, block_rows, -1)
    depth = own_block.shape[2]
    scaling = 1.0 / math.sqrt(depth)
    block_index = lax.axis_index("chan")
    slot_list = pair_list[0]
    nearby = []
    for distance in range(-REACH, REACH + 1):
        if distance == 0:
            nearby.append(own_block)
        else:
            nearby.append(shifted(own_block, "chan", -distance))
    stacked = jnp.stack(nearby)

    def fetch_partner(partner_index):
        return lax.dynamic_index_in_dim(
            stacked, partner_index - block_index + REACH, 0, keepdims=False
        )

    left_side = jnp.concatenate([own_block[0], own_block[1]], axis=1)
    flipped = jnp.concatenate([own_block[1], -own_block[0]], axis=1)
    contract = (((1,), (1,)), ((), ()))

    def one_slot(partner_index):
        partner = fetch_partner(partner_index)
        right_side = jnp.concatenate([partner[0], partner[1]], axis=1)
        real_part = (
            lax.dot_general(left_side, right_side, contract, preferred_element_type=jnp.float32)
            * scaling
        )
        imag_part = (
            lax.dot_general(flipped, right_side, contract, preferred_element_type=jnp.float32)
            * scaling
        )
        crossed = jnp.stack([real_part, imag_part])
        return jnp.where(partner_index >= 0, crossed, jnp.zeros((), jnp.float32))

    result = jnp.stack([one_slot(slot_list[slot_index]) for slot_index in range(SLOTS)])
    return result.reshape(1, SLOTS, 1, 2, block_rows, block_rows)


def solution(mesh):
    placed = (
        P(("days", "chan", "freq"), "tm"),
        P(("days", "chan", "freq"), None),
        P(("chan", "freq"), None),
        P(("days", "chan"), None),
    )
    return jax.shard_map(
        local,
        mesh=mesh,
        in_specs=placed,
        out_specs=P(("days", "chan"), None, ("tm", "freq"), None, None, None),
        check_vma=False,
    )
```

profile of v0, /device:TPU:0, one launch (start us, length us, event | category | flops | bytes accessed | tf_op | source)
XLA Modules:
  0.0 278.5 jit_solution(4303380736802716633)
XLA Ops:
  0.0 1.4 collective-permute-start
  1.4 0.1 fusion.64
  1.5 0.1 multiply_subtract_fusion
  1.5 0.0 copy-start.1
  1.6 19.2 %multiply_convert_fusion.2 = (bf16[2048,256]{1,0:T(8,128)(2,1)S(1)}, bf16[2048,256]{1,0:T(8,128)(2,1)S(1)}, bf16[2048,256]{1,0:T(8,128)(2,1)S(1)}, bf16[2048,256]{1,0:T(8,128)(2,1)}) fusion(f32[2048]{0:T(1024)S(1)} %fusion.64, s32[256]{0:T(256)S(1)} %iota_add_fusion, f32[2048]{0:T(1024)S(1)} %multiply_subtract_fusion), kind=kLoop, calls=%fused_computation.26 | loop fusion | flops 20971520 | bytes 4211712 | tf_op jit(solution)/shard_map/convert_element_type | solution.py:42
  20.7 0.0 collective-permute-done
  20.7 1.0 broadcast_select_fusion
  21.7 0.0 copy-start.3
  21.7 1.8 fusion.34
  23.6 0.5 fusion.31
  24.1 2.4 collective-permute-start.1
  26.5 1.3 collective-permute-start.2
  27.8 0.1 fusion.46
  27.8 0.1 reshape.222
  28.0 195.9 %gather_fusion = bf16[24576]{0:T(1024)(128)(2,1)S(1)} fusion(bf16[128,64]{0,1:T(8,128)(2,1)S(1)} %copy-done, s32[24576]{0:T(1024)S(1)} %reshape.222), kind=kCustom, calls=%fused_computation | custom fusion | bytes 294912 | tf_op jit(solution)/shard_map/jit(take_along_axis)/gather | solution.py:78
  223.8 0.0 copy-start.2
  223.8 0.1 reshape.225
  224.0 0.0 collective-permute-done.1
  224.0 0.2 fusion.22
  224.2 0.9 copy.28
  225.1 6.6 %all-to-all-start = ((bf16[1,2,128,1,512]{2,1,3,0,4:T(2,128)(2,1)}), bf16[1,2,128,1,512]{2,1,3,0,4:T(2,128)(2,1)S(1)}, u32[]{:S(2)}, u32[]{:S(2)}) async-start(bf16[1,2,128,1,512]{2,1,3,0,4:T(2,128)(2,1)} %copy.28), calls=%async_computation | async-start | bytes 524288 | tf_op jit(solution)/shard_map/all_to_all | solution.py:86
  231.7 0.7 fusion.84
  237.5 0.5 all-to-all-done
  238.1 0.2 copy.30
  238.3 0.3 copy.33
  238.6 0.2 reshape_reshape.3
  238.7 5.6 %collective-permute-start.3 = (bf16[2,256,256]{2,1,0:T(8,128)(2,1)S(1)}, bf16[2,256,256]{2,1,0:T(8,128)(2,1)S(1)}, u32[]{:S(2)}, u32[]{:S(2)}) collective-permute-start(bf16[2,256,256]{2,1,0:T(8,128)(2,1)S(1)} %reshape_reshape.3), channel_id=1, source_target_pairs={{0,12},{1,13},{2,14},{3,15},{16,28},{17,29},{18,30},{19,31}} | collective-permute-start | bytes 786440 | tf_op jit(solution)/shard_map/ppermute | solution.py:16
  244.4 1.3 collective-permute-start.4
  245.7 2.5 collective-permute-start.5
  248.2 1.3 collective-permute-start.6
  249.4 1.3 collective-permute-start.7
  250.8 0.1 copy.31
  251.0 0.1 copy.32
  251.1 0.2 stack_reshape_reshape.3
  251.3 1.3 collective-permute-start.8
  252.7 4.0 %collective-permute-done.4 = bf16[2,256,256]{2,1,0:T(8,128)(2,1)S(1)} collective-permute-done((bf16[2,256,256]{2,1,0:T(8,128)(2,1)S(1)}, bf16[2,256,256]{2,1,0:T(8,128)(2,1)S(1)}, u32[]{:S(2)}, u32[]{:S(2)}) %collective-permute-start.4) | collective-permute-done | bytes 262176 | tf_op jit(solution)/shard_map/ppermute | solution.py:16
  256.7 5.0 %collective-permute-done.5 = bf16[2,256,256]{2,1,0:T(8,128)(2,1)S(1)} collective-permute-done((bf16[2,256,256]{2,1,0:T(8,128)(2,1)S(1)}, bf16[2,256,256]{2,1,0:T(8,128)(2,1)S(1)}, u32[]{:S(2)}, u32[]{:S(2)}) %collective-permute-start.5) | collective-permute-done | bytes 262176 | tf_op jit(solution)/shard_map/ppermute | solution.py:16
  261.8 12.8 %collective-permute-done.7 = bf16[2,256,256]{2,1,0:T(8,128)(2,1)S(1)} collective-permute-done((bf16[2,256,256]{2,1,0:T(8,128)(2,1)S(1)}, bf16[2,256,256]{2,1,0:T(8,128)(2,1)S(1)}, u32[]{:S(2)}, u32[]{:S(2)}) %collective-permute-start.7) | collective-permute-done | bytes 262176 | tf_op jit(solution)/shard_map/ppermute | solution.py:16
  274.6 0.1 dynamic-slice_bitcast_fusion.7
  274.7 0.3 fusion.30
  275.0 0.3 fusion.29
  275.3 0.3 fusion.28
  275.5 0.3 fusion.27
  275.8 0.3 fusion.26
  276.1 0.3 fusion.25
  276.4 0.3 fusion.24
  276.6 0.3 fusion.23
  277.1 1.5 maximum_bitcast_fusion
  (31 shorter events, 0.5 us)
Async XLA Ops:
  0.0 27.9 %copy-start = (bf16[128,64]{0,1:T(8,128)(2,1)S(1)}, bf16[128,64]{0,1:T(8,128)(2,1)}, u32[]{:S(2)}) copy-start(bf16[128,64]{0,1:T(8,128)(2,1)} %param.6) | copy-start | bytes 49156
  0.0 20.7 %collective-permute-start = (bf16[128,1024]{1,0:T(8,128)(2,1)}, bf16[128,1024]{1,0:T(8,128)(2,1)}, u32[]{:S(2)}, u32[]{:S(2)}) collective-permute-start(bf16[128,1024]{1,0:T(8,128)(2,1)} %param.4), channel_id=1, source_target_pairs={{2,0},{3,1},{6,4},{7,5},{10,8},{11,9},{14,12},{15,13},{18,16},{19,... | collective-permute-start | bytes 786440 | tf_op jit(solution)/shard_map/ppermute | solution.py:16
  1.5 19.2 %copy-start.1 = (bf16[128,1024]{1,0:T(8,128)(2,1)S(1)}, bf16[128,1024]{1,0:T(8,128)(2,1)}, u32[]{:S(2)}) copy-start(bf16[128,1024]{1,0:T(8,128)(2,1)} %param.5) | copy-start | bytes 786436
  21.7 1.8 copy-start.3
  24.1 199.8 %collective-permute-start.1 = (bf16[2,32,512]{2,1,0:T(8,128)(2,1)S(1)}, bf16[2,32,512]{2,1,0:T(8,128)(2,1)S(1)}, u32[]{:S(2)}, u32[]{:S(2)}) collective-permute-start(bf16[2,32,512]{2,1,0:T(8,128)(2,1)S(1)} %get-tuple-element.15), channel_id=1, source_target_pairs={{0,1},{1,4},{4,5},{5,8},{8,9},{9,12},{12,13},{2,3},{3,6},{6,7},{7,... | collective-permute-start | bytes 196616 | tf_op jit(solution)/shard_map/ppermute | solution.py:26
  26.5 197.5 %collective-permute-start.2 = (bf16[2,32,512]{2,1,0:T(8,128)(2,1)S(1)}, bf16[2,32,512]{2,1,0:T(8,128)(2,1)S(1)}, u32[]{:S(2)}, u32[]{:S(2)}) collective-permute-start(bf16[2,32,512]{2,1,0:T(8,128)(2,1)S(1)} %get-tuple-element.16), channel_id=1, source_target_pairs={{1,0},{4,1},{5,4},{8,5},{9,8},{12,9},{13,12},{3,2},{6,3},{7,6},{10... | collective-permute-start | bytes 196616 | tf_op jit(solution)/shard_map/ppermute | solution.py:27
  223.8 7.8 %copy-start.2 = (s32[1,4]{1,0:T(1,128)S(1)}, s32[1,4]{1,0:T(1,128)}, u32[]{:S(2)}) copy-start(s32[1,4]{1,0:T(1,128)} %param.7) | copy-start | bytes 52
  225.1 13.0 %all-to-all-start = ((bf16[1,2,128,1,512]{2,1,3,0,4:T(2,128)(2,1)}), bf16[1,2,128,1,512]{2,1,3,0,4:T(2,128)(2,1)S(1)}, u32[]{:S(2)}, u32[]{:S(2)}) async-start(bf16[1,2,128,1,512]{2,1,3,0,4:T(2,128)(2,1)} %copy.28), calls=%async_computation | async-start | bytes 524288 | tf_op jit(solution)/shard_map/all_to_all | solution.py:86
  238.7 12.6 %collective-permute-start.3 = (bf16[2,256,256]{2,1,0:T(8,128)(2,1)S(1)}, bf16[2,256,256]{2,1,0:T(8,128)(2,1)S(1)}, u32[]{:S(2)}, u32[]{:S(2)}) collective-permute-start(bf16[2,256,256]{2,1,0:T(8,128)(2,1)S(1)} %reshape_reshape.3), channel_id=1, source_target_pairs={{0,12},{1,13},{2,14},{3,15},{16,28},{17,29},{18,30},{19,31}} | collective-permute-start | bytes 786440 | tf_op jit(solution)/shard_map/ppermute | solution.py:16
  244.4 12.3 %collective-permute-start.4 = (bf16[2,256,256]{2,1,0:T(8,128)(2,1)S(1)}, bf16[2,256,256]{2,1,0:T(8,128)(2,1)S(1)}, u32[]{:S(2)}, u32[]{:S(2)}) collective-permute-start(bf16[2,256,256]{2,1,0:T(8,128)(2,1)S(1)} %reshape_reshape.3), channel_id=1, source_target_pairs={{0,8},{4,12},{1,9},{5,13},{2,10},{6,14},{3,11},{7,15},{16,24},{20,... | collective-permute-start | bytes 786440 | tf_op jit(solution)/shard_map/ppermute | solution.py:16
  245.7 16.0 %collective-permute-start.5 = (bf16[2,256,256]{2,1,0:T(8,128)(2,1)S(1)}, bf16[2,256,256]{2,1,0:T(8,128)(2,1)S(1)}, u32[]{:S(2)}, u32[]{:S(2)}) collective-permute-start(bf16[2,256,256]{2,1,0:T(8,128)(2,1)S(1)} %reshape_reshape.3), channel_id=1, source_target_pairs={{0,4},{4,8},{8,12},{1,5},{5,9},{9,13},{2,6},{6,10},{10,14},{3,7},{... | collective-permute-start | bytes 786440 | tf_op jit(solution)/shard_map/ppermute | solution.py:16
  248.2 13.6 %collective-permute-start.6 = (bf16[2,256,256]{2,1,0:T(8,128)(2,1)S(1)}, bf16[2,256,256]{2,1,0:T(8,128)(2,1)S(1)}, u32[]{:S(2)}, u32[]{:S(2)}) collective-permute-start(bf16[2,256,256]{2,1,0:T(8,128)(2,1)S(1)} %reshape_reshape.3), channel_id=1, source_target_pairs={{4,0},{8,4},{12,8},{5,1},{9,5},{13,9},{6,2},{10,6},{14,10},{7,3},{... | collective-permute-start | bytes 786440 | tf_op jit(solution)/shard_map/ppermute | solution.py:16
  249.4 25.1 %collective-permute-start.7 = (bf16[2,256,256]{2,1,0:T(8,128)(2,1)S(1)}, bf16[2,256,256]{2,1,0:T(8,128)(2,1)S(1)}, u32[]{:S(2)}, u32[]{:S(2)}) collective-permute-start(bf16[2,256,256]{2,1,0:T(8,128)(2,1)S(1)} %reshape_reshape.3), channel_id=1, source_target_pairs={{8,0},{12,4},{9,1},{13,5},{10,2},{14,6},{11,3},{15,7},{24,16},{28,... | collective-permute-start | bytes 786440 | tf_op jit(solution)/shard_map/ppermute | solution.py:16
  251.3 23.3 %collective-permute-start.8 = (bf16[2,256,256]{2,1,0:T(8,128)(2,1)S(1)}, bf16[2,256,256]{2,1,0:T(8,128)(2,1)S(1)}, u32[]{:S(2)}, u32[]{:S(2)}) collective-permute-start(bf16[2,256,256]{2,1,0:T(8,128)(2,1)S(1)} %reshape_reshape.3), channel_id=1, source_target_pairs={{12,0},{13,1},{14,2},{15,3},{28,16},{29,17},{30,18},{31,19}} | collective-permute-start | bytes 786440 | tf_op jit(solution)/shard_map/ppermute | solution.py:16
where the time goes:
time: 279 us
  local copies, waits for them, and re-layouts  199 us (71%)
  starting transfers between devices  24.9 us (9%)
  waiting for transfers between devices  22.4 us (8%)
  other arithmetic  22 us (8%)
  between operations  5.63 us (2%)
  matrix products  4.59 us (2%)
    gather x3, local copies, waits for them, and re-layouts, local(): jnp.take_along_axis(whiten_filter, jnp.clip(offset, 0, tap_count - 1), ax...  196 us
    ppermute x7, waiting for transfers between devices, shifted(): return lax.ppermute(block, axis, route)  21.8 us
    convert_element_type x1, other arithmetic, fourier_table(): (-taper[:, None] * jnp.sin(angle) * normaliser).astype(jnp.bfloat16)  19.2 us
    ppermute x7, starting transfers between devices, shifted(): return lax.ppermute(block, axis, route)  14.7 us
    all_to_all x1, starting transfers between devices, local(): lax.all_to_all(spectra[None], ('tm', 'freq'), split_axis=4, concat_axis=0...  6.59 us
  transfers between devices with their start and end apart: 10, of which 4 were waited for; matrix products, arithmetic and copies ran while one was open for 78% of the time, Pallas kernels for 0%

commit v1 on v0

v1 whole, which is shorter than its diff:
```python
import functools
import math

import jax
import jax.numpy as jnp
import ml_dtypes
import numpy as np
from jax import lax
from jax.experimental import pallas as pl
from jax.experimental.pallas import tpu as pltpu
from jax.sharding import PartitionSpec as P

FB = 512
REACH = 3
SLOTS = 4
LANES = 128


def band_tables(bands, length):
    samples = np.arange(length, dtype=np.int64)[:, None]
    bins = np.arange(FB, dtype=np.int64)[None, :]
    phase = (samples * bins % length).astype(np.float32)
    angle = np.float32(2.0 * math.pi / length) * phase
    ramp = np.float32(2.0 * math.pi / length) * np.arange(length, dtype=np.float32)
    taper = (np.float32(0.5) - np.float32(0.5) * np.cos(ramp))[:, None]
    normaliser = np.float32(1.0 / math.sqrt(0.375 * length))
    cosine = (taper * np.cos(angle) * normaliser).astype(ml_dtypes.bfloat16)
    sine = (-taper * np.sin(angle) * normaliser).astype(ml_dtypes.bfloat16)
    both = np.stack([cosine, sine], axis=1).reshape(length, 2, bands, FB // bands)
    return np.ascontiguousarray(both.transpose(2, 0, 1, 3)).reshape(bands, length, 2 * FB // bands)


def swapped(value, axis):
    return lax.ppermute(value, axis, [(0, 1), (1, 0)])


def transform_kernel(span_count, *refs):
    own, other = refs[: span_count + 1], refs[span_count + 1 : 2 * span_count + 2]
    table, out, signal = refs[2 * span_count + 2 :]
    span, half = lax.axis_index("tm"), lax.axis_index("freq")
    rows, hop = own[0].shape
    for group, which in ((own, half), (other, 1 - half)):
        base = pl.multiple_of(which * rows, rows)
        for step in range(span_count):
            place = lax.rem(span - step + span_count, span_count)
            signal[pl.ds(base, rows), pl.ds(pl.multiple_of(place * hop, hop), hop)] = group[step][...]
        signal[pl.ds(base, rows), span_count * hop :] = group[span_count][...]
    for segment in range(span_count):
        window = signal[:, segment * hop : (segment + 2) * hop]
        product = jnp.dot(window, table[...], preferred_element_type=jnp.float32)
        out[segment] = product.astype(jnp.bfloat16)


def band_kernel(weights, out):
    blocks, rows, width = out.shape
    taps = weights.shape[1]
    for block in range(blocks):
        tile = weights[block * rows : (block + 1) * rows, :].astype(jnp.float32)
        wide = jnp.concatenate([tile, jnp.zeros((rows, width - taps), jnp.float32)], axis=1)
        out[block] = pltpu.roll(wide, 0, 1, stride=1, stride_axis=0).astype(jnp.bfloat16)


def cross_kernel(places, rims, scaling, slots, where, *refs):
    count = len(places)
    blocks, refs = refs[:count], refs[count:]
    edges, refs = refs[:rims], refs[rims:]
    band, out, padded, own_left, own_flip = refs
    segments, rows, width = blocks[0].shape
    total = padded.shape[1]
    rim = 32
    slot = pl.program_id(0)

    def whitened(block):
        start = pl.multiple_of(block * rows, rows)
        matrix = band[block]
        result = []
        for segment in range(segments):
            window = padded[segment, pl.ds(start, matrix.shape[1]), :]
            predicted = jnp.dot(matrix, window, preferred_element_type=jnp.float32)
            raw = padded[segment, pl.ds(pl.multiple_of(start + rim, rim), rows), :]
            result.append((raw.astype(jnp.float32) - predicted).astype(jnp.bfloat16))
        return result

    @pl.when(slot == 0)
    def _():
        first = jnp.zeros((segments, rim, width), jnp.bfloat16)
        padded[:, :rim, :] = edges[0][...] if rims else first
        if rims:
            padded[:, total - 3 * rim : total - 2 * rim, :] = edges[1][...]
        else:
            padded[:, total - 3 * rim : total - 2 * rim, :] = first
        padded[:, total - 2 * rim :, :] = jnp.zeros((segments, 2 * rim, width), jnp.bfloat16)
        for index in range(count):
            start = pl.multiple_of(where[index] * rows + rim, rim)
            padded[:, pl.ds(start, rows), :] = blocks[index][...]
        mine = whitened(where[0])
        half = width // 2
        for segment in range(segments):
            own_left[segment] = mine[segment]
            own_flip[segment] = jnp.concatenate(
                [mine[segment][:, half:], -mine[segment][:, :half]], axis=1
            )

    partner = slots[slot]

    @pl.when(partner >= 0)
    def _():
        theirs = whitened(partner)
        contract = (((1,), (1,)), ((), ()))
        for part, left in enumerate((own_left, own_flip)):
            value = jnp.zeros((rows, rows), jnp.float32)
            for segment in range(segments):
                value += lax.dot_general(
                    left[segment], theirs[segment], contract, preferred_element_type=jnp.float32
                )
            out[0, part] = value * scaling

    @pl.when(partner < 0)
    def _():
        out[...] = jnp.zeros(out.shape, out.dtype)


def local(tables, recording, trailing, whiten_filter, pair_list):
    rows, hop = recording.shape
    spans, halves, chain = (lax.axis_size(axis) for axis in ("tm", "freq", "chan"))
    bands = spans * halves
    bins2 = 2 * FB // bands
    block_rows = halves * rows
    taps = whiten_filter.shape[1]
    rim = taps // 2
    here = lax.axis_index("chan")

    own = [recording]
    for step in range(1, spans):
        own.append(lax.ppermute(recording, "tm", [(i, (i + step) % spans) for i in range(spans)]))
    own.append(trailing)
    other = [swapped(value, "freq") for value in own]
    band_index = lax.axis_index("tm") * halves + lax.axis_index("freq")
    table = lax.dynamic_index_in_dim(tables, band_index, 0, keepdims=False)
    raw = pl.pallas_call(
        functools.partial(transform_kernel, spans),
        out_shape=jax.ShapeDtypeStruct((spans, block_rows, bins2), jnp.bfloat16),
        scratch_shapes=[pltpu.VMEM((block_rows, (spans + 1) * hop), jnp.bfloat16)],
        compiler_params=pltpu.CompilerParams(vmem_limit_bytes=24 * 2**20),
        name="transform",
    )(*own, *other, table)

    everyone = lax.all_gather(whiten_filter, ("chan", "freq"), axis=0, tiled=True)
    if chain == 4:
        send = lambda value, route: lax.ppermute(value, "chan", route)
        first = send(raw, [(0, 2), (2, 3), (3, 1), (1, 0)])
        second = send(raw, [(1, 3), (3, 2), (2, 0), (0, 1)])
        third = send(raw, [(1, 2), (2, 1)])
        fourth = send(first, [(2, 3), (1, 0)])
        inner = (here == 1) | (here == 2)
        blocks = [raw, first, second, jnp.where(inner, third, fourth)]
        pick = lambda *options: jnp.array(options, jnp.int32)[here]
        places = [here, pick(1, 3, 0, 2), pick(2, 0, 3, 1), pick(3, 2, 1, 0)]
        edges, near = [], chain
        base = jnp.int32(0)
        weights = everyone
    else:
        def shifted(value, distance):
            route = [(i - distance, i) for i in range(chain) if 0 <= i - distance < chain]
            return lax.ppermute(value, "chan", route)

        blocks, places = [raw], [jnp.int32(REACH)]
        for distance in range(-REACH, REACH + 1):
            if distance:
                blocks.append(shifted(raw, -distance))
                places.append(jnp.int32(distance + REACH))
        edges = [
            shifted(raw[:, block_rows - rim :, :], REACH + 1),
            shifted(raw[:, :rim, :], -REACH - 1),
        ]
        near = 2 * REACH + 1
        base = here - REACH
        beyond = jnp.pad(everyone, ((REACH * block_rows, REACH * block_rows), (0, 0)))
        weights = lax.dynamic_slice_in_dim(beyond, here * block_rows, near * block_rows, 0)
    window = -(-(block_rows + taps) // LANES) * LANES
    band = pl.pallas_call(
        band_kernel,
        out_shape=jax.ShapeDtypeStruct((near, block_rows, window), jnp.bfloat16),
        compiler_params=pltpu.CompilerParams(vmem_limit_bytes=24 * 2**20),
        name="band_matrix",
    )(weights)

    slots = pair_list[0]
    slots = jnp.where(slots >= 0, slots - base, -1)
    where = jnp.stack(places).astype(jnp.int32)
    whole = lambda shape: pl.BlockSpec(shape, lambda i, *_: (0,) * len(shape))
    result = pl.pallas_call(
        functools.partial(
            cross_kernel, places, len(edges), 1.0 / math.sqrt(spans * bins2 // 2)
        ),
        out_shape=jax.ShapeDtypeStruct((SLOTS, 2, block_rows, block_rows), jnp.float32),
        grid_spec=pltpu.PrefetchScalarGridSpec(
            num_scalar_prefetch=2,
            grid=(SLOTS,),
            in_specs=[whole(value.shape) for value in (*blocks, *edges, band)],
            out_specs=pl.BlockSpec((1, 2, block_rows, block_rows), lambda i, *_: (i, 0, 0, 0)),
            scratch_shapes=[
                pltpu.VMEM((spans, near * block_rows + 4 * rim, bins2), jnp.bfloat16),
                pltpu.VMEM((spans, block_rows, bins2), jnp.bfloat16),
                pltpu.VMEM((spans, block_rows, bins2), jnp.bfloat16),
            ],
        ),
        compiler_params=pltpu.CompilerParams(vmem_limit_bytes=32 * 2**20),
        name="cross",
    )(slots, where, *blocks, *edges, band)
    return result.reshape(1, SLOTS, 1, 2, block_rows, block_rows)


def solution(mesh):
    placed = (
        P(("days", "chan", "freq"), "tm"),
        P(("days", "chan", "freq"), None),
        P(("chan", "freq"), None),
        P(("days", "chan"), None),
    )
    bands = mesh.shape["tm"] * mesh.shape["freq"]

    def step(recording, trailing, whiten_filter, pair_list):
        tables = band_tables(bands, 2 * trailing.shape[1])
        return jax.shard_map(
            functools.partial(local, tables),
            mesh=mesh,
            in_specs=placed,
            out_specs=P(("days", "chan"), None, ("tm", "freq"), None, None, None),
            check_vma=False,
        )(recording, trailing, whiten_filter, pair_list)

    return step
```

time: 279 us -> 51.1 us (0.18)
  local copies, waits for them, and re-layouts: 199 us -> 5.12 us
  other arithmetic: 22 us -> 1.9 us
  blocking collectives: 0 us -> 18.3 us
  starting transfers between devices: 24.9 us -> 11 us
  waiting for transfers between devices: 22.4 us -> 9.66 us
  between operations: 5.63 us -> 0.12 us
  Pallas kernels: 0 us -> 4.67 us
  matrix products: 4.59 us -> 0 us
    gather x3 -> x0, local copies, waits for them, and re-layouts: 196 us -> none  [local(): jnp.take_along_axis(whiten_filter, jnp.clip(offset, 0, tap_count - 1), ax...]
    convert_element_type x1 -> x0, other arithmetic: 19.2 us -> none  [fourier_table(): (-taper[:, None] * jnp.sin(angle) * normaliser).astype(jnp.bfloat16)]
    all_gather x0 -> x1, blocking collectives: none -> 18.3 us  [local(): lax.all_gather(whiten_filter, ('chan', 'freq'), axis=0, tiled=True)]
    ppermute x9 -> x8, waiting for transfers between devices: 21.8 us -> 9.66 us  [the longest x1 6.01 us: local(): lax.ppermute(recording, 'tm', [(i, (i + step) % spans) for i in range(spa...]
    ppermute x9 -> x8, starting transfers between devices: 18.3 us -> 11 us  [the longest x4 7.5 us: local(): send = lambda value, route: lax.ppermute(value, 'chan', route)]
    all_to_all x1 -> x0, starting transfers between devices: 6.59 us -> none  [local(): lax.all_to_all(spectra[None], ('tm', 'freq'), split_axis=4, concat_axis=0...]
    pallas_call x0 -> x3, Pallas kernels: none -> 4.67 us  [the longest x1 3.74 us: local(): pl.pallas_call(functools.partial(cross_kernel, places, len(edges), 1.0 /...]
    dot_general x11 -> x0, matrix products: 4.59 us -> none  [the longest x2 2.26 us: local(): jnp.dot(stacked_segments, joined, preferred_element_type=jnp.float32)]
  transfers between devices with their start and end apart: 10 -> 8, of which waited for: 4 -> 3; matrix products, arithmetic and copies ran while one was open for 78% -> 10% of each run, Pallas kernels for 0% -> 0%
where the time goes in v1:
time: 51.1 us; the launch traced here: 50.8 us
  blocking collectives  18.3 us (36%)
  starting transfers between devices  11 us (22%)
  waiting for transfers between devices  9.66 us (19%)
  local copies, waits for them, and re-layouts  5.12 us (10%)
  Pallas kernels  4.67 us (9%)
  other arithmetic  1.9 us (4%)
    all_gather x1, blocking collectives, local(): lax.all_gather(whiten_filter, ('chan', 'freq'), axis=0, tiled=True)  18.3 us
    ppermute x4, starting transfers between devices, local(): send = lambda value, route: lax.ppermute(value, 'chan', route)  7.5 us
    ppermute x1, waiting for transfers between devices, local(): lax.ppermute(recording, 'tm', [(i, (i + step) % spans) for i in range(spa...  6.01 us
    pallas_call x1, Pallas kernels, local(): pl.pallas_call(functools.partial(cross_kernel, places, len(edges), 1.0 /...  3.74 us
    ppermute x4, waiting for transfers between devices, local(): send = lambda value, route: lax.ppermute(value, 'chan', route)  3.43 us
    ppermute x1, starting transfers between devices, local(): lax.ppermute(recording, 'tm', [(i, (i + step) % spans) for i in range(spa...  3.02 us
    unnamed x15, local copies, waits for them, and re-layouts  2.03 us
    select_n x1, other arithmetic, local(): slots = jnp.where(slots >= 0, slots - base, -1)  1.87 us
  transfers between devices with their start and end apart: 8, of which 3 were waited for; matrix products, arithmetic and copies ran while one was open for 10% of the time, Pallas kernels for 0%

profile of v1, /device:TPU:0, one launch (start us, length us, event | category | flops | bytes accessed | tf_op | source)
XLA Modules:
  0.0 50.8 jit_solution(17142171410522318545)
XLA Ops:
  0.0 0.0 copy-start.6
  0.0 0.0 copy-start.5
  0.0 0.0 copy-start.4
  0.0 0.0 copy-start.2
  0.0 0.0 copy-start.3
  0.0 3.0 %collective-permute-start = (bf16[128,1024]{1,0:T(8,128)(2,1)}, bf16[128,1024]{1,0:T(8,128)(2,1)S(1)}, u32[]{:S(2)}, u32[]{:S(2)}) collective-permute-start(bf16[128,1024]{1,0:T(8,128)(2,1)} %refs_0_.1), channel_id=1, source_target_pairs={{0,2},{2,0},{1,3},{3,1},{4,6},{6,4},{5,7},{7,5},{8,10},{10,8},{9,1... | collective-permute-start | bytes 786440 | tf_op jit(solution)/shard_map/ppermute | solution.py:135
  3.0 0.0 collective-permute-start.1
  3.0 0.5 collective-permute-start.3
  3.5 6.0 %collective-permute-done.refs_1_ = bf16[128,1024]{1,0:T(8,128)(2,1)S(1)} collective-permute-done((bf16[128,1024]{1,0:T(8,128)(2,1)}, bf16[128,1024]{1,0:T(8,128)(2,1)S(1)}, u32[]{:S(2)}, u32[]{:S(2)}) %collective-permute-start) | collective-permute-done | bytes 262176 | tf_op jit(solution)/shard_map/ppermute | solution.py:135
  9.6 0.0 collective-permute-start.2
  9.6 1.3 %dynamic-slice_bitcast_fusion.refs_6_ = bf16[2048,256]{1,0:T(8,128)(2,1)S(1)} fusion(bf16[4,2048,256]{2,1,0:T(8,128)(2,1)} %constant.34.clone, s32[]{:T(128)S(6)} %select_n.23), kind=kLoop, calls=%fused_computation | loop fusion | bytes 2097156 | tf_op jit(solution)/shard_map/jit(dynamic_index_in_dim)/squeeze | solution.py:139
  10.9 0.0 collective-permute-done.3.refs_5_
  10.9 0.0 collective-permute-done.1.refs_3_
  10.9 0.2 collective-permute-done.2.refs_4_
  11.1 0.0 copy-start
  11.1 0.9 %copy-done = bf16[128,1024]{1,0:T(8,128)(2,1)S(1)} copy-done((bf16[128,1024]{1,0:T(8,128)(2,1)S(1)}, bf16[128,1024]{1,0:T(8,128)(2,1)}, u32[]{:S(2)}) %copy-start) | copy-done | bytes 262168
  12.0 0.0 copy-start.1
  12.0 0.9 %copy-done.1 = bf16[128,1024]{1,0:T(8,128)(2,1)S(1)} copy-done((bf16[128,1024]{1,0:T(8,128)(2,1)S(1)}, bf16[128,1024]{1,0:T(8,128)(2,1)}, u32[]{:S(2)}) %copy-start.1) | copy-done | bytes 262168
  13.0 0.8 %transform.1.refs_0_ = bf16[2,256,256]{2,1,0:T(8,128)(2,1)S(1)} custom-call(bf16[128,1024]{1,0:T(8,128)(2,1)S(1)} %copy-done, bf16[128,1024]{1,0:T(8,128)(2,1)S(1)} %collective-permute-done.refs_1_, bf16[128,1024]{1,0:T(8,128)(2,1)S(1)} %copy-done.1, bf16[128,1024]{1,0:T(8,128)(2,1)S(1)} %collective-permute-done.1.refs_3_, ...), custom_call_target="tpu_custom_call" | custom-call | tf_op jit(solution)/shard_map/transform/pallas_call | solution.py:140
  13.8 2.9 %collective-permute-start.4 = (bf16[2,256,256]{2,1,0:T(8,128)(2,1)S(1)}, bf16[2,256,256]{2,1,0:T(8,128)(2,1)S(1)}, u32[]{:S(2)}, u32[]{:S(2)}) collective-permute-start(bf16[2,256,256]{2,1,0:T(8,128)(2,1)S(1)} %transform.1.refs_0_), channel_id=1, source_target_pairs={{0,8},{8,12},{12,4},{4,0},{1,9},{9,13},{13,5},{5,1},{2,10},{10,14}... | collective-permute-start | bytes 786440 | tf_op jit(solution)/shard_map/ppermute | solution.py:150
  16.7 0.0 copy-done.6
  16.7 0.6 %dynamic_slice.15 = s32[1]{0:T(128)} dynamic-slice(s32[4]{0:T(128)S(1)} %copy-done.6, s32[]{:T(128)S(6)} %select_n.22), dynamic_slice_sizes={1} | dynamic-slice | bytes 12 | tf_op jit(solution)/shard_map/dynamic_slice | solution.py:157
  17.3 0.0 copy-done.5
  17.3 0.6 %dynamic_slice.14 = s32[1]{0:T(128)} dynamic-slice(s32[4]{0:T(128)S(1)} %copy-done.5, s32[]{:T(128)S(6)} %select_n.22), dynamic_slice_sizes={1} | dynamic-slice | bytes 12 | tf_op jit(solution)/shard_map/dynamic_slice | solution.py:157
  17.9 0.0 copy-done.4
  17.9 0.6 %dynamic_slice.13 = s32[1]{0:T(128)} dynamic-slice(s32[4]{0:T(128)S(1)} %copy-done.4, s32[]{:T(128)S(6)} %select_n.22), dynamic_slice_sizes={1} | dynamic-slice | bytes 12 | tf_op jit(solution)/shard_map/dynamic_slice | solution.py:157
  18.5 0.0 copy-done.2
  18.5 0.1 copy.9
  18.6 0.7 %collective-permute-start.6 = (bf16[2,256,256]{2,1,0:T(8,128)(2,1)S(1)}, bf16[2,256,256]{2,1,0:T(8,128)(2,1)S(1)}, u32[]{:S(2)}, u32[]{:S(2)}) collective-permute-start(bf16[2,256,256]{2,1,0:T(8,128)(2,1)S(1)} %transform.1.refs_0_), channel_id=1, source_target_pairs={{4,8},{8,4},{5,9},{9,5},{6,10},{10,6},{7,11},{11,7},{20,24},{24,20... | collective-permute-start | bytes 786440 | tf_op jit(solution)/shard_map/ppermute | solution.py:150
  19.3 3.4 %collective-permute-done.4.refs_1_ = bf16[2,256,256]{2,1,0:T(8,128)(2,1)S(1)} collective-permute-done((bf16[2,256,256]{2,1,0:T(8,128)(2,1)S(1)}, bf16[2,256,256]{2,1,0:T(8,128)(2,1)S(1)}, u32[]{:S(2)}, u32[]{:S(2)}) %collective-permute-start.4) | collective-permute-done | bytes 262176 | tf_op jit(solution)/shard_map/ppermute | solution.py:150
  22.7 1.3 %collective-permute-start.7 = (bf16[2,256,256]{2,1,0:T(8,128)(2,1)S(1)}, bf16[2,256,256]{2,1,0:T(8,128)(2,1)S(1)}, u32[]{:S(2)}, u32[]{:S(2)}) collective-permute-start(bf16[2,256,256]{2,1,0:T(8,128)(2,1)S(1)} %collective-permute-done.4.refs_1_), channel_id=1, source_target_pairs={{8,12},{4,0},{9,13},{5,1},{10,14},{6,2},{11,15},{7,3},{24,28},{20,... | collective-permute-start | bytes 786440 | tf_op jit(solution)/shard_map/ppermute | solution.py:150
  24.0 0.0 copy-done.3
  24.0 1.9 %compare_select_fusion = (s32[4]{0:T(128)S(1)}, s32[4]{0:T(128)S(1)}) fusion(s32[1,4]{1,0:T(1,128)S(1)} %copy-done.3, s32[1]{0:T(128)} %dynamic_slice.15, s32[1]{0:T(128)} %dynamic_slice.14, s32[1]{0:T(128)} %dynamic_slice.13, s32[1]{0:T(128)} %bitcast.1), kind=kLoop, calls=%fused_computation.2 | loop fusion | flops 20 | bytes 64 | tf_op jit(solution)/shard_map/jit(_where)/select_n | solution.py:189
  25.9 2.7 %collective-permute-start.5 = (bf16[2,256,256]{2,1,0:T(8,128)(2,1)S(1)}, bf16[2,256,256]{2,1,0:T(8,128)(2,1)S(1)}, u32[]{:S(2)}, u32[]{:S(2)}) collective-permute-start(bf16[2,256,256]{2,1,0:T(8,128)(2,1)S(1)} %transform.1.refs_0_), channel_id=1, source_target_pairs={{4,12},{12,8},{8,0},{0,4},{5,13},{13,9},{9,1},{1,5},{6,14},{14,10}... | collective-permute-start | bytes 786440 | tf_op jit(solution)/shard_map/ppermute | solution.py:150
  28.5 18.3 %all_gather.3.weights = bf16[1024,64]{1,0:T(8,128)(2,1)S(1)} all-gather(bf16[128,64]{1,0:T(8,128)(2,1)S(1)} %copy.9), channel_id=1, replica_groups=mesh['days'=2,'chan'=4,'tm'=2,'freq'=2] {'chan','freq'}, dimensions={0}, use_global_device_ids=true | all-gather | bytes 147456 | tf_op jit(solution)/shard_map/all_gather | solution.py:148
  46.8 0.2 band_matrix.1.refs_4_
  47.0 0.0 collective-permute-done.6
  47.0 0.0 collective-permute-done.7
  47.1 0.0 collective-permute-done.5.refs_2_
  47.1 3.7 %cross.1 = f32[4,2,256,256]{3,2,1,0:T(8,128)} custom-call(s32[4]{0:T(128)S(1)} %get-tuple-element.5.slots, s32[4]{0:T(128)S(1)} %get-tuple-element.6.where, bf16[2,256,256]{2,1,0:T(8,128)(2,1)S(1)} %transform.1.refs_0_, bf16[2,256,256]{2,1,0:T(8,128)(2,1)S(1)} %collective-permute-done.4.refs_1_, bf16[2,256,256]{2,1,0:T(8,128)(2,1)S(1)} %collective-permute-done.5.refs_2_, ...), custom_call_target="tpu_custom_call" | custom-call | tf_op jit(solution)/shard_map/cross/pallas_call | solution.py:192
  (1 shorter events, 0.0 us)
Async XLA Ops:
  0.0 16.7 %copy-start.6 = (s32[4]{0:T(128)S(1)}, s32[4]{0:T(128)}, u32[]{:S(2)}) copy-start(s32[4]{0:T(128)} %constant.37.clone) | copy-start | bytes 52
  0.0 17.3 %copy-start.5 = (s32[4]{0:T(128)S(1)}, s32[4]{0:T(128)}, u32[]{:S(2)}) copy-start(s32[4]{0:T(128)} %constant.36.clone) | copy-start | bytes 52
  0.0 17.9 %copy-start.4 = (s32[4]{0:T(128)S(1)}, s32[4]{0:T(128)}, u32[]{:S(2)}) copy-start(s32[4]{0:T(128)} %constant.35.clone) | copy-start | bytes 52
  0.0 18.5 %copy-start.2 = (bf16[128,64]{0,1:T(8,128)(2,1)S(1)}, bf16[128,64]{0,1:T(8,128)(2,1)}, u32[]{:S(2)}) copy-start(bf16[128,64]{0,1:T(8,128)(2,1)} %param.10) | copy-start | bytes 49156
  0.0 24.0 %copy-start.3 = (s32[1,4]{1,0:T(1,128)S(1)}, s32[1,4]{1,0:T(1,128)}, u32[]{:S(2)}) copy-start(s32[1,4]{1,0:T(1,128)} %param.11) | copy-start | bytes 52
  0.0 9.5 %collective-permute-start = (bf16[128,1024]{1,0:T(8,128)(2,1)}, bf16[128,1024]{1,0:T(8,128)(2,1)S(1)}, u32[]{:S(2)}, u32[]{:S(2)}) collective-permute-start(bf16[128,1024]{1,0:T(8,128)(2,1)} %refs_0_.1), channel_id=1, source_target_pairs={{0,2},{2,0},{1,3},{3,1},{4,6},{6,4},{5,7},{7,5},{8,10},{10,8},{9,1... | collective-permute-start | bytes 786440 | tf_op jit(solution)/shard_map/ppermute | solution.py:135
  3.0 7.8 %collective-permute-start.1 = (bf16[128,1024]{1,0:T(8,128)(2,1)}, bf16[128,1024]{1,0:T(8,128)(2,1)S(1)}, u32[]{:S(2)}, u32[]{:S(2)}) collective-permute-start(bf16[128,1024]{1,0:T(8,128)(2,1)} %refs_0_.1), channel_id=1, source_target_pairs={{0,1},{1,0},{2,3},{3,2},{4,5},{5,4},{6,7},{7,6},{8,9},{9,8},{10,11... | collective-permute-start | bytes 786440 | tf_op jit(solution)/shard_map/ppermute | solution.py:34
  3.0 7.8 %collective-permute-start.3 = (bf16[128,1024]{1,0:T(8,128)(2,1)}, bf16[128,1024]{1,0:T(8,128)(2,1)S(1)}, u32[]{:S(2)}, u32[]{:S(2)}) collective-permute-start(bf16[128,1024]{1,0:T(8,128)(2,1)} %refs_2_.1), channel_id=1, source_target_pairs={{0,1},{1,0},{2,3},{3,2},{4,5},{5,4},{6,7},{7,6},{8,9},{9,8},{10,11... | collective-permute-start | bytes 786440 | tf_op jit(solution)/shard_map/ppermute | solution.py:34
  9.6 1.5 %collective-permute-start.2 = (bf16[128,1024]{1,0:T(8,128)(2,1)S(1)}, bf16[128,1024]{1,0:T(8,128)(2,1)S(1)}, u32[]{:S(2)}, u32[]{:S(2)}) collective-permute-start(bf16[128,1024]{1,0:T(8,128)(2,1)S(1)} %collective-permute-done.refs_1_), channel_id=1, source_target_pairs={{0,1},{1,0},{2,3},{3,2},{4,5},{5,4},{6,7},{7,6},{8,9},{9,8},{10,11... | collective-permute-start | bytes 786440 | tf_op jit(solution)/shard_map/ppermute | solution.py:34
  11.1 1.0 %copy-start = (bf16[128,1024]{1,0:T(8,128)(2,1)S(1)}, bf16[128,1024]{1,0:T(8,128)(2,1)}, u32[]{:S(2)}) copy-start(bf16[128,1024]{1,0:T(8,128)(2,1)} %refs_0_.1) | copy-start | bytes 786436
  12.0 0.9 %copy-start.1 = (bf16[128,1024]{1,0:T(8,128)(2,1)S(1)}, bf16[128,1024]{1,0:T(8,128)(2,1)}, u32[]{:S(2)}) copy-start(bf16[128,1024]{1,0:T(8,128)(2,1)} %refs_2_.1) | copy-start | bytes 786436
  13.8 8.9 %collective-permute-start.4 = (bf16[2,256,256]{2,1,0:T(8,128)(2,1)S(1)}, bf16[2,256,256]{2,1,0:T(8,128)(2,1)S(1)}, u32[]{:S(2)}, u32[]{:S(2)}) collective-permute-start(bf16[2,256,256]{2,1,0:T(8,128)(2,1)S(1)} %transform.1.refs_0_), channel_id=1, source_target_pairs={{0,8},{8,12},{12,4},{4,0},{1,9},{9,13},{13,5},{5,1},{2,10},{10,14}... | collective-permute-start | bytes 786440 | tf_op jit(solution)/shard_map/ppermute | solution.py:150
  18.6 28.4 %collective-permute-start.6 = (bf16[2,256,256]{2,1,0:T(8,128)(2,1)S(1)}, bf16[2,256,256]{2,1,0:T(8,128)(2,1)S(1)}, u32[]{:S(2)}, u32[]{:S(2)}) collective-permute-start(bf16[2,256,256]{2,1,0:T(8,128)(2,1)S(1)} %transform.1.refs_0_), channel_id=1, source_target_pairs={{4,8},{8,4},{5,9},{9,5},{6,10},{10,6},{7,11},{11,7},{20,24},{24,20... | collective-permute-start | bytes 786440 | tf_op jit(solution)/shard_map/ppermute | solution.py:150
  22.7 24.3 %collective-permute-start.7 = (bf16[2,256,256]{2,1,0:T(8,128)(2,1)S(1)}, bf16[2,256,256]{2,1,0:T(8,128)(2,1)S(1)}, u32[]{:S(2)}, u32[]{:S(2)}) collective-permute-start(bf16[2,256,256]{2,1,0:T(8,128)(2,1)S(1)} %collective-permute-done.4.refs_1_), channel_id=1, source_target_pairs={{8,12},{4,0},{9,13},{5,1},{10,14},{6,2},{11,15},{7,3},{24,28},{20,... | collective-permute-start | bytes 786440 | tf_op jit(solution)/shard_map/ppermute | solution.py:150
  25.9 21.2 %collective-permute-start.5 = (bf16[2,256,256]{2,1,0:T(8,128)(2,1)S(1)}, bf16[2,256,256]{2,1,0:T(8,128)(2,1)S(1)}, u32[]{:S(2)}, u32[]{:S(2)}) collective-permute-start(bf16[2,256,256]{2,1,0:T(8,128)(2,1)S(1)} %transform.1.refs_0_), channel_id=1, source_target_pairs={{4,12},{12,8},{8,0},{0,4},{5,13},{13,9},{9,1},{1,5},{6,14},{14,10}... | collective-permute-start | bytes 786440 | tf_op jit(solution)/shard_map/ppermute | solution.py:150

commit v2 on v1

v2 whole, which is shorter than its diff:
```python
import functools
import math

import jax
import jax.numpy as jnp
import ml_dtypes
import numpy as np
from jax import lax
from jax.experimental import pallas as pl
from jax.experimental.pallas import tpu as pltpu
from jax.sharding import PartitionSpec as P

FB = 512
REACH = 3
SLOTS = 4
LANES = 128


def band_tables(bands, length):
    samples = np.arange(length, dtype=np.int64)[:, None]
    bins = np.arange(FB, dtype=np.int64)[None, :]
    phase = (samples * bins % length).astype(np.float32)
    angle = np.float32(2.0 * math.pi / length) * phase
    ramp = np.float32(2.0 * math.pi / length) * np.arange(length, dtype=np.float32)
    taper = (np.float32(0.5) - np.float32(0.5) * np.cos(ramp))[:, None]
    normaliser = np.float32(1.0 / math.sqrt(0.375 * length))
    cosine = (taper * np.cos(angle) * normaliser).astype(ml_dtypes.bfloat16)
    sine = (-taper * np.sin(angle) * normaliser).astype(ml_dtypes.bfloat16)
    both = np.stack([cosine, sine], axis=1).reshape(length, 2, bands, FB // bands)
    return np.ascontiguousarray(both.transpose(2, 0, 1, 3)).reshape(bands, length, 2 * FB // bands)


def swapped(value, axis):
    return lax.ppermute(value, axis, [(0, 1), (1, 0)])


def block_of(own, other):
    low = lax.axis_index("freq") == 0
    a, b = own[...], other[...]
    return jnp.concatenate([jnp.where(low, a, b), jnp.where(low, b, a)], axis=0)


def hop_part(place, segment, value, table):
    hop = value.shape[1]
    half = place - segment
    start = pl.multiple_of(jnp.clip(half, 0, 1) * hop, hop)
    product = jnp.dot(value, table[pl.ds(start, hop), :], preferred_element_type=jnp.float32)
    return jnp.where((half == 0) | (half == 1), product, 0.0)


def begin_kernel(own, other, other_next, tables, total, table, sems):
    span = lax.axis_index("tm")
    band = span * lax.axis_size("freq") + lax.axis_index("freq")
    copy = pltpu.make_async_copy(tables.at[band], table, sems.at[0])
    copy.start()
    width = table.shape[1]
    segments = total.shape[1] // width
    mine = block_of(own.at[0], other)
    following = block_of(own.at[1], other_next)
    copy.wait()
    for segment in range(segments):
        value = hop_part(span, segment, mine, table)
        if segment == segments - 1:
            value += hop_part(segments, segment, following, table)
        total[:, segment * width : (segment + 1) * width] = value


def finish_kernel(spans, *refs):
    own, refs = refs[: spans - 1], refs[spans - 1 :]
    other, (table, begun, out) = refs[: spans - 1], refs[spans - 1 :]
    width = table.shape[1]
    blocks = [block_of(a, b) for a, b in zip(own, other)]
    for segment in range(spans):
        columns = slice(segment * width, (segment + 1) * width)
        value = begun[:, columns]
        for step in range(1, spans):
            place = lax.rem(lax.axis_index("tm") - step + spans, spans)
            value += hop_part(place, segment, blocks[step - 1], table)
        out[:, columns] = value.astype(jnp.bfloat16)


def band_kernel(chain, *refs):
    *weights, out = refs
    blocks, rows, width = out.shape
    here = lax.axis_index("chan")
    low = lax.axis_index("freq") == 0
    for block in range(blocks):
        if chain == 4:
            own, other = (ref[block].astype(jnp.float32) for ref in weights)
            place = jnp.bitwise_xor(here, block)
            tile = jnp.concatenate([jnp.where(low, own, other), jnp.where(low, other, own)], axis=1).T
        else:
            place = block
            tile = weights[0][block * rows : (block + 1) * rows, :].astype(jnp.float32)
        blank = jnp.zeros((rows, width - tile.shape[1]), jnp.float32)
        wide = jnp.concatenate([tile, blank], axis=1)
        out[place] = pltpu.roll(wide, 0, 1, stride=1, stride_axis=0).astype(jnp.bfloat16)


def cross_kernel(chain, segments, scaling, slots, *refs):
    here = lax.axis_index("chan")
    if chain == 4:
        raw, first, second, third, fourth, band, *refs = refs
        pick = lambda a, b, c, d: jnp.where(here == 0, a, jnp.where(here == 1, b, jnp.where(here == 2, c, d)))
        inner = (here == 1) | (here == 2)
        blocks = [
            (here, raw[...]),
            (pick(1, 3, 0, 2), first[...]),
            (pick(2, 0, 3, 1), second[...]),
            (pick(3, 2, 1, 0), jnp.where(inner, third[...], fourth[...])),
        ]
        edges = None
        mine, base = here, 0
    else:
        near = [0] + [d for d in range(-REACH, REACH + 1) if d]
        blocks = [(d + REACH, ref[...]) for d, ref in zip(near, refs)]
        refs = refs[len(near) :]
        before, after, band, *refs = refs
        edges = (before[...], after[...])
        mine, base = REACH, here - REACH
    out, padded, spectra, left, result, sems = refs
    rows, columns = left.shape[0] // 2, left.shape[1]
    count = len(blocks)
    rim = (padded.shape[0] - count * rows) // 4
    edge = count * rows + rim

    nothing = jnp.zeros((rim, columns), jnp.bfloat16)
    padded[:rim, :] = edges[0] if edges else nothing
    padded[edge : edge + rim, :] = edges[1] if edges else nothing
    padded[edge + rim :, :] = jnp.zeros((2 * rim, columns), jnp.bfloat16)
    for place, value in blocks:
        padded[pl.ds(pl.multiple_of(place * rows + rim, rim), rows), :] = value

    for block in range(count):
        start = block * rows
        matrix = band[block]
        window = padded[start : start + matrix.shape[1], :]
        predicted = jnp.dot(matrix, window, preferred_element_type=jnp.float32)
        raw = padded[start + rim : start + rim + rows, :].astype(jnp.float32)
        spectra[block] = (raw - predicted).astype(jnp.bfloat16)

    own = spectra[mine]
    left[:rows, :] = own
    half = columns // (2 * segments)
    turned = []
    for segment in range(segments):
        start = 2 * segment * half
        turned += [own[:, start + half : start + 2 * half], -own[:, start : start + half]]
    left[rows:, :] = jnp.concatenate(turned, axis=1)

    contract = (((1,), (1,)), ((), ()))
    for slot in range(SLOTS):
        partner = slots[0, slot]
        theirs = spectra[jnp.clip(partner - base, 0, count - 1)]
        both = lax.dot_general(left[...], theirs, contract, preferred_element_type=jnp.float32)
        both = jnp.where(partner >= 0, both * scaling, 0.0)
        result[slot, 0] = both[:rows]
        result[slot, 1] = both[rows:]
        pltpu.make_async_copy(result.at[slot], out.at[slot], sems.at[slot]).start()
    for slot in range(SLOTS):
        pltpu.make_async_copy(result.at[slot], out.at[slot], sems.at[slot]).wait()


def local(tables, recording, trailing, whiten_filter, pair_list):
    rows, hop = recording.shape
    spans, halves, chain = (lax.axis_size(axis) for axis in ("tm", "freq", "chan"))
    bands = spans * halves
    bins2 = 2 * FB // bands
    block_rows = halves * rows
    taps = whiten_filter.shape[1]
    rim = taps // 2
    here = lax.axis_index("chan")

    in_vmem = pl.BlockSpec(memory_space=pltpu.VMEM)
    small = pltpu.CompilerParams(vmem_limit_bytes=16 * 2**20)

    received = [
        lax.ppermute(recording, "tm", [(i, (i + step) % spans) for i in range(spans)])
        for step in range(1, spans)
    ]
    if chain == 4:
        filters = [
            lax.ppermute(whiten_filter.T, "chan", [(i, i ^ step) for i in range(chain)])
            for step in range(1, chain)
        ]
    else:
        filters = [lax.all_gather(whiten_filter, ("chan", "freq"), axis=0, tiled=True)]
    own = jnp.stack([recording, trailing])
    total = (block_rows, spans * bins2)
    in_hbm = pl.BlockSpec(memory_space=pltpu.HBM)
    begun, table = pl.pallas_call(
        begin_kernel,
        out_shape=[
            jax.ShapeDtypeStruct(total, jnp.float32),
            jax.ShapeDtypeStruct(tables.shape[1:], jnp.bfloat16),
        ],
        in_specs=[in_vmem, in_vmem, in_vmem, in_hbm],
        out_specs=[in_vmem, in_vmem],
        scratch_shapes=[pltpu.SemaphoreType.DMA((1,))],
        compiler_params=pltpu.CompilerParams(vmem_limit_bytes=48 * 2**20),
        name="begin_transform",
    )(own, swapped(recording, "freq"), swapped(trailing, "freq"), jnp.asarray(tables))
    received, filters, begun = lax.optimization_barrier((received, filters, begun))
    raw = pl.pallas_call(
        functools.partial(finish_kernel, spans),
        out_shape=jax.ShapeDtypeStruct(total, jnp.bfloat16),
        in_specs=[in_vmem] * (2 * spans),
        out_specs=in_vmem,
        compiler_params=small,
        name="finish_transform",
    )(*received, *(swapped(value, "freq") for value in received), table, begun)

    if chain == 4:
        near = chain
        weights = jnp.stack([whiten_filter.T, *filters])
        weights = (weights, swapped(weights, "freq"))
    else:
        near = 2 * REACH + 1
        beyond = jnp.pad(filters[0], ((REACH * block_rows, REACH * block_rows), (0, 0)))
        weights = (lax.dynamic_slice_in_dim(beyond, here * block_rows, near * block_rows, 0),)
    window = -(-(block_rows + taps) // LANES) * LANES
    band = pl.pallas_call(
        functools.partial(band_kernel, chain),
        out_shape=jax.ShapeDtypeStruct((near, block_rows, window), jnp.bfloat16),
        in_specs=[in_vmem] * len(weights),
        out_specs=in_vmem,
        compiler_params=small,
        name="band_matrix",
    )(*weights)

    if chain == 4:
        first = lax.ppermute(raw, "chan", [(0, 2), (2, 3), (3, 1), (1, 0)])
        second = lax.ppermute(raw, "chan", [(1, 3), (3, 2), (2, 0), (0, 1)])
        first, late = lax.optimization_barrier((first, raw))
        third = lax.ppermute(late, "chan", [(1, 2), (2, 1)])
        fourth = lax.ppermute(first, "chan", [(2, 3), (1, 0)])
        blocks = [raw, first, second, third, fourth]
    else:

        def shifted(value, distance):
            route = [(i - distance, i) for i in range(chain) if 0 <= i - distance < chain]
            return lax.ppermute(value, "chan", route)

        blocks = [raw]
        blocks += [shifted(raw, -d) for d in range(-REACH, REACH + 1) if d]
        blocks.append(shifted(raw[block_rows - rim :, :], REACH + 1))
        blocks.append(shifted(raw[:rim, :], -REACH - 1))

    out_shape = (SLOTS, 2, block_rows, block_rows)
    result = pl.pallas_call(
        functools.partial(cross_kernel, chain, spans, 1.0 / math.sqrt(spans * bins2 // 2)),
        out_shape=jax.ShapeDtypeStruct(out_shape, jnp.float32),
        in_specs=[pl.BlockSpec(memory_space=pltpu.SMEM)] + [in_vmem] * (len(blocks) + 1),
        out_specs=in_hbm,
        scratch_shapes=[
            pltpu.VMEM((near * block_rows + 4 * rim, total[1]), jnp.bfloat16),
            pltpu.VMEM((near, *total), jnp.bfloat16),
            pltpu.VMEM((2 * block_rows, total[1]), jnp.bfloat16),
            pltpu.VMEM(out_shape, jnp.float32),
            pltpu.SemaphoreType.DMA((SLOTS,)),
        ],
        compiler_params=pltpu.CompilerParams(vmem_limit_bytes=24 * 2**20),
        name="cross",
    )(pair_list, *blocks, band)
    return result.reshape(1, SLOTS, 1, 2, block_rows, block_rows)


def solution(mesh):
    placed = (
        P(("days", "chan", "freq"), "tm"),
        P(("days", "chan", "freq"), None),
        P(("chan", "freq"), None),
        P(("days", "chan"), None),
    )
    bands = mesh.shape["tm"] * mesh.shape["freq"]

    def step(recording, trailing, whiten_filter, pair_list):
        tables = band_tables(bands, 2 * trailing.shape[1])
        return jax.shard_map(
            functools.partial(local, tables),
            mesh=mesh,
            in_specs=placed,
            out_specs=P(("days", "chan"), None, ("tm", "freq"), None, None, None),
            check_vma=False,
        )(recording, trailing, whiten_filter, pair_list)

    return step
```

time: 51.1 us -> 37.9 us (0.74)
  blocking collectives: 18.3 us -> 0 us
  waiting for transfers between devices: 9.66 us -> 18.8 us
  local copies, waits for them, and re-layouts: 5.12 us -> 0.01 us
  Pallas kernels: 4.67 us -> 5.82 us
  starting transfers between devices: 11 us -> 11.9 us
  other arithmetic: 1.9 us -> 1.1 us
    all_gather x1 -> x0, blocking collectives: 18.3 us -> none  [local(): lax.all_gather(whiten_filter, ('chan', 'freq'), axis=0, tiled=True)]
    ppermute x4 -> x7, waiting for transfers between devices: 3.43 us -> 16 us  [the longest x1 6.72 us: local(): first = lax.ppermute(raw, 'chan', [(0, 2), (2, 3), (3, 1), (1, 0)])]
    ppermute x1, waiting for transfers between devices: 6.01 us -> 0.01 us  [local(): lax.ppermute(recording, 'tm', [(i, (i + step) % spans) for i in range(spa...]
    ppermute x3 -> x4, waiting for transfers between devices: 0.22 us -> 2.77 us  [swapped(): return lax.ppermute(value, axis, [(0, 1), (1, 0)])]
    unnamed x15 -> x4, local copies, waits for them, and re-layouts: 2.03 us -> 0.01 us
    select_n x2 -> x0, other arithmetic: 1.9 us -> none  [the longest x1 1.87 us: local(): slots = jnp.where(slots >= 0, slots - base, -1)]
    dynamic_slice x3 -> x0, local copies, waits for them, and re-layouts: 1.8 us -> none  [local(): pick = lambda *options: jnp.array(options, jnp.int32)[here]]
    squeeze x1 -> x0, local copies, waits for them, and re-layouts: 1.29 us -> none  [local(): table = lax.dynamic_index_in_dim(tables, band_index, 0, keepdims=False)]
  transfers between devices with their start and end apart: 8 -> 12, of which waited for: 3 -> 6; matrix products, arithmetic and copies ran while one was open for 10% -> 3% of each run, Pallas kernels for 0% -> 6%
where the time goes in v2:
time: 37.9 us; the launch traced here: 37.8 us
  waiting for transfers between devices  18.8 us (50%)
  starting transfers between devices  11.9 us (31%)
  Pallas kernels  5.82 us (15%)
  other arithmetic  1.1 us (3%)
    ppermute x1, waiting for transfers between devices, local(): first = lax.ppermute(raw, 'chan', [(0, 2), (2, 3), (3, 1), (1, 0)])  6.72 us
    ppermute x1, waiting for transfers between devices, local(): fourth = lax.ppermute(first, 'chan', [(2, 3), (1, 0)])  5.64 us
    ppermute x3, starting transfers between devices, local(): lax.ppermute(whiten_filter.T, 'chan', [(i, i ^ step) for i in range(chain)])  4.39 us
    pallas_call x1, Pallas kernels, local(): pl.pallas_call(functools.partial(cross_kernel, chain, spans, 1.0 / math.s...  3.25 us
    ppermute x1, starting transfers between devices, local(): lax.ppermute(recording, 'tm', [(i, (i + step) % spans) for i in range(spa...  2.94 us
    ppermute x4, waiting for transfers between devices, swapped(): return lax.ppermute(value, axis, [(0, 1), (1, 0)])  2.77 us
    ppermute x1, waiting for transfers between devices, local(): second = lax.ppermute(raw, 'chan', [(1, 3), (3, 2), (2, 0), (0, 1)])  2.54 us
    ppermute x1, starting transfers between devices, local(): first = lax.ppermute(raw, 'chan', [(0, 2), (2, 3), (3, 1), (1, 0)])  2.08 us
  transfers between devices with their start and end apart: 12, of which 6 were waited for; matrix products, arithmetic and copies ran while one was open for 3% of the time, Pallas kernels for 6%

profile of v2, /device:TPU:0, one launch (start us, length us, event | category | flops | bytes accessed | tf_op | source)
XLA Modules:
  0.0 37.8 jit_solution(11659570030999692542)
XLA Ops:
  0.0 0.5 %collective-permute-start.5 = (bf16[128,1024]{1,0:T(8,128)(2,1)}, bf16[128,1024]{1,0:T(8,128)(2,1)S(1)}, u32[]{:S(2)}, u32[]{:S(2)}) collective-permute-start(bf16[128,1024]{1,0:T(8,128)(2,1)} %param.6), channel_id=1, source_target_pairs={{0,1},{1,0},{2,3},{3,2},{4,5},{5,4},{6,7},{7,6},{8,9},{9,8},{10,11... | collective-permute-start | bytes 786440 | tf_op jit(solution)/shard_map/ppermute | solution.py:34
  0.5 0.1 collective-permute-start.4
  0.5 2.9 %collective-permute-start = (bf16[128,1024]{1,0:T(8,128)(2,1)}, bf16[128,1024]{1,0:T(8,128)(2,1)S(1)}, u32[]{:S(2)}, u32[]{:S(2)}) collective-permute-start(bf16[128,1024]{1,0:T(8,128)(2,1)} %param.5), channel_id=1, source_target_pairs={{0,2},{2,0},{1,3},{3,1},{4,6},{6,4},{5,7},{7,5},{8,10},{10,8},{9,1... | collective-permute-start | bytes 786440 | tf_op jit(solution)/shard_map/ppermute | solution.py:178
  3.5 3.6 %collective-permute-start.3 = (bf16[64,128]{1,0:T(8,128)(2,1)}, bf16[64,128]{1,0:T(8,128)(2,1)S(1)}, u32[]{:S(2)}, u32[]{:S(2)}) collective-permute-start(bf16[64,128]{1,0:T(8,128)(2,1)} %bitcast.13), channel_id=1, source_target_pairs={{0,12},{4,8},{8,4},{12,0},{1,13},{5,9},{9,5},{13,1},{2,14},{6,10},... | collective-permute-start | bytes 49160 | tf_op jit(solution)/shard_map/ppermute | solution.py:183
  7.1 0.0 collective-permute-start.2
  7.1 0.0 collective-permute-done.5.other_next
  7.1 0.8 %collective-permute-start.1 = (bf16[64,128]{1,0:T(8,128)(2,1)}, bf16[64,128]{1,0:T(8,128)(2,1)S(1)}, u32[]{:S(2)}, u32[]{:S(2)}) collective-permute-start(bf16[64,128]{1,0:T(8,128)(2,1)} %bitcast.15), channel_id=1, source_target_pairs={{0,4},{4,0},{8,12},{12,8},{1,5},{5,1},{9,13},{13,9},{2,6},{6,2},{1... | collective-permute-start | bytes 49160 | tf_op jit(solution)/shard_map/ppermute | solution.py:183
  7.8 0.0 copy-start.1
  7.8 1.1 %pad_maximum_fusion.own = bf16[2,128,1024]{2,1,0:T(8,128)(2,1)S(1)} fusion(bf16[1,128,1024]{2,1,0:T(8,128)(2,1)} %bitcast.11, bf16[1,128,1024]{2,1,0:T(8,128)(2,1)} %bitcast.12), kind=kLoop, calls=%fused_computation | loop fusion | flops 262144 | bytes 1048576 | tf_op jit(solution)/shard_map/stack | solution.py:188
  8.9 0.0 copy-start
  9.0 0.0 collective-permute-done.4.other
  9.0 1.8 %begin_transform.1 = (f32[256,512]{1,0:T(8,128)S(1)}, bf16[2048,256]{1,0:T(8,128)(2,1)S(1)}) custom-call(bf16[2,128,1024]{2,1,0:T(8,128)(2,1)S(1)} %pad_maximum_fusion.own, bf16[128,1024]{1,0:T(8,128)(2,1)S(1)} %collective-permute-done.4.other, bf16[128,1024]{1,0:T(8,128)(2,1)S(1)} %collective-permute-done.5.other_next, ...), custom_call_target="tpu_custom_call" | custom-call | tf_op jit(solution)/shard_map/begin_transform/pallas_call | solution.py:191
  10.8 0.0 collective-permute-done.3
  10.8 1.1 %collective-permute-done.2 = bf16[64,128]{1,0:T(8,128)(2,1)S(1)} collective-permute-done((bf16[64,128]{1,0:T(8,128)(2,1)}, bf16[64,128]{1,0:T(8,128)(2,1)S(1)}, u32[]{:S(2)}, u32[]{:S(2)}) %collective-permute-start.2) | collective-permute-done | bytes 16416 | tf_op jit(solution)/shard_map/ppermute | solution.py:183
  11.9 0.0 collective-permute-done.1
  11.9 0.0 collective-permute-done.refs_0_
  11.9 0.0 collective-permute-start.6
  11.9 1.5 %collective-permute-done.6.refs_1_ = bf16[128,1024]{1,0:T(8,128)(2,1)S(1)} collective-permute-done((bf16[128,1024]{1,0:T(8,128)(2,1)S(1)}, bf16[128,1024]{1,0:T(8,128)(2,1)S(1)}, u32[]{:S(2)}, u32[]{:S(2)}) %collective-permute-start.6) | collective-permute-done | bytes 262176 | tf_op jit(solution)/shard_map/ppermute | solution.py:34
  13.4 0.5 %finish_transform.1.refs_0_ = bf16[256,512]{1,0:T(8,128)(2,1)S(1)} custom-call(bf16[128,1024]{1,0:T(8,128)(2,1)S(1)} %collective-permute-done.refs_0_, bf16[128,1024]{1,0:T(8,128)(2,1)S(1)} %collective-permute-done.6.refs_1_, bf16[2048,256]{1,0:T(8,128)(2,1)S(1)} %get-tuple-element.16.refs_2_, f32[256,512]{1,0:T(8,128)S(1)} %get-tuple-element.17.refs_3_), custom_call_target="tpu_custom_call" | custom-call | tf_op jit(solution)/shard_map/finish_transform/pallas_call | solution.py:204
  13.9 2.1 %collective-permute-start.7 = (bf16[256,512]{1,0:T(8,128)(2,1)S(1)}, bf16[256,512]{1,0:T(8,128)(2,1)S(1)}, u32[]{:S(2)}, u32[]{:S(2)}) collective-permute-start(bf16[256,512]{1,0:T(8,128)(2,1)S(1)} %finish_transform.1.refs_0_), channel_id=1, source_target_pairs={{0,8},{8,12},{12,4},{4,0},{1,9},{9,13},{13,5},{5,1},{2,10},{10,14}... | collective-permute-start | bytes 786440 | tf_op jit(solution)/shard_map/ppermute | solution.py:232
  16.0 0.0 collective-permute-start.8
  16.0 6.7 %collective-permute-done.7.refs_1_ = bf16[256,512]{1,0:T(8,128)(2,1)S(1)} collective-permute-done((bf16[256,512]{1,0:T(8,128)(2,1)S(1)}, bf16[256,512]{1,0:T(8,128)(2,1)S(1)}, u32[]{:S(2)}, u32[]{:S(2)}) %collective-permute-start.7) | collective-permute-done | bytes 262176 | tf_op jit(solution)/shard_map/ppermute | solution.py:232
  22.7 0.7 %collective-permute-start.9 = (bf16[256,512]{1,0:T(8,128)(2,1)S(1)}, bf16[256,512]{1,0:T(8,128)(2,1)S(1)}, u32[]{:S(2)}, u32[]{:S(2)}) collective-permute-start(bf16[256,512]{1,0:T(8,128)(2,1)S(1)} %finish_transform.1.refs_0_), channel_id=1, source_target_pairs={{4,8},{8,4},{5,9},{9,5},{6,10},{10,6},{7,11},{11,7},{20,24},{24,20... | collective-permute-start | bytes 786440 | tf_op jit(solution)/shard_map/ppermute | solution.py:235
  23.4 1.3 %collective-permute-start.10 = (bf16[256,512]{1,0:T(8,128)(2,1)S(1)}, bf16[256,512]{1,0:T(8,128)(2,1)S(1)}, u32[]{:S(2)}, u32[]{:S(2)}) collective-permute-start(bf16[256,512]{1,0:T(8,128)(2,1)S(1)} %collective-permute-done.7.refs_1_), channel_id=1, source_target_pairs={{8,12},{4,0},{9,13},{5,1},{10,14},{6,2},{11,15},{7,3},{24,28},{20,... | collective-permute-start | bytes 786440 | tf_op jit(solution)/shard_map/ppermute | solution.py:236
  24.7 0.0 copy-done.1
  24.7 0.1 collective-permute-start.11
  24.8 1.2 %collective-permute-done.11.refs_1_ = bf16[4,64,128]{2,1,0:T(8,128)(2,1)S(1)} collective-permute-done((bf16[4,64,128]{2,1,0:T(8,128)(2,1)S(1)}, bf16[4,64,128]{2,1,0:T(8,128)(2,1)S(1)}, u32[]{:S(2)}, u32[]{:S(2)}) %collective-permute-start.11) | collective-permute-done | bytes 65568 | tf_op jit(solution)/shard_map/ppermute | solution.py:34
  26.0 0.3 band_matrix.1.refs_5_
  26.3 2.5 %collective-permute-done.8.refs_2_ = bf16[256,512]{1,0:T(8,128)(2,1)S(1)} collective-permute-done((bf16[256,512]{1,0:T(8,128)(2,1)S(1)}, bf16[256,512]{1,0:T(8,128)(2,1)S(1)}, u32[]{:S(2)}, u32[]{:S(2)}) %collective-permute-start.8) | collective-permute-done | bytes 262176 | tf_op jit(solution)/shard_map/ppermute | solution.py:233
  28.9 0.0 collective-permute-done.9.refs_3_
  28.9 5.6 %collective-permute-done.10.refs_4_ = bf16[256,512]{1,0:T(8,128)(2,1)S(1)} collective-permute-done((bf16[256,512]{1,0:T(8,128)(2,1)S(1)}, bf16[256,512]{1,0:T(8,128)(2,1)S(1)}, u32[]{:S(2)}, u32[]{:S(2)}) %collective-permute-start.10) | collective-permute-done | bytes 262176 | tf_op jit(solution)/shard_map/ppermute | solution.py:236
  34.5 0.0 copy-done
  34.5 3.2 %cross.1 = f32[4,2,256,256]{3,2,1,0:T(8,128)} custom-call(s32[1,4]{1,0:T(1,128)S(1)} %copy-done, bf16[256,512]{1,0:T(8,128)(2,1)S(1)} %finish_transform.1.refs_0_, bf16[256,512]{1,0:T(8,128)(2,1)S(1)} %collective-permute-done.7.refs_1_, bf16[256,512]{1,0:T(8,128)(2,1)S(1)} %collective-permute-done.8.refs_2_, ...), custom_call_target="tpu_custom_call" | custom-call | tf_op jit(solution)/shard_map/cross/pallas_call | solution.py:250
  (1 shorter events, 0.0 us)
Async XLA Ops:
  0.0 7.1 %collective-permute-start.5 = (bf16[128,1024]{1,0:T(8,128)(2,1)}, bf16[128,1024]{1,0:T(8,128)(2,1)S(1)}, u32[]{:S(2)}, u32[]{:S(2)}) collective-permute-start(bf16[128,1024]{1,0:T(8,128)(2,1)} %param.6), channel_id=1, source_target_pairs={{0,1},{1,0},{2,3},{3,2},{4,5},{5,4},{6,7},{7,6},{8,9},{9,8},{10,11... | collective-permute-start | bytes 786440 | tf_op jit(solution)/shard_map/ppermute | solution.py:34
  0.5 8.5 %collective-permute-start.4 = (bf16[128,1024]{1,0:T(8,128)(2,1)}, bf16[128,1024]{1,0:T(8,128)(2,1)S(1)}, u32[]{:S(2)}, u32[]{:S(2)}) collective-permute-start(bf16[128,1024]{1,0:T(8,128)(2,1)} %param.5), channel_id=1, source_target_pairs={{0,1},{1,0},{2,3},{3,2},{4,5},{5,4},{6,7},{7,6},{8,9},{9,8},{10,11... | collective-permute-start | bytes 786440 | tf_op jit(solution)/shard_map/ppermute | solution.py:34
  0.5 11.4 %collective-permute-start = (bf16[128,1024]{1,0:T(8,128)(2,1)}, bf16[128,1024]{1,0:T(8,128)(2,1)S(1)}, u32[]{:S(2)}, u32[]{:S(2)}) collective-permute-start(bf16[128,1024]{1,0:T(8,128)(2,1)} %param.5), channel_id=1, source_target_pairs={{0,2},{2,0},{1,3},{3,1},{4,6},{6,4},{5,7},{7,5},{8,10},{10,8},{9,1... | collective-permute-start | bytes 786440 | tf_op jit(solution)/shard_map/ppermute | solution.py:178
  3.5 7.3 %collective-permute-start.3 = (bf16[64,128]{1,0:T(8,128)(2,1)}, bf16[64,128]{1,0:T(8,128)(2,1)S(1)}, u32[]{:S(2)}, u32[]{:S(2)}) collective-permute-start(bf16[64,128]{1,0:T(8,128)(2,1)} %bitcast.13), channel_id=1, source_target_pairs={{0,12},{4,8},{8,4},{12,0},{1,13},{5,9},{9,5},{13,1},{2,14},{6,10},... | collective-permute-start | bytes 49160 | tf_op jit(solution)/shard_map/ppermute | solution.py:183
  7.1 4.8 %collective-permute-start.2 = (bf16[64,128]{1,0:T(8,128)(2,1)}, bf16[64,128]{1,0:T(8,128)(2,1)S(1)}, u32[]{:S(2)}, u32[]{:S(2)}) collective-permute-start(bf16[64,128]{1,0:T(8,128)(2,1)} %bitcast.14), channel_id=1, source_target_pairs={{0,8},{4,12},{8,0},{12,4},{1,9},{5,13},{9,1},{13,5},{2,10},{6,14},... | collective-permute-start | bytes 49160 | tf_op jit(solution)/shard_map/ppermute | solution.py:183
  7.1 4.8 %collective-permute-start.1 = (bf16[64,128]{1,0:T(8,128)(2,1)}, bf16[64,128]{1,0:T(8,128)(2,1)S(1)}, u32[]{:S(2)}, u32[]{:S(2)}) collective-permute-start(bf16[64,128]{1,0:T(8,128)(2,1)} %bitcast.15), channel_id=1, source_target_pairs={{0,4},{4,0},{8,12},{12,8},{1,5},{5,1},{9,13},{13,9},{2,6},{6,2},{1... | collective-permute-start | bytes 49160 | tf_op jit(solution)/shard_map/ppermute | solution.py:183
  7.8 16.8 %copy-start.1 = (bf16[128,64]{0,1:T(8,128)(2,1)S(1)}, bf16[128,64]{0,1:T(8,128)(2,1)}, u32[]{:S(2)}) copy-start(bf16[128,64]{0,1:T(8,128)(2,1)} %param.7) | copy-start | bytes 49156
  8.9 25.6 %copy-start = (s32[1,4]{1,0:T(1,128)S(1)}, s32[1,4]{1,0:T(1,128)}, u32[]{:S(2)}) copy-start(s32[1,4]{1,0:T(1,128)} %slots.1) | copy-start | bytes 52
  11.9 1.5 %collective-permute-start.6 = (bf16[128,1024]{1,0:T(8,128)(2,1)S(1)}, bf16[128,1024]{1,0:T(8,128)(2,1)S(1)}, u32[]{:S(2)}, u32[]{:S(2)}) collective-permute-start(bf16[128,1024]{1,0:T(8,128)(2,1)S(1)} %collective-permute-done.refs_0_), channel_id=1, source_target_pairs={{0,1},{1,0},{2,3},{3,2},{4,5},{5,4},{6,7},{7,6},{8,9},{9,8},{10,11... | collective-permute-start | bytes 786440 | tf_op jit(solution)/shard_map/ppermute | solution.py:34
  13.9 8.8 %collective-permute-start.7 = (bf16[256,512]{1,0:T(8,128)(2,1)S(1)}, bf16[256,512]{1,0:T(8,128)(2,1)S(1)}, u32[]{:S(2)}, u32[]{:S(2)}) collective-permute-start(bf16[256,512]{1,0:T(8,128)(2,1)S(1)} %finish_transform.1.refs_0_), channel_id=1, source_target_pairs={{0,8},{8,12},{12,4},{4,0},{1,9},{9,13},{13,5},{5,1},{2,10},{10,14}... | collective-permute-start | bytes 786440 | tf_op jit(solution)/shard_map/ppermute | solution.py:232
  16.0 12.9 %collective-permute-start.8 = (bf16[256,512]{1,0:T(8,128)(2,1)S(1)}, bf16[256,512]{1,0:T(8,128)(2,1)S(1)}, u32[]{:S(2)}, u32[]{:S(2)}) collective-permute-start(bf16[256,512]{1,0:T(8,128)(2,1)S(1)} %finish_transform.1.refs_0_), channel_id=1, source_target_pairs={{4,12},{12,8},{8,0},{0,4},{5,13},{13,9},{9,1},{1,5},{6,14},{14,10}... | collective-permute-start | bytes 786440 | tf_op jit(solution)/shard_map/ppermute | solution.py:233
  22.7 6.2 %collective-permute-start.9 = (bf16[256,512]{1,0:T(8,128)(2,1)S(1)}, bf16[256,512]{1,0:T(8,128)(2,1)S(1)}, u32[]{:S(2)}, u32[]{:S(2)}) collective-permute-start(bf16[256,512]{1,0:T(8,128)(2,1)S(1)} %finish_transform.1.refs_0_), channel_id=1, source_target_pairs={{4,8},{8,4},{5,9},{9,5},{6,10},{10,6},{7,11},{11,7},{20,24},{24,20... | collective-permute-start | bytes 786440 | tf_op jit(solution)/shard_map/ppermute | solution.py:235
  23.4 11.1 %collective-permute-start.10 = (bf16[256,512]{1,0:T(8,128)(2,1)S(1)}, bf16[256,512]{1,0:T(8,128)(2,1)S(1)}, u32[]{:S(2)}, u32[]{:S(2)}) collective-permute-start(bf16[256,512]{1,0:T(8,128)(2,1)S(1)} %collective-permute-done.7.refs_1_), channel_id=1, source_target_pairs={{8,12},{4,0},{9,13},{5,1},{10,14},{6,2},{11,15},{7,3},{24,28},{20,... | collective-permute-start | bytes 786440 | tf_op jit(solution)/shard_map/ppermute | solution.py:236
  24.7 1.3 %collective-permute-start.11 = (bf16[4,64,128]{2,1,0:T(8,128)(2,1)S(1)}, bf16[4,64,128]{2,1,0:T(8,128)(2,1)S(1)}, u32[]{:S(2)}, u32[]{:S(2)}) collective-permute-start(bf16[4,64,128]{2,1,0:T(8,128)(2,1)S(1)} %pad_maximum_fusion.1.refs_0_), channel_id=1, source_target_pairs={{0,1},{1,0},{2,3},{3,2},{4,5},{5,4},{6,7},{7,6},{8,9},{9,8},{10,11... | collective-permute-start | bytes 196616 | tf_op jit(solution)/shard_map/ppermute | solution.py:34

commit v3 on v2

v3 whole, which is shorter than its diff:
```python
import functools
import math

import jax
import jax.numpy as jnp
import ml_dtypes
import numpy as np
from jax import lax
from jax.experimental import pallas as pl
from jax.experimental.pallas import tpu as pltpu
from jax.sharding import PartitionSpec as P

FB = 512
REACH = 3
SLOTS = 4
LANES = 128


def band_tables(spans, halves, length):
    samples = np.arange(length, dtype=np.int64)[:, None]
    bins = np.arange(FB, dtype=np.int64)[None, :]
    phase = (samples * bins % length).astype(np.float32)
    angle = np.float32(2.0 * math.pi / length) * phase
    ramp = np.float32(2.0 * math.pi / length) * np.arange(length, dtype=np.float32)
    taper = (np.float32(0.5) - np.float32(0.5) * np.cos(ramp))[:, None]
    normaliser = np.float32(1.0 / math.sqrt(0.375 * length))
    cosine = (taper * np.cos(angle) * normaliser).astype(ml_dtypes.bfloat16)
    sine = (-taper * np.sin(angle) * normaliser).astype(ml_dtypes.bfloat16)
    both = np.stack([cosine, sine], axis=1).reshape(length, 2, spans, halves, -1)
    return np.ascontiguousarray(both.transpose(2, 0, 3, 1, 4)).reshape(spans, length, -1)


def swapped(value, axis):
    return lax.ppermute(value, axis, [(0, 1), (1, 0)])


def block_of(own, other):
    low = lax.axis_index("freq") == 0
    a, b = own[...], other[...]
    return jnp.concatenate([jnp.where(low, a, b), jnp.where(low, b, a)], axis=0)


def hop_part(place, segment, value, table):
    hop = value.shape[1]
    half = place - segment
    start = pl.multiple_of(jnp.clip(half, 0, 1) * hop, hop)
    product = jnp.dot(value, table[pl.ds(start, hop), :], preferred_element_type=jnp.float32)
    return jnp.where((half == 0) | (half == 1), product, 0.0)


def begin_kernel(own, tables, total, table, sems):
    span = lax.axis_index("tm")
    copy = pltpu.make_async_copy(tables.at[span], table, sems.at[0])
    copy.start()
    width = table.shape[1]
    segments = total.shape[1] // width
    copy.wait()
    for segment in range(segments):
        value = hop_part(span, segment, own[0], table)
        if segment == segments - 1:
            value += hop_part(segments, segment, own[1], table)
        total[:, segment * width : (segment + 1) * width] = value


def finish_kernel(spans, *refs):
    hops, (table, begun, mine, theirs) = refs[: spans - 1], refs[spans - 1 :]
    width = table.shape[1]
    part = width // 2
    low = lax.axis_index("freq") == 0
    for segment in range(spans):
        value = begun[:, segment * width : (segment + 1) * width]
        for step in range(1, spans):
            place = lax.rem(lax.axis_index("tm") - step + spans, spans)
            value += hop_part(place, segment, hops[step - 1][...], table)
        first, second = value[:, :part].astype(jnp.bfloat16), value[:, part:].astype(jnp.bfloat16)
        columns = slice(segment * part, (segment + 1) * part)
        mine[:, columns] = jnp.where(low, first, second)
        theirs[:, columns] = jnp.where(low, second, first)


def block_kernel(own, other, out):
    out[...] = block_of(own, other)


def band_kernel(chain, *refs):
    *weights, out = refs
    blocks, rows, width = out.shape
    here = lax.axis_index("chan")
    low = lax.axis_index("freq") == 0
    for block in range(blocks):
        if chain == 4:
            own, other = (ref[block].astype(jnp.float32) for ref in weights)
            place = jnp.bitwise_xor(here, block)
            tile = jnp.concatenate([jnp.where(low, own, other), jnp.where(low, other, own)], axis=1).T
        else:
            place = block
            tile = weights[0][block * rows : (block + 1) * rows, :].astype(jnp.float32)
        blank = jnp.zeros((rows, width - tile.shape[1]), jnp.float32)
        wide = jnp.concatenate([tile, blank], axis=1)
        out[place] = pltpu.roll(wide, 0, 1, stride=1, stride_axis=0).astype(jnp.bfloat16)


def whitened(band, window, raw):
    predicted = jnp.dot(band, window, preferred_element_type=jnp.float32)
    return (raw.astype(jnp.float32) - predicted).astype(jnp.bfloat16)


def pair_products(slots, spectra, mine, base, segments, scaling, out, left, result, sems):
    count, rows, columns = spectra.shape
    own = spectra[mine]
    left[:rows, :] = own
    half = columns // (2 * segments)
    turned = []
    for segment in range(segments):
        start = 2 * segment * half
        turned += [own[:, start + half : start + 2 * half], -own[:, start : start + half]]
    left[rows:, :] = jnp.concatenate(turned, axis=1)

    contract = (((1,), (1,)), ((), ()))
    for slot in range(SLOTS):
        partner = slots[0, slot]
        theirs = spectra[jnp.clip(partner - base, 0, count - 1)]
        both = lax.dot_general(left[...], theirs, contract, preferred_element_type=jnp.float32)
        both = jnp.where(partner >= 0, both * scaling, 0.0)
        result[slot, 0] = both[:rows]
        result[slot, 1] = both[rows:]
        pltpu.make_async_copy(result.at[slot], out.at[slot], sems.at[slot]).start()
    for slot in range(SLOTS):
        pltpu.make_async_copy(result.at[slot], out.at[slot], sems.at[slot]).wait()


def cross_kernel(segments, scaling, slots, *refs):
    near = [0] + [d for d in range(-REACH, REACH + 1) if d]
    blocks, (before, after, band, out, padded, spectra, left, result, sems) = refs[: len(near)], refs[len(near) :]
    count, rows, columns = spectra.shape
    rim = before.shape[0]
    edge = count * rows + rim
    padded[:rim, :] = before[...]
    padded[edge : edge + rim, :] = after[...]
    padded[edge + rim :, :] = jnp.zeros((padded.shape[0] - edge - rim, columns), jnp.bfloat16)
    for distance, value in zip(near, blocks):
        start = (distance + REACH) * rows + rim
        padded[start : start + rows, :] = value[...]
    for block in range(count):
        start = block * rows
        window = padded[start : start + band.shape[2], :]
        spectra[block] = whitened(band[block], window, padded[start + rim : start + rim + rows, :])
    base = lax.axis_index("chan") - REACH
    pair_products(slots, spectra, REACH, base, segments, scaling, out, left, result, sems)


def chosen(a, b, c, d):
    here = lax.axis_index("chan")
    return jnp.where(here == 0, a, jnp.where(here == 1, b, jnp.where(here == 2, c, d)))


def relay_kernel(raw, first, first_other, arrived, down, up):
    here = lax.axis_index("chan")
    value = block_of(first, first_other)
    arrived[...] = value
    down[...] = jnp.where(here == 1, value, raw[...])
    up[...] = jnp.where(here == 2, value, raw[...])


def early_kernel(raw, first, second, band, padded, spectra):
    count, rows, columns = spectra.shape
    rim = (padded.shape[0] - count * rows) // 4
    edge = count * rows + rim
    padded[:rim, :] = jnp.zeros((rim, columns), jnp.bfloat16)
    padded[edge:, :] = jnp.zeros((3 * rim, columns), jnp.bfloat16)
    last = chosen(3, 2, 1, 0)
    padded[pl.ds(pl.multiple_of(last * rows + rim, rim), rows), :] = jnp.zeros((rows, columns), jnp.bfloat16)
    for place, value in (
        (lax.axis_index("chan"), raw),
        (chosen(1, 3, 0, 2), first),
        (chosen(2, 0, 3, 1), second),
    ):
        padded[pl.ds(pl.multiple_of(place * rows + rim, rim), rows), :] = value[...]
    for block in range(count):
        start = block * rows
        window = padded[start : start + band.shape[2], :]
        spectra[block] = whitened(band[block], window, padded[start + rim : start + rim + rows, :])


def late_kernel(segments, scaling, slots, padded, early, third, fourth, band, out, spectra, left, result, sems):
    count, rows, columns = spectra.shape
    width = band.shape[2]
    rim = (padded.shape[0] - count * rows) // 4
    here = lax.axis_index("chan")
    last = chosen(3, 2, 1, 0)
    value = jnp.where(here <= 1, third[...], fourth[...])
    spectra[...] = early[...]

    start = pl.multiple_of(last * rows, rows)
    above = padded[pl.ds(start, rim), :]
    below = padded[pl.ds(start + rim + rows, width - rim - rows), :]
    window = jnp.concatenate([above, value, below], axis=0)
    spectra[last] = whitened(band[last], window, value)

    @pl.when(last > 0)
    def _():
        block = last - 1
        half = rows // 2
        upper = padded[pl.ds(pl.multiple_of(start - half, half), half + rim), :]
        window = jnp.concatenate([upper, value[: width - rows - rim]], axis=0)
        strip = whitened(band[block, rows - rim :, half:], window, above)
        spectra[block, rows - rim :, :] = strip

    @pl.when(last < count - 1)
    def _():
        block = last + 1
        lower = padded[pl.ds(start + rows + rim, LANES - rim), :]
        window = jnp.concatenate([value[rows - rim :], lower], axis=0)
        strip = whitened(band[block, :rim, :LANES], window, lower[:rim])
        spectra[block, :rim, :] = strip

    pair_products(slots, spectra, here, 0, segments, scaling, out, left, result, sems)


def local(tables, recording, trailing, whiten_filter, pair_list):
    rows, hop = recording.shape
    spans, halves, chain = (lax.axis_size(axis) for axis in ("tm", "freq", "chan"))
    bands = spans * halves
    bins2 = 2 * FB // bands
    block_rows = halves * rows
    taps = whiten_filter.shape[1]
    rim = taps // 2
    here = lax.axis_index("chan")

    in_vmem = pl.BlockSpec(memory_space=pltpu.VMEM)
    small = pltpu.CompilerParams(vmem_limit_bytes=16 * 2**20)

    received = [
        lax.ppermute(recording, "tm", [(i, (i + step) % spans) for i in range(spans)])
        for step in range(1, spans)
    ]
    if chain == 4:
        filters = [
            lax.ppermute(whiten_filter.T, "chan", [(i, i ^ step) for i in range(chain)])
            for step in range(1, chain)
        ]
    else:
        filters = [lax.all_gather(whiten_filter, ("chan", "freq"), axis=0, tiled=True)]
    own = jnp.stack([recording, trailing])
    total = (block_rows, spans * bins2)
    in_hbm = pl.BlockSpec(memory_space=pltpu.HBM)
    begun, table = pl.pallas_call(
        begin_kernel,
        out_shape=[
            jax.ShapeDtypeStruct((rows, halves * total[1]), jnp.float32),
            jax.ShapeDtypeStruct(tables.shape[1:], jnp.bfloat16),
        ],
        in_specs=[in_vmem, in_hbm],
        out_specs=[in_vmem, in_vmem],
        scratch_shapes=[pltpu.SemaphoreType.DMA((1,))],
        compiler_params=pltpu.CompilerParams(vmem_limit_bytes=48 * 2**20),
        name="begin_transform",
    )(own, jnp.asarray(tables))
    received, filters, begun = lax.optimization_barrier((received, filters, begun))
    half_rows = (rows, total[1])
    mine, theirs = pl.pallas_call(
        functools.partial(finish_kernel, spans),
        out_shape=[jax.ShapeDtypeStruct(half_rows, jnp.bfloat16)] * 2,
        in_specs=[in_vmem] * (spans + 1),
        out_specs=[in_vmem] * 2,
        compiler_params=small,
        name="finish_transform",
    )(*received, table, begun)
    raw = pl.pallas_call(
        block_kernel,
        out_shape=jax.ShapeDtypeStruct(total, jnp.bfloat16),
        in_specs=[in_vmem] * 2,
        out_specs=in_vmem,
        compiler_params=small,
        name="block",
    )(mine, swapped(theirs, "freq"))

    if chain == 4:
        near = chain
        weights = jnp.stack([whiten_filter.T, *filters])
        weights = (weights, swapped(weights, "freq"))
    else:
        near = 2 * REACH + 1
        beyond = jnp.pad(filters[0], ((REACH * block_rows, REACH * block_rows), (0, 0)))
        weights = (lax.dynamic_slice_in_dim(beyond, here * block_rows, near * block_rows, 0),)
    window = -(-(block_rows + taps) // LANES) * LANES
    band = pl.pallas_call(
        functools.partial(band_kernel, chain),
        out_shape=jax.ShapeDtypeStruct((near, block_rows, window), jnp.bfloat16),
        in_specs=[in_vmem] * len(weights),
        out_specs=in_vmem,
        compiler_params=small,
        name="band_matrix",
    )(*weights)

    if chain == 4:
        route = [(0, 2), (2, 3), (3, 1), (1, 0)]
        first = lax.ppermute(mine, "chan", route)
        across = [(2 * i + half, 2 * j + 1 - half) for i, j in route for half in range(2)]
        first_other = lax.ppermute(theirs, ("chan", "freq"), across)
        second = lax.ppermute(raw, "chan", [(1, 3), (3, 2), (2, 0), (0, 1)])
        first, down, up = pl.pallas_call(
            relay_kernel,
            out_shape=[jax.ShapeDtypeStruct(total, jnp.bfloat16)] * 3,
            in_specs=[in_vmem] * 3,
            out_specs=[in_vmem] * 3,
            compiler_params=small,
            name="relay",
        )(raw, first, first_other)
        third = lax.ppermute(down, "chan", [(1, 0), (2, 1)])
        fourth = lax.ppermute(up, "chan", [(2, 3), (1, 2)])
    else:

        def shifted(value, distance):
            route = [(i - distance, i) for i in range(chain) if 0 <= i - distance < chain]
            return lax.ppermute(value, "chan", route)

        blocks = [raw]
        blocks += [shifted(raw, -d) for d in range(-REACH, REACH + 1) if d]
        blocks.append(shifted(raw[block_rows - rim :, :], REACH + 1))
        blocks.append(shifted(raw[:rim, :], -REACH - 1))

    padded = (near * block_rows + 4 * rim, total[1])
    spectra = (near, *total)
    if chain == 4:
        operands = pl.pallas_call(
            early_kernel,
            out_shape=[jax.ShapeDtypeStruct(shape, jnp.bfloat16) for shape in (padded, spectra)],
            in_specs=[in_vmem] * 4,
            out_specs=[in_vmem] * 2,
            compiler_params=small,
            name="early_whitening",
        )(raw, first, second, band)
        operands = (*operands, third, fourth, band)
        kernel, scratch = late_kernel, []
    else:
        operands = (*blocks, band)
        kernel, scratch = cross_kernel, [pltpu.VMEM(padded, jnp.bfloat16)]
    out_shape = (SLOTS, 2, block_rows, block_rows)
    result = pl.pallas_call(
        functools.partial(kernel, spans, 1.0 / math.sqrt(spans * bins2 // 2)),
        out_shape=jax.ShapeDtypeStruct(out_shape, jnp.float32),
        in_specs=[pl.BlockSpec(memory_space=pltpu.SMEM)] + [in_vmem] * len(operands),
        out_specs=in_hbm,
        scratch_shapes=[
            *scratch,
            pltpu.VMEM(spectra, jnp.bfloat16),
            pltpu.VMEM((2 * block_rows, total[1]), jnp.bfloat16),
            pltpu.VMEM(out_shape, jnp.float32),
            pltpu.SemaphoreType.DMA((SLOTS,)),
        ],
        compiler_params=pltpu.CompilerParams(vmem_limit_bytes=24 * 2**20),
        name="cross",
    )(pair_list, *operands)
    return result.reshape(1, SLOTS, 1, 2, block_rows, block_rows)


def solution(mesh):
    placed = (
        P(("days", "chan", "freq"), "tm"),
        P(("days", "chan", "freq"), None),
        P(("chan", "freq"), None),
        P(("days", "chan"), None),
    )

    def step(recording, trailing, whiten_filter, pair_list):
        tables = band_tables(mesh.shape["tm"], mesh.shape["freq"], 2 * trailing.shape[1])
        return jax.shard_map(
            functools.partial(local, tables),
            mesh=mesh,
            in_specs=placed,
            out_specs=P(("days", "chan"), None, ("tm", "freq"), None, None, None),
            check_vma=False,
        )(recording, trailing, whiten_filter, pair_list)

    return step
```

time: 37.9 us -> 36.1 us (0.953)
  waiting for transfers between devices: 18.8 us -> 14.4 us
  starting transfers between devices: 11.9 us -> 13.5 us
  Pallas kernels: 5.82 us -> 6.72 us
    ppermute x3 -> x4, waiting for transfers between devices: 12.4 us -> 9.47 us  [the longest x1 4.68 us: local(): third = lax.ppermute(down, 'chan', [(1, 0), (2, 1)])]
    ppermute x4 -> x2, waiting for transfers between devices: 2.77 us -> 1.07 us  [swapped(): return lax.ppermute(value, axis, [(0, 1), (1, 0)])]
    ppermute x3 -> x4, starting transfers between devices: 4.04 us -> 5.24 us  [the longest x1 2.07 us: local(): first = lax.ppermute(mine, 'chan', route)]
    pallas_call x3 -> x6, Pallas kernels: 5.53 us -> 6.43 us  [the longest x1 2.83 us: local(): pl.pallas_call(functools.partial(kernel, spans, 1.0 / math.sqrt(spans * b...]
    ppermute x1, starting transfers between devices: 0.01 us -> 0.64 us  [local(): second = lax.ppermute(raw, 'chan', [(1, 3), (3, 2), (2, 0), (0, 1)])]
    ppermute x1, waiting for transfers between devices: 2.54 us -> 3.12 us  [local(): second = lax.ppermute(raw, 'chan', [(1, 3), (3, 2), (2, 0), (0, 1)])]
  transfers between devices with their start and end apart: 12 -> 11, of which waited for: 6 -> 6; matrix products, arithmetic and copies ran while one was open for 3% -> 3% of each run, Pallas kernels for 6% -> 10%
where the time goes in v3:
time: 36.1 us; the launch traced here: 35.9 us
  waiting for transfers between devices  14.4 us (40%)
  starting transfers between devices  13.5 us (37%)
  Pallas kernels  6.72 us (19%)
  other arithmetic  1.09 us (3%)
    ppermute x1, waiting for transfers between devices, local(): third = lax.ppermute(down, 'chan', [(1, 0), (2, 1)])  4.68 us
    ppermute x3, starting transfers between devices, local(): lax.ppermute(whiten_filter.T, 'chan', [(i, i ^ step) for i in range(chain)])  4.39 us
    ppermute x1, waiting for transfers between devices, local(): second = lax.ppermute(raw, 'chan', [(1, 3), (3, 2), (2, 0), (0, 1)])  3.12 us
    ppermute x1, starting transfers between devices, local(): lax.ppermute(recording, 'tm', [(i, (i + step) % spans) for i in range(spa...  2.94 us
    pallas_call x1, Pallas kernels, local(): pl.pallas_call(functools.partial(kernel, spans, 1.0 / math.sqrt(spans * b...  2.83 us
    ppermute x1, waiting for transfers between devices, local(): first = lax.ppermute(mine, 'chan', route)  2.4 us
    ppermute x1, waiting for transfers between devices, local(): first_other = lax.ppermute(theirs, ('chan', 'freq'), across)  2.38 us
    pallas_call x1, Pallas kernels, local(): pl.pallas_call(begin_kernel, out_shape=[jax.ShapeDtypeStruct((rows, halve...  2.2 us
  transfers between devices with their start and end apart: 11, of which 6 were waited for; matrix products, arithmetic and copies ran while one was open for 3% of the time, Pallas kernels for 10%

profile of v3, /device:TPU:0, one launch (start us, length us, event | category | flops | bytes accessed | tf_op | source)
XLA Modules:
  0.0 35.9 jit_solution(11528326489602417263)
XLA Ops:
  0.0 2.9 %collective-permute-start = (bf16[128,1024]{1,0:T(8,128)(2,1)}, bf16[128,1024]{1,0:T(8,128)(2,1)S(1)}, u32[]{:S(2)}, u32[]{:S(2)}) collective-permute-start(bf16[128,1024]{1,0:T(8,128)(2,1)} %param.5), channel_id=1, source_target_pairs={{0,2},{2,0},{1,3},{3,1},{4,6},{6,4},{5,7},{7,5},{8,10},{10,8},{9,1... | collective-permute-start | bytes 786440 | tf_op jit(solution)/shard_map/ppermute | solution.py:234
  2.9 3.6 %collective-permute-start.3 = (bf16[64,128]{1,0:T(8,128)(2,1)}, bf16[64,128]{1,0:T(8,128)(2,1)S(1)}, u32[]{:S(2)}, u32[]{:S(2)}) collective-permute-start(bf16[64,128]{1,0:T(8,128)(2,1)} %bitcast.13), channel_id=1, source_target_pairs={{0,12},{4,8},{8,4},{12,0},{1,13},{5,9},{9,5},{13,1},{2,14},{6,10},... | collective-permute-start | bytes 49160 | tf_op jit(solution)/shard_map/ppermute | solution.py:239
  6.5 0.0 collective-permute-start.2
  6.5 0.8 %collective-permute-start.1 = (bf16[64,128]{1,0:T(8,128)(2,1)}, bf16[64,128]{1,0:T(8,128)(2,1)S(1)}, u32[]{:S(2)}, u32[]{:S(2)}) collective-permute-start(bf16[64,128]{1,0:T(8,128)(2,1)} %bitcast.15), channel_id=1, source_target_pairs={{0,4},{4,0},{8,12},{12,8},{1,5},{5,1},{9,13},{13,9},{2,6},{6,2},{1... | collective-permute-start | bytes 49160 | tf_op jit(solution)/shard_map/ppermute | solution.py:239
  7.3 1.1 %pad_maximum_fusion.own = bf16[2,128,1024]{2,1,0:T(8,128)(2,1)S(1)} fusion(bf16[1,128,1024]{2,1,0:T(8,128)(2,1)} %bitcast.11, bf16[1,128,1024]{2,1,0:T(8,128)(2,1)} %bitcast.12), kind=kLoop, calls=%fused_computation | loop fusion | flops 262144 | bytes 1048576 | tf_op jit(solution)/shard_map/stack | solution.py:244
  8.4 2.2 %begin_transform.1 = (f32[128,1024]{1,0:T(8,128)S(1)}, bf16[2048,512]{1,0:T(8,128)(2,1)S(1)}) custom-call(bf16[2,128,1024]{2,1,0:T(8,128)(2,1)S(1)} %pad_maximum_fusion.own, bf16[2,2048,512]{2,1,0:T(8,128)(2,1)} %constant.2.clone.tables), custom_call_target="tpu_custom_call" | custom-call | tf_op jit(solution)/shard_map/begin_transform/pallas_call | solution.py:247
  10.6 0.0 copy-start.1
  10.6 0.0 collective-permute-done.3
  10.6 0.7 %collective-permute-done.2 = bf16[64,128]{1,0:T(8,128)(2,1)S(1)} collective-permute-done((bf16[64,128]{1,0:T(8,128)(2,1)}, bf16[64,128]{1,0:T(8,128)(2,1)S(1)}, u32[]{:S(2)}, u32[]{:S(2)}) %collective-permute-start.2) | collective-permute-done | bytes 16416 | tf_op jit(solution)/shard_map/ppermute | solution.py:239
  11.4 0.0 collective-permute-done.1
  11.4 0.0 collective-permute-done.refs_0_
  11.4 0.5 %finish_transform.1 = (bf16[128,512]{1,0:T(8,128)(2,1)S(1)}, bf16[128,512]{1,0:T(8,128)(2,1)S(1)}) custom-call(bf16[128,1024]{1,0:T(8,128)(2,1)S(1)} %collective-permute-done.refs_0_, bf16[2048,512]{1,0:T(8,128)(2,1)S(1)} %get-tuple-element.21.refs_1_, f32[128,1024]{1,0:T(8,128)S(1)} %get-tuple-element.22.refs_2_), custom_call_target="tpu_custom_call" | custom-call | tf_op jit(solution)/shard_map/finish_transform/pallas_call | solution.py:261
  11.9 0.0 copy-start
  11.9 0.1 collective-permute-start.4
  12.0 2.1 %collective-permute-start.5 = (bf16[128,512]{1,0:T(8,128)(2,1)S(1)}, bf16[128,512]{1,0:T(8,128)(2,1)S(1)}, u32[]{:S(2)}, u32[]{:S(2)}) collective-permute-start(bf16[128,512]{1,0:T(8,128)(2,1)S(1)} %get-tuple-element.23.own), channel_id=1, source_target_pairs={{0,8},{8,12},{12,4},{4,0},{1,9},{9,13},{13,5},{5,1},{2,10},{10,14}... | collective-permute-start | bytes 393224 | tf_op jit(solution)/shard_map/ppermute | solution.py:298
  14.0 1.2 %collective-permute-start.6 = (bf16[128,512]{1,0:T(8,128)(2,1)S(1)}, bf16[128,512]{1,0:T(8,128)(2,1)S(1)}, u32[]{:S(2)}, u32[]{:S(2)}) collective-permute-start(bf16[128,512]{1,0:T(8,128)(2,1)S(1)} %get-tuple-element.24), channel_id=1, source_target_pairs={{0,9},{1,8},{8,13},{9,12},{12,5},{13,4},{4,1},{5,0},{2,11},{3,10},... | collective-permute-start | bytes 393224 | tf_op jit(solution)/shard_map/ppermute | solution.py:300
  15.2 0.0 collective-permute-done.4.other
  15.3 0.6 %collective-permute-start.7 = (bf16[256,512]{1,0:T(8,128)(2,1)S(1)}, bf16[256,512]{1,0:T(8,128)(2,1)S(1)}, u32[]{:S(2)}, u32[]{:S(2)}) collective-permute-start(bf16[256,512]{1,0:T(8,128)(2,1)S(1)} %block.1.raw), channel_id=1, source_target_pairs={{4,12},{12,8},{8,0},{0,4},{5,13},{13,9},{9,1},{1,5},{6,14},{14,10}... | collective-permute-start | bytes 786440 | tf_op jit(solution)/shard_map/ppermute | solution.py:301
  15.9 2.4 %collective-permute-done.5.first = bf16[128,512]{1,0:T(8,128)(2,1)S(1)} collective-permute-done((bf16[128,512]{1,0:T(8,128)(2,1)S(1)}, bf16[128,512]{1,0:T(8,128)(2,1)S(1)}, u32[]{:S(2)}, u32[]{:S(2)}) %collective-permute-start.5) | collective-permute-done | bytes 131104 | tf_op jit(solution)/shard_map/ppermute | solution.py:298
  18.3 2.4 %collective-permute-done.6.first_other = bf16[128,512]{1,0:T(8,128)(2,1)S(1)} collective-permute-done((bf16[128,512]{1,0:T(8,128)(2,1)S(1)}, bf16[128,512]{1,0:T(8,128)(2,1)S(1)}, u32[]{:S(2)}, u32[]{:S(2)}) %collective-permute-start.6) | collective-permute-done | bytes 131104 | tf_op jit(solution)/shard_map/ppermute | solution.py:300
  20.7 0.1 relay.1
  20.8 1.3 %collective-permute-start.9 = (bf16[256,512]{1,0:T(8,128)(2,1)S(1)}, bf16[256,512]{1,0:T(8,128)(2,1)S(1)}, u32[]{:S(2)}, u32[]{:S(2)}) collective-permute-start(bf16[256,512]{1,0:T(8,128)(2,1)S(1)} %get-tuple-element.31), channel_id=1, source_target_pairs={{4,0},{8,4},{5,1},{9,5},{6,2},{10,6},{7,3},{11,7},{20,16},{24,20},... | collective-permute-start | bytes 786440 | tf_op jit(solution)/shard_map/ppermute | solution.py:310
  22.1 0.7 %collective-permute-start.10 = (bf16[256,512]{1,0:T(8,128)(2,1)S(1)}, bf16[256,512]{1,0:T(8,128)(2,1)S(1)}, u32[]{:S(2)}, u32[]{:S(2)}) collective-permute-start(bf16[256,512]{1,0:T(8,128)(2,1)S(1)} %get-tuple-element.32), channel_id=1, source_target_pairs={{8,12},{4,8},{9,13},{5,9},{10,14},{6,10},{11,15},{7,11},{24,28},{2... | collective-permute-start | bytes 786440 | tf_op jit(solution)/shard_map/ppermute | solution.py:311
  22.8 0.0 copy-done.1
  22.8 0.3 collective-permute-start.8
  23.1 1.1 %collective-permute-done.8.refs_1_ = bf16[4,64,128]{2,1,0:T(8,128)(2,1)S(1)} collective-permute-done((bf16[4,64,128]{2,1,0:T(8,128)(2,1)S(1)}, bf16[4,64,128]{2,1,0:T(8,128)(2,1)S(1)}, u32[]{:S(2)}, u32[]{:S(2)}) %collective-permute-start.8) | collective-permute-done | bytes 65568 | tf_op jit(solution)/shard_map/ppermute | solution.py:34
  24.1 0.3 band_matrix.1.band
  24.4 3.1 %collective-permute-done.7.second = bf16[256,512]{1,0:T(8,128)(2,1)S(1)} collective-permute-done((bf16[256,512]{1,0:T(8,128)(2,1)S(1)}, bf16[256,512]{1,0:T(8,128)(2,1)S(1)}, u32[]{:S(2)}, u32[]{:S(2)}) %collective-permute-start.7) | collective-permute-done | bytes 262176 | tf_op jit(solution)/shard_map/ppermute | solution.py:301
  27.5 0.8 %early_whitening.1 = (bf16[1152,512]{1,0:T(8,128)(2,1)S(1)}, bf16[4,256,512]{2,1,0:T(8,128)(2,1)S(1)}) custom-call(bf16[256,512]{1,0:T(8,128)(2,1)S(1)} %block.1.raw, bf16[256,512]{1,0:T(8,128)(2,1)S(1)} %get-tuple-element.25.first, bf16[256,512]{1,0:T(8,128)(2,1)S(1)} %collective-permute-done.7.second, bf16[4,256,384]{2,1,0:T(8,128)(2,1)S(1)} %band_matrix.1.band), custom_call_target="tpu_custom_call" | custom-call | tf_op jit(solution)/shard_map/early_whitening/pallas_call | solution.py:326
  28.4 4.7 %collective-permute-done.9.third = bf16[256,512]{1,0:T(8,128)(2,1)S(1)} collective-permute-done((bf16[256,512]{1,0:T(8,128)(2,1)S(1)}, bf16[256,512]{1,0:T(8,128)(2,1)S(1)}, u32[]{:S(2)}, u32[]{:S(2)}) %collective-permute-start.9) | collective-permute-done | bytes 262176 | tf_op jit(solution)/shard_map/ppermute | solution.py:310
  33.0 0.0 collective-permute-done.10.fourth
  33.1 0.0 copy-done
  33.1 2.8 %cross.1 = f32[4,2,256,256]{3,2,1,0:T(8,128)} custom-call(s32[1,4]{1,0:T(1,128)S(1)} %copy-done, bf16[1152,512]{1,0:T(8,128)(2,1)S(1)} %get-tuple-element.29.padded, bf16[4,256,512]{2,1,0:T(8,128)(2,1)S(1)} %get-tuple-element.30.early, bf16[256,512]{1,0:T(8,128)(2,1)S(1)} %collective-permute-done.9.third, ...), custom_call_target="tpu_custom_call" | custom-call | tf_op jit(solution)/shard_map/cross/pallas_call | solution.py:340
  (2 shorter events, 0.0 us)
Async XLA Ops:
  0.0 11.4 %collective-permute-start = (bf16[128,1024]{1,0:T(8,128)(2,1)}, bf16[128,1024]{1,0:T(8,128)(2,1)S(1)}, u32[]{:S(2)}, u32[]{:S(2)}) collective-permute-start(bf16[128,1024]{1,0:T(8,128)(2,1)} %param.5), channel_id=1, source_target_pairs={{0,2},{2,0},{1,3},{3,1},{4,6},{6,4},{5,7},{7,5},{8,10},{10,8},{9,1... | collective-permute-start | bytes 786440 | tf_op jit(solution)/shard_map/ppermute | solution.py:234
  2.9 7.7 %collective-permute-start.3 = (bf16[64,128]{1,0:T(8,128)(2,1)}, bf16[64,128]{1,0:T(8,128)(2,1)S(1)}, u32[]{:S(2)}, u32[]{:S(2)}) collective-permute-start(bf16[64,128]{1,0:T(8,128)(2,1)} %bitcast.13), channel_id=1, source_target_pairs={{0,12},{4,8},{8,4},{12,0},{1,13},{5,9},{9,5},{13,1},{2,14},{6,10},... | collective-permute-start | bytes 49160 | tf_op jit(solution)/shard_map/ppermute | solution.py:239
  6.5 4.8 %collective-permute-start.2 = (bf16[64,128]{1,0:T(8,128)(2,1)}, bf16[64,128]{1,0:T(8,128)(2,1)S(1)}, u32[]{:S(2)}, u32[]{:S(2)}) collective-permute-start(bf16[64,128]{1,0:T(8,128)(2,1)} %bitcast.14), channel_id=1, source_target_pairs={{0,8},{4,12},{8,0},{12,4},{1,9},{5,13},{9,1},{13,5},{2,10},{6,14},... | collective-permute-start | bytes 49160 | tf_op jit(solution)/shard_map/ppermute | solution.py:239
  6.5 4.8 %collective-permute-start.1 = (bf16[64,128]{1,0:T(8,128)(2,1)}, bf16[64,128]{1,0:T(8,128)(2,1)S(1)}, u32[]{:S(2)}, u32[]{:S(2)}) collective-permute-start(bf16[64,128]{1,0:T(8,128)(2,1)} %bitcast.15), channel_id=1, source_target_pairs={{0,4},{4,0},{8,12},{12,8},{1,5},{5,1},{9,13},{13,9},{2,6},{6,2},{1... | collective-permute-start | bytes 49160 | tf_op jit(solution)/shard_map/ppermute | solution.py:239
  10.6 12.2 %copy-start.1 = (bf16[128,64]{0,1:T(8,128)(2,1)S(1)}, bf16[128,64]{0,1:T(8,128)(2,1)}, u32[]{:S(2)}) copy-start(bf16[128,64]{0,1:T(8,128)(2,1)} %param.7) | copy-start | bytes 49156
  11.9 21.2 %copy-start = (s32[1,4]{1,0:T(1,128)S(1)}, s32[1,4]{1,0:T(1,128)}, u32[]{:S(2)}) copy-start(s32[1,4]{1,0:T(1,128)} %slots.1) | copy-start | bytes 52
  11.9 3.4 %collective-permute-start.4 = (bf16[128,512]{1,0:T(8,128)(2,1)S(1)}, bf16[128,512]{1,0:T(8,128)(2,1)S(1)}, u32[]{:S(2)}, u32[]{:S(2)}) collective-permute-start(bf16[128,512]{1,0:T(8,128)(2,1)S(1)} %get-tuple-element.24), channel_id=1, source_target_pairs={{0,1},{1,0},{2,3},{3,2},{4,5},{5,4},{6,7},{7,6},{8,9},{9,8},{10,11... | collective-permute-start | bytes 393224 | tf_op jit(solution)/shard_map/ppermute | solution.py:34
  12.0 6.3 %collective-permute-start.5 = (bf16[128,512]{1,0:T(8,128)(2,1)S(1)}, bf16[128,512]{1,0:T(8,128)(2,1)S(1)}, u32[]{:S(2)}, u32[]{:S(2)}) collective-permute-start(bf16[128,512]{1,0:T(8,128)(2,1)S(1)} %get-tuple-element.23.own), channel_id=1, source_target_pairs={{0,8},{8,12},{12,4},{4,0},{1,9},{9,13},{13,5},{5,1},{2,10},{10,14}... | collective-permute-start | bytes 393224 | tf_op jit(solution)/shard_map/ppermute | solution.py:298
  14.0 6.7 %collective-permute-start.6 = (bf16[128,512]{1,0:T(8,128)(2,1)S(1)}, bf16[128,512]{1,0:T(8,128)(2,1)S(1)}, u32[]{:S(2)}, u32[]{:S(2)}) collective-permute-start(bf16[128,512]{1,0:T(8,128)(2,1)S(1)} %get-tuple-element.24), channel_id=1, source_target_pairs={{0,9},{1,8},{8,13},{9,12},{12,5},{13,4},{4,1},{5,0},{2,11},{3,10},... | collective-permute-start | bytes 393224 | tf_op jit(solution)/shard_map/ppermute | solution.py:300
  15.3 12.3 %collective-permute-start.7 = (bf16[256,512]{1,0:T(8,128)(2,1)S(1)}, bf16[256,512]{1,0:T(8,128)(2,1)S(1)}, u32[]{:S(2)}, u32[]{:S(2)}) collective-permute-start(bf16[256,512]{1,0:T(8,128)(2,1)S(1)} %block.1.raw), channel_id=1, source_target_pairs={{4,12},{12,8},{8,0},{0,4},{5,13},{13,9},{9,1},{1,5},{6,14},{14,10}... | collective-permute-start | bytes 786440 | tf_op jit(solution)/shard_map/ppermute | solution.py:301
  20.8 12.3 %collective-permute-start.9 = (bf16[256,512]{1,0:T(8,128)(2,1)S(1)}, bf16[256,512]{1,0:T(8,128)(2,1)S(1)}, u32[]{:S(2)}, u32[]{:S(2)}) collective-permute-start(bf16[256,512]{1,0:T(8,128)(2,1)S(1)} %get-tuple-element.31), channel_id=1, source_target_pairs={{4,0},{8,4},{5,1},{9,5},{6,2},{10,6},{7,3},{11,7},{20,16},{24,20},... | collective-permute-start | bytes 786440 | tf_op jit(solution)/shard_map/ppermute | solution.py:310
  22.1 11.0 %collective-permute-start.10 = (bf16[256,512]{1,0:T(8,128)(2,1)S(1)}, bf16[256,512]{1,0:T(8,128)(2,1)S(1)}, u32[]{:S(2)}, u32[]{:S(2)}) collective-permute-start(bf16[256,512]{1,0:T(8,128)(2,1)S(1)} %get-tuple-element.32), channel_id=1, source_target_pairs={{8,12},{4,8},{9,13},{5,9},{10,14},{6,10},{11,15},{7,11},{24,28},{2... | collective-permute-start | bytes 786440 | tf_op jit(solution)/shard_map/ppermute | solution.py:311
  22.8 1.3 %collective-permute-start.8 = (bf16[4,64,128]{2,1,0:T(8,128)(2,1)S(1)}, bf16[4,64,128]{2,1,0:T(8,128)(2,1)S(1)}, u32[]{:S(2)}, u32[]{:S(2)}) collective-permute-start(bf16[4,64,128]{2,1,0:T(8,128)(2,1)S(1)} %pad_maximum_fusion.1.refs_0_), channel_id=1, source_target_pairs={{0,1},{1,0},{2,3},{3,2},{4,5},{5,4},{6,7},{7,6},{8,9},{9,8},{10,11... | collective-permute-start | bytes 196616 | tf_op jit(solution)/shard_map/ppermute | solution.py:34

commit v4 on v3

--- a/solution.py
+++ b/solution.py
@@ -48,17 +48,24 @@
     return jnp.where((half == 0) | (half == 1), product, 0.0)
 
 
-def begin_kernel(own, tables, total, table, sems):
+def begin_kernel(recording, trailing, tables, total, table, hop, following, sems):
     span = lax.axis_index("tm")
-    copy = pltpu.make_async_copy(tables.at[span], table, sems.at[0])
-    copy.start()
+    copies = [
+        pltpu.make_async_copy(source, target, sems.at[index])
+        for index, (source, target) in enumerate(
+            ((recording, hop), (trailing, following), (tables.at[span], table))
+        )
+    ]
+    for copy in copies:
+        copy.start()
+    for copy in copies:
+        copy.wait()
     width = table.shape[1]
     segments = total.shape[1] // width
-    copy.wait()
     for segment in range(segments):
-        value = hop_part(span, segment, own[0], table)
+        value = hop_part(span, segment, hop[...], table)
         if segment == segments - 1:
-            value += hop_part(segments, segment, own[1], table)
+            value += hop_part(segments, segment, following[...], table)
         total[:, segment * width : (segment + 1) * width] = value
 
 
@@ -105,9 +112,8 @@
     return (raw.astype(jnp.float32) - predicted).astype(jnp.bfloat16)
 
 
-def pair_products(slots, spectra, mine, base, segments, scaling, out, left, result, sems):
-    count, rows, columns = spectra.shape
-    own = spectra[mine]
+def pair_products(slots, own, spectra_of, segments, scaling, out, left, result, sems):
+    rows, columns = own.shape
     left[:rows, :] = own
     half = columns // (2 * segments)
     turned = []
@@ -119,7 +125,7 @@
     contract = (((1,), (1,)), ((), ()))
     for slot in range(SLOTS):
         partner = slots[0, slot]
-        theirs = spectra[jnp.clip(partner - base, 0, count - 1)]
+        theirs = spectra_of(jnp.maximum(partner, 0))
         both = lax.dot_general(left[...], theirs, contract, preferred_element_type=jnp.float32)
         both = jnp.where(partner >= 0, both * scaling, 0.0)
         result[slot, 0] = both[:rows]
@@ -146,7 +152,8 @@
         window = padded[start : start + band.shape[2], :]
         spectra[block] = whitened(band[block], window, padded[start + rim : start + rim + rows, :])
     base = lax.axis_index("chan") - REACH
-    pair_products(slots, spectra, REACH, base, segments, scaling, out, left, result, sems)
+    spectra_of = lambda block: spectra[jnp.clip(block - base, 0, count - 1)]
+    pair_products(slots, spectra[REACH], spectra_of, segments, scaling, out, left, result, sems)
 
 
 def chosen(a, b, c, d):
@@ -182,39 +189,40 @@
         spectra[block] = whitened(band[block], window, padded[start + rim : start + rim + rows, :])
 
 
-def late_kernel(segments, scaling, slots, padded, early, third, fourth, band, out, spectra, left, result, sems):
-    count, rows, columns = spectra.shape
+def late_kernel(segments, scaling, slots, padded, early, third, fourth, band, out, left, result, sems):
+    count, rows, columns = early.shape
     width = band.shape[2]
     rim = (padded.shape[0] - count * rows) // 4
     here = lax.axis_index("chan")
     last = chosen(3, 2, 1, 0)
     value = jnp.where(here <= 1, third[...], fourth[...])
-    spectra[...] = early[...]
 
     start = pl.multiple_of(last * rows, rows)
     above = padded[pl.ds(start, rim), :]
     below = padded[pl.ds(start + rim + rows, width - rim - rows), :]
     window = jnp.concatenate([above, value, below], axis=0)
-    spectra[last] = whitened(band[last], window, value)
-
-    @pl.when(last > 0)
-    def _():
-        block = last - 1
-        half = rows // 2
-        upper = padded[pl.ds(pl.multiple_of(start - half, half), half + rim), :]
-        window = jnp.concatenate([upper, value[: width - rows - rim]], axis=0)
-        strip = whitened(band[block, rows - rim :, half:], window, above)
-        spectra[block, rows - rim :, :] = strip
-
-    @pl.when(last < count - 1)
-    def _():
-        block = last + 1
-        lower = padded[pl.ds(start + rows + rim, LANES - rim), :]
-        window = jnp.concatenate([value[rows - rim :], lower], axis=0)
-        strip = whitened(band[block, :rim, :LANES], window, lower[:rim])
-        spectra[block, :rim, :] = strip
-
-    pair_products(slots, spectra, here, 0, segments, scaling, out, left, result, sems)
+    arrived = whitened(band[last], window, value)
+
+    half = rows // 2
+    upper = padded[pl.ds(pl.multiple_of(jnp.maximum(start - half, 0), half), half + rim), :]
+    window = jnp.concatenate([upper, value[: width - rows - rim]], axis=0)
+    bottom = whitened(band[jnp.maximum(last - 1, 0), rows - rim :, half:], window, above)
+    lower = below[: LANES - rim]
+    window = jnp.concatenate([value[rows - rim :], lower], axis=0)
+    top = whitened(band[jnp.minimum(last + 1, count - 1), :rim, :LANES], window, lower[:rim])
+
+    def spectra_of(block):
+        known = jnp.where(block == last, arrived, early[block])
+        return jnp.concatenate(
+            [
+                jnp.where(block == last + 1, top, known[:rim]),
+                known[rim : rows - rim],
+                jnp.where(block == last - 1, bottom, known[rows - rim :]),
+            ],
+            axis=0,
+        )
+
+    pair_products(slots, spectra_of(here), spectra_of, segments, scaling, out, left, result, sems)
 
 
 def local(tables, recording, trailing, whiten_filter, pair_list):
@@ -241,7 +249,6 @@
         ]
     else:
         filters = [lax.all_gather(whiten_filter, ("chan", "freq"), axis=0, tiled=True)]
-    own = jnp.stack([recording, trailing])
     total = (block_rows, spans * bins2)
     in_hbm = pl.BlockSpec(memory_space=pltpu.HBM)
     begun, table = pl.pallas_call(
@@ -250,12 +257,21 @@
             jax.ShapeDtypeStruct((rows, halves * total[1]), jnp.float32),
             jax.ShapeDtypeStruct(tables.shape[1:], jnp.bfloat16),
         ],
-        in_specs=[in_vmem, in_hbm],
-        out_specs=[in_vmem, in_vmem],
-        scratch_shapes=[pltpu.SemaphoreType.DMA((1,))],
-        compiler_params=pltpu.CompilerParams(vmem_limit_bytes=48 * 2**20),
+        in_specs=[in_hbm] * 3,
+        out_specs=[in_vmem] * 2,
+        scratch_shapes=[
+            pltpu.VMEM(recording.shape, jnp.bfloat16),
+            pltpu.VMEM(trailing.shape, jnp.bfloat16),
+            pltpu.SemaphoreType.DMA((3,)),
+        ],
+        compiler_params=small,
         name="begin_transform",
-    )(own, jnp.asarray(tables))
+    )(
+        *(
+            pltpu.with_memory_space_constraint(value, pltpu.HBM)
+            for value in (recording, trailing, jnp.asarray(tables))
+        )
+    )
     received, filters, begun = lax.optimization_barrier((received, filters, begun))
     half_rows = (rows, total[1])
     mine, theirs = pl.pallas_call(
@@ -335,7 +351,7 @@
         kernel, scratch = late_kernel, []
     else:
         operands = (*blocks, band)
-        kernel, scratch = cross_kernel, [pltpu.VMEM(padded, jnp.bfloat16)]
+        kernel, scratch = cross_kernel, [pltpu.VMEM(shape, jnp.bfloat16) for shape in (padded, spectra)]
     out_shape = (SLOTS, 2, block_rows, block_rows)
     result = pl.pallas_call(
         functools.partial(kernel, spans, 1.0 / math.sqrt(spans * bins2 // 2)),
@@ -344,7 +360,6 @@
         out_specs=in_hbm,
         scratch_shapes=[
             *scratch,
-            pltpu.VMEM(spectra, jnp.bfloat16),
             pltpu.VMEM((2 * block_rows, total[1]), jnp.bfloat16),
             pltpu.VMEM(out_shape, jnp.float32),
             pltpu.SemaphoreType.DMA((SLOTS,)),

time: 36.1 us -> 35 us (0.970)
  other arithmetic: 1.09 us -> 0.01 us
    another operation x1 -> x0, other arithmetic: 1.08 us -> none  [local(): own = jnp.stack([recording, trailing])]
    ppermute x1, waiting for transfers between devices: 3.12 us -> 2.21 us  [local(): second = lax.ppermute(raw, 'chan', [(1, 3), (3, 2), (2, 0), (0, 1)])]
    ppermute x1, starting transfers between devices: 0.64 us -> 1.54 us  [local(): second = lax.ppermute(raw, 'chan', [(1, 3), (3, 2), (2, 0), (0, 1)])]
    ppermute x1, starting transfers between devices: 1.21 us -> 0.31 us  [local(): first_other = lax.ppermute(theirs, ('chan', 'freq'), across)]
    ppermute x3, waiting for transfers between devices: 0.75 us -> 1.65 us  [local(): lax.ppermute(whiten_filter.T, 'chan', [(i, i ^ step) for i in range(chain)])]
  transfers between devices with their start and end apart: 11 -> 11, of which waited for: 6 -> 6; matrix products, arithmetic and copies ran while one was open for 3% -> 0% of each run, Pallas kernels for 10% -> 10%
where the time goes in v4:
time: 35 us; the launch traced here: 34.9 us
  waiting for transfers between devices  14.3 us (41%)
  starting transfers between devices  13.6 us (39%)
  Pallas kernels  6.79 us (19%)
    ppermute x1, waiting for transfers between devices, local(): third = lax.ppermute(down, 'chan', [(1, 0), (2, 1)])  4.69 us
    ppermute x3, starting transfers between devices, local(): lax.ppermute(whiten_filter.T, 'chan', [(i, i ^ step) for i in range(chain)])  4.39 us
    ppermute x1, starting transfers between devices, local(): lax.ppermute(recording, 'tm', [(i, (i + step) % spans) for i in range(spa...  2.94 us
    pallas_call x1, Pallas kernels, local(): pl.pallas_call(functools.partial(kernel, spans, 1.0 / math.sqrt(spans * b...  2.72 us
    ppermute x1, waiting for transfers between devices, local(): first = lax.ppermute(mine, 'chan', route)  2.4 us
    ppermute x1, waiting for transfers between devices, local(): first_other = lax.ppermute(theirs, ('chan', 'freq'), across)  2.38 us
    pallas_call x1, Pallas kernels, local(): pl.pallas_call(begin_kernel, out_shape=[jax.ShapeDtypeStruct((rows, halve...  2.38 us
    ppermute x1, waiting for transfers between devices, local(): second = lax.ppermute(raw, 'chan', [(1, 3), (3, 2), (2, 0), (0, 1)])  2.21 us
  transfers between devices with their start and end apart: 11, of which 6 were waited for; matrix products, arithmetic and copies ran while one was open for 0% of the time, Pallas kernels for 10%

profile of v4, /device:TPU:0, one launch (start us, length us, event | category | flops | bytes accessed | tf_op | source)
XLA Modules:
  0.0 34.9 jit_solution(13969663785733683258)
XLA Ops:
  0.0 2.9 %collective-permute-start = (bf16[128,1024]{1,0:T(8,128)(2,1)}, bf16[128,1024]{1,0:T(8,128)(2,1)S(1)}, u32[]{:S(2)}, u32[]{:S(2)}) collective-permute-start(bf16[128,1024]{1,0:T(8,128)(2,1)} %recording.1), channel_id=1, source_target_pairs={{0,2},{2,0},{1,3},{3,1},{4,6},{6,4},{5,7},{7,5},{8,10},{10,8},{9,1... | collective-permute-start | bytes 786440 | tf_op jit(solution)/shard_map/ppermute | solution.py:242
  2.9 3.6 %collective-permute-start.3 = (bf16[64,128]{1,0:T(8,128)(2,1)}, bf16[64,128]{1,0:T(8,128)(2,1)S(1)}, u32[]{:S(2)}, u32[]{:S(2)}) collective-permute-start(bf16[64,128]{1,0:T(8,128)(2,1)} %bitcast.9), channel_id=1, source_target_pairs={{0,12},{4,8},{8,4},{12,0},{1,13},{5,9},{9,5},{13,1},{2,14},{6,10},... | collective-permute-start | bytes 49160 | tf_op jit(solution)/shard_map/ppermute | solution.py:247
  6.5 0.0 collective-permute-start.2
  6.5 0.8 %collective-permute-start.1 = (bf16[64,128]{1,0:T(8,128)(2,1)}, bf16[64,128]{1,0:T(8,128)(2,1)S(1)}, u32[]{:S(2)}, u32[]{:S(2)}) collective-permute-start(bf16[64,128]{1,0:T(8,128)(2,1)} %bitcast.11), channel_id=1, source_target_pairs={{0,4},{4,0},{8,12},{12,8},{1,5},{5,1},{9,13},{13,9},{2,6},{6,2},{1... | collective-permute-start | bytes 49160 | tf_op jit(solution)/shard_map/ppermute | solution.py:247
  7.3 2.4 %begin_transform.1 = (f32[128,1024]{1,0:T(8,128)S(1)}, bf16[2048,512]{1,0:T(8,128)(2,1)S(1)}) custom-call(bf16[128,1024]{1,0:T(8,128)(2,1)} %recording.1, bf16[128,1024]{1,0:T(8,128)(2,1)} %trailing.1, bf16[2,2048,512]{2,1,0:T(8,128)(2,1)} %constant.2.clone.tables), custom_call_target="tpu_custom_call" | custom-call | tf_op jit(solution)/shard_map/begin_transform/pallas_call | solution.py:254
  9.7 0.0 copy-start.1
  9.7 0.0 collective-permute-done.3
  9.7 1.6 %collective-permute-done.2 = bf16[64,128]{1,0:T(8,128)(2,1)S(1)} collective-permute-done((bf16[64,128]{1,0:T(8,128)(2,1)}, bf16[64,128]{1,0:T(8,128)(2,1)S(1)}, u32[]{:S(2)}, u32[]{:S(2)}) %collective-permute-start.2) | collective-permute-done | bytes 16416 | tf_op jit(solution)/shard_map/ppermute | solution.py:247
  11.4 0.0 collective-permute-done.1
  11.4 0.0 collective-permute-done.refs_0_
  11.4 0.5 %finish_transform.1 = (bf16[128,512]{1,0:T(8,128)(2,1)S(1)}, bf16[128,512]{1,0:T(8,128)(2,1)S(1)}) custom-call(bf16[128,1024]{1,0:T(8,128)(2,1)S(1)} %collective-permute-done.refs_0_, bf16[2048,512]{1,0:T(8,128)(2,1)S(1)} %get-tuple-element.21.refs_1_, f32[128,1024]{1,0:T(8,128)S(1)} %get-tuple-element.22.refs_2_), custom_call_target="tpu_custom_call" | custom-call | tf_op jit(solution)/shard_map/finish_transform/pallas_call | solution.py:277
  11.9 0.0 copy-start
  11.9 0.1 collective-permute-start.4
  12.0 2.1 %collective-permute-start.5 = (bf16[128,512]{1,0:T(8,128)(2,1)S(1)}, bf16[128,512]{1,0:T(8,128)(2,1)S(1)}, u32[]{:S(2)}, u32[]{:S(2)}) collective-permute-start(bf16[128,512]{1,0:T(8,128)(2,1)S(1)} %get-tuple-element.23.own), channel_id=1, source_target_pairs={{0,8},{8,12},{12,4},{4,0},{1,9},{9,13},{13,5},{5,1},{2,10},{10,14}... | collective-permute-start | bytes 393224 | tf_op jit(solution)/shard_map/ppermute | solution.py:314
  14.0 0.3 collective-permute-start.6
  14.3 0.0 collective-permute-done.4.other
  14.4 1.5 %collective-permute-start.7 = (bf16[256,512]{1,0:T(8,128)(2,1)S(1)}, bf16[256,512]{1,0:T(8,128)(2,1)S(1)}, u32[]{:S(2)}, u32[]{:S(2)}) collective-permute-start(bf16[256,512]{1,0:T(8,128)(2,1)S(1)} %block.1.raw), channel_id=1, source_target_pairs={{4,12},{12,8},{8,0},{0,4},{5,13},{13,9},{9,1},{1,5},{6,14},{14,10}... | collective-permute-start | bytes 786440 | tf_op jit(solution)/shard_map/ppermute | solution.py:317
  15.9 2.4 %collective-permute-done.5.first = bf16[128,512]{1,0:T(8,128)(2,1)S(1)} collective-permute-done((bf16[128,512]{1,0:T(8,128)(2,1)S(1)}, bf16[128,512]{1,0:T(8,128)(2,1)S(1)}, u32[]{:S(2)}, u32[]{:S(2)}) %collective-permute-start.5) | collective-permute-done | bytes 131104 | tf_op jit(solution)/shard_map/ppermute | solution.py:314
  18.3 2.4 %collective-permute-done.6.first_other = bf16[128,512]{1,0:T(8,128)(2,1)S(1)} collective-permute-done((bf16[128,512]{1,0:T(8,128)(2,1)S(1)}, bf16[128,512]{1,0:T(8,128)(2,1)S(1)}, u32[]{:S(2)}, u32[]{:S(2)}) %collective-permute-start.6) | collective-permute-done | bytes 131104 | tf_op jit(solution)/shard_map/ppermute | solution.py:316
  20.7 0.1 relay.1
  20.8 1.3 %collective-permute-start.9 = (bf16[256,512]{1,0:T(8,128)(2,1)S(1)}, bf16[256,512]{1,0:T(8,128)(2,1)S(1)}, u32[]{:S(2)}, u32[]{:S(2)}) collective-permute-start(bf16[256,512]{1,0:T(8,128)(2,1)S(1)} %get-tuple-element.31), channel_id=1, source_target_pairs={{4,0},{8,4},{5,1},{9,5},{6,2},{10,6},{7,3},{11,7},{20,16},{24,20},... | collective-permute-start | bytes 786440 | tf_op jit(solution)/shard_map/ppermute | solution.py:326
  22.1 0.7 %collective-permute-start.10 = (bf16[256,512]{1,0:T(8,128)(2,1)S(1)}, bf16[256,512]{1,0:T(8,128)(2,1)S(1)}, u32[]{:S(2)}, u32[]{:S(2)}) collective-permute-start(bf16[256,512]{1,0:T(8,128)(2,1)S(1)} %get-tuple-element.32), channel_id=1, source_target_pairs={{8,12},{4,8},{9,13},{5,9},{10,14},{6,10},{11,15},{7,11},{24,28},{2... | collective-permute-start | bytes 786440 | tf_op jit(solution)/shard_map/ppermute | solution.py:327
  22.8 0.0 copy-done.1
  22.8 0.4 %collective-permute-start.8 = (bf16[4,64,128]{2,1,0:T(8,128)(2,1)S(1)}, bf16[4,64,128]{2,1,0:T(8,128)(2,1)S(1)}, u32[]{:S(2)}, u32[]{:S(2)}) collective-permute-start(bf16[4,64,128]{2,1,0:T(8,128)(2,1)S(1)} %pad_maximum_fusion.refs_0_), channel_id=1, source_target_pairs={{0,1},{1,0},{2,3},{3,2},{4,5},{5,4},{6,7},{7,6},{8,9},{9,8},{10,11... | collective-permute-start | bytes 196616 | tf_op jit(solution)/shard_map/ppermute | solution.py:34
  23.2 0.9 %collective-permute-done.8.refs_1_ = bf16[4,64,128]{2,1,0:T(8,128)(2,1)S(1)} collective-permute-done((bf16[4,64,128]{2,1,0:T(8,128)(2,1)S(1)}, bf16[4,64,128]{2,1,0:T(8,128)(2,1)S(1)}, u32[]{:S(2)}, u32[]{:S(2)}) %collective-permute-start.8) | collective-permute-done | bytes 65568 | tf_op jit(solution)/shard_map/ppermute | solution.py:34
  24.1 0.3 band_matrix.1.band
  24.4 2.2 %collective-permute-done.7.second = bf16[256,512]{1,0:T(8,128)(2,1)S(1)} collective-permute-done((bf16[256,512]{1,0:T(8,128)(2,1)S(1)}, bf16[256,512]{1,0:T(8,128)(2,1)S(1)}, u32[]{:S(2)}, u32[]{:S(2)}) %collective-permute-start.7) | collective-permute-done | bytes 262176 | tf_op jit(solution)/shard_map/ppermute | solution.py:317
  26.6 0.8 %early_whitening.1 = (bf16[1152,512]{1,0:T(8,128)(2,1)S(1)}, bf16[4,256,512]{2,1,0:T(8,128)(2,1)S(1)}) custom-call(bf16[256,512]{1,0:T(8,128)(2,1)S(1)} %block.1.raw, bf16[256,512]{1,0:T(8,128)(2,1)S(1)} %get-tuple-element.25.first, bf16[256,512]{1,0:T(8,128)(2,1)S(1)} %collective-permute-done.7.second, bf16[4,256,384]{2,1,0:T(8,128)(2,1)S(1)} %band_matrix.1.band), custom_call_target="tpu_custom_call" | custom-call | tf_op jit(solution)/shard_map/early_whitening/pallas_call | solution.py:342
  27.5 4.7 %collective-permute-done.9.third = bf16[256,512]{1,0:T(8,128)(2,1)S(1)} collective-permute-done((bf16[256,512]{1,0:T(8,128)(2,1)S(1)}, bf16[256,512]{1,0:T(8,128)(2,1)S(1)}, u32[]{:S(2)}, u32[]{:S(2)}) %collective-permute-start.9) | collective-permute-done | bytes 262176 | tf_op jit(solution)/shard_map/ppermute | solution.py:326
  32.1 0.0 collective-permute-done.10.fourth
  32.2 0.0 copy-done
  32.2 2.7 %cross.1 = f32[4,2,256,256]{3,2,1,0:T(8,128)} custom-call(s32[1,4]{1,0:T(1,128)S(1)} %copy-done, bf16[1152,512]{1,0:T(8,128)(2,1)S(1)} %get-tuple-element.29.padded, bf16[4,256,512]{2,1,0:T(8,128)(2,1)S(1)} %get-tuple-element.30.early, bf16[256,512]{1,0:T(8,128)(2,1)S(1)} %collective-permute-done.9.third, ...), custom_call_target="tpu_custom_call" | custom-call | tf_op jit(solution)/shard_map/cross/pallas_call | solution.py:356
  (2 shorter events, 0.0 us)
Async XLA Ops:
  0.0 11.4 %collective-permute-start = (bf16[128,1024]{1,0:T(8,128)(2,1)}, bf16[128,1024]{1,0:T(8,128)(2,1)S(1)}, u32[]{:S(2)}, u32[]{:S(2)}) collective-permute-start(bf16[128,1024]{1,0:T(8,128)(2,1)} %recording.1), channel_id=1, source_target_pairs={{0,2},{2,0},{1,3},{3,1},{4,6},{6,4},{5,7},{7,5},{8,10},{10,8},{9,1... | collective-permute-start | bytes 786440 | tf_op jit(solution)/shard_map/ppermute | solution.py:242
  2.9 6.8 %collective-permute-start.3 = (bf16[64,128]{1,0:T(8,128)(2,1)}, bf16[64,128]{1,0:T(8,128)(2,1)S(1)}, u32[]{:S(2)}, u32[]{:S(2)}) collective-permute-start(bf16[64,128]{1,0:T(8,128)(2,1)} %bitcast.9), channel_id=1, source_target_pairs={{0,12},{4,8},{8,4},{12,0},{1,13},{5,9},{9,5},{13,1},{2,14},{6,10},... | collective-permute-start | bytes 49160 | tf_op jit(solution)/shard_map/ppermute | solution.py:247
  6.5 4.8 %collective-permute-start.2 = (bf16[64,128]{1,0:T(8,128)(2,1)}, bf16[64,128]{1,0:T(8,128)(2,1)S(1)}, u32[]{:S(2)}, u32[]{:S(2)}) collective-permute-start(bf16[64,128]{1,0:T(8,128)(2,1)} %bitcast.10), channel_id=1, source_target_pairs={{0,8},{4,12},{8,0},{12,4},{1,9},{5,13},{9,1},{13,5},{2,10},{6,14},... | collective-permute-start | bytes 49160 | tf_op jit(solution)/shard_map/ppermute | solution.py:247
  6.5 4.8 %collective-permute-start.1 = (bf16[64,128]{1,0:T(8,128)(2,1)}, bf16[64,128]{1,0:T(8,128)(2,1)S(1)}, u32[]{:S(2)}, u32[]{:S(2)}) collective-permute-start(bf16[64,128]{1,0:T(8,128)(2,1)} %bitcast.11), channel_id=1, source_target_pairs={{0,4},{4,0},{8,12},{12,8},{1,5},{5,1},{9,13},{13,9},{2,6},{6,2},{1... | collective-permute-start | bytes 49160 | tf_op jit(solution)/shard_map/ppermute | solution.py:247
  9.7 13.1 %copy-start.1 = (bf16[128,64]{0,1:T(8,128)(2,1)S(1)}, bf16[128,64]{0,1:T(8,128)(2,1)}, u32[]{:S(2)}) copy-start(bf16[128,64]{0,1:T(8,128)(2,1)} %param.7) | copy-start | bytes 49156
  11.9 20.3 %copy-start = (s32[1,4]{1,0:T(1,128)S(1)}, s32[1,4]{1,0:T(1,128)}, u32[]{:S(2)}) copy-start(s32[1,4]{1,0:T(1,128)} %slots.1) | copy-start | bytes 52
  11.9 2.5 %collective-permute-start.4 = (bf16[128,512]{1,0:T(8,128)(2,1)S(1)}, bf16[128,512]{1,0:T(8,128)(2,1)S(1)}, u32[]{:S(2)}, u32[]{:S(2)}) collective-permute-start(bf16[128,512]{1,0:T(8,128)(2,1)S(1)} %get-tuple-element.24), channel_id=1, source_target_pairs={{0,1},{1,0},{2,3},{3,2},{4,5},{5,4},{6,7},{7,6},{8,9},{9,8},{10,11... | collective-permute-start | bytes 393224 | tf_op jit(solution)/shard_map/ppermute | solution.py:34
  12.0 6.3 %collective-permute-start.5 = (bf16[128,512]{1,0:T(8,128)(2,1)S(1)}, bf16[128,512]{1,0:T(8,128)(2,1)S(1)}, u32[]{:S(2)}, u32[]{:S(2)}) collective-permute-start(bf16[128,512]{1,0:T(8,128)(2,1)S(1)} %get-tuple-element.23.own), channel_id=1, source_target_pairs={{0,8},{8,12},{12,4},{4,0},{1,9},{9,13},{13,5},{5,1},{2,10},{10,14}... | collective-permute-start | bytes 393224 | tf_op jit(solution)/shard_map/ppermute | solution.py:314
  14.0 6.7 %collective-permute-start.6 = (bf16[128,512]{1,0:T(8,128)(2,1)S(1)}, bf16[128,512]{1,0:T(8,128)(2,1)S(1)}, u32[]{:S(2)}, u32[]{:S(2)}) collective-permute-start(bf16[128,512]{1,0:T(8,128)(2,1)S(1)} %get-tuple-element.24), channel_id=1, source_target_pairs={{0,9},{1,8},{8,13},{9,12},{12,5},{13,4},{4,1},{5,0},{2,11},{3,10},... | collective-permute-start | bytes 393224 | tf_op jit(solution)/shard_map/ppermute | solution.py:316
  14.4 12.3 %collective-permute-start.7 = (bf16[256,512]{1,0:T(8,128)(2,1)S(1)}, bf16[256,512]{1,0:T(8,128)(2,1)S(1)}, u32[]{:S(2)}, u32[]{:S(2)}) collective-permute-start(bf16[256,512]{1,0:T(8,128)(2,1)S(1)} %block.1.raw), channel_id=1, source_target_pairs={{4,12},{12,8},{8,0},{0,4},{5,13},{13,9},{9,1},{1,5},{6,14},{14,10}... | collective-permute-start | bytes 786440 | tf_op jit(solution)/shard_map/ppermute | solution.py:317
  20.8 11.4 %collective-permute-start.9 = (bf16[256,512]{1,0:T(8,128)(2,1)S(1)}, bf16[256,512]{1,0:T(8,128)(2,1)S(1)}, u32[]{:S(2)}, u32[]{:S(2)}) collective-permute-start(bf16[256,512]{1,0:T(8,128)(2,1)S(1)} %get-tuple-element.31), channel_id=1, source_target_pairs={{4,0},{8,4},{5,1},{9,5},{6,2},{10,6},{7,3},{11,7},{20,16},{24,20},... | collective-permute-start | bytes 786440 | tf_op jit(solution)/shard_map/ppermute | solution.py:326
  22.1 10.1 %collective-permute-start.10 = (bf16[256,512]{1,0:T(8,128)(2,1)S(1)}, bf16[256,512]{1,0:T(8,128)(2,1)S(1)}, u32[]{:S(2)}, u32[]{:S(2)}) collective-permute-start(bf16[256,512]{1,0:T(8,128)(2,1)S(1)} %get-tuple-element.32), channel_id=1, source_target_pairs={{8,12},{4,8},{9,13},{5,9},{10,14},{6,10},{11,15},{7,11},{24,28},{2... | collective-permute-start | bytes 786440 | tf_op jit(solution)/shard_map/ppermute | solution.py:327
  22.8 1.3 %collective-permute-start.8 = (bf16[4,64,128]{2,1,0:T(8,128)(2,1)S(1)}, bf16[4,64,128]{2,1,0:T(8,128)(2,1)S(1)}, u32[]{:S(2)}, u32[]{:S(2)}) collective-permute-start(bf16[4,64,128]{2,1,0:T(8,128)(2,1)S(1)} %pad_maximum_fusion.refs_0_), channel_id=1, source_target_pairs={{0,1},{1,0},{2,3},{3,2},{4,5},{5,4},{6,7},{7,6},{8,9},{9,8},{10,11... | collective-permute-start | bytes 196616 | tf_op jit(solution)/shard_map/ppermute | solution.py:34

commit v5 on v4

--- a/solution.py
+++ b/solution.py
@@ -40,32 +40,40 @@
     return jnp.concatenate([jnp.where(low, a, b), jnp.where(low, b, a)], axis=0)
 
 
-def hop_part(place, segment, value, table):
+def hop_parts(place, value, table, segments):
     hop = value.shape[1]
-    half = place - segment
-    start = pl.multiple_of(jnp.clip(half, 0, 1) * hop, hop)
-    product = jnp.dot(value, table[pl.ds(start, hop), :], preferred_element_type=jnp.float32)
-    return jnp.where((half == 0) | (half == 1), product, 0.0)
+    first = jnp.dot(value, table[:hop, :], preferred_element_type=jnp.float32)
+    second = jnp.dot(value, table[hop:, :], preferred_element_type=jnp.float32)
+    for segment in range(segments):
+        yield jnp.where(place == segment, first, jnp.where(place == segment + 1, second, 0.0))
 
 
 def begin_kernel(recording, trailing, tables, total, table, hop, following, sems):
     span = lax.axis_index("tm")
+    width = table.shape[1]
+    segments = total.shape[1] // width
+    size = hop.shape[1]
     copies = [
         pltpu.make_async_copy(source, target, sems.at[index])
         for index, (source, target) in enumerate(
-            ((recording, hop), (trailing, following), (tables.at[span], table))
+            (
+                (trailing, following),
+                (tables.at[span, pl.ds(size, size)], table.at[pl.ds(size, size)]),
+                (recording, hop),
+                (tables.at[span, pl.ds(0, size)], table.at[pl.ds(0, size)]),
+            )
         )
     ]
     for copy in copies:
         copy.start()
-    for copy in copies:
+    for copy in copies[:2]:
         copy.wait()
-    width = table.shape[1]
-    segments = total.shape[1] // width
-    for segment in range(segments):
-        value = hop_part(span, segment, hop[...], table)
+    last = jnp.dot(following[...], table[size:, :], preferred_element_type=jnp.float32)
+    for copy in copies[2:]:
+        copy.wait()
+    for segment, value in enumerate(hop_parts(span, hop[...], table, segments)):
         if segment == segments - 1:
-            value += hop_part(segments, segment, following[...], table)
+            value += last
         total[:, segment * width : (segment + 1) * width] = value
 
 
@@ -74,11 +82,14 @@
     width = table.shape[1]
     part = width // 2
     low = lax.axis_index("freq") == 0
-    for segment in range(spans):
+    parts = [
+        hop_parts(lax.rem(lax.axis_index("tm") - step + spans, spans), hop[...], table, spans)
+        for step, hop in enumerate(hops, 1)
+    ]
+    for segment, added in enumerate(zip(*parts)):
         value = begun[:, segment * width : (segment + 1) * width]
-        for step in range(1, spans):
-            place = lax.rem(lax.axis_index("tm") - step + spans, spans)
-            value += hop_part(place, segment, hops[step - 1][...], table)
+        for more in added:
+            value += more
         first, second = value[:, :part].astype(jnp.bfloat16), value[:, part:].astype(jnp.bfloat16)
         columns = slice(segment * part, (segment + 1) * part)
         mine[:, columns] = jnp.where(low, first, second)
@@ -97,7 +108,7 @@
     for block in range(blocks):
         if chain == 4:
             own, other = (ref[block].astype(jnp.float32) for ref in weights)
-            place = jnp.bitwise_xor(here, block)
+            place = jnp.bitwise_xor(here, (0, 1, 3, 2)[block])
             tile = jnp.concatenate([jnp.where(low, own, other), jnp.where(low, other, own)], axis=1).T
         else:
             place = block
@@ -126,13 +137,13 @@
     for slot in range(SLOTS):
         partner = slots[0, slot]
         theirs = spectra_of(jnp.maximum(partner, 0))
-        both = lax.dot_general(left[...], theirs, contract, preferred_element_type=jnp.float32)
-        both = jnp.where(partner >= 0, both * scaling, 0.0)
-        result[slot, 0] = both[:rows]
-        result[slot, 1] = both[rows:]
-        pltpu.make_async_copy(result.at[slot], out.at[slot], sems.at[slot]).start()
+        for part, lhs in enumerate((left[:rows, :], left[rows:, :])):
+            value = lax.dot_general(lhs, theirs, contract, preferred_element_type=jnp.float32)
+            result[slot, part] = jnp.where(partner >= 0, value * scaling, 0.0)
+            pltpu.make_async_copy(result.at[slot, part], out.at[slot, part], sems.at[slot, part]).start()
     for slot in range(SLOTS):
-        pltpu.make_async_copy(result.at[slot], out.at[slot], sems.at[slot]).wait()
+        for part in range(2):
+            pltpu.make_async_copy(result.at[slot, part], out.at[slot, part], sems.at[slot, part]).wait()
 
 
 def cross_kernel(segments, scaling, slots, *refs):
@@ -161,15 +172,7 @@
     return jnp.where(here == 0, a, jnp.where(here == 1, b, jnp.where(here == 2, c, d)))
 
 
-def relay_kernel(raw, first, first_other, arrived, down, up):
-    here = lax.axis_index("chan")
-    value = block_of(first, first_other)
-    arrived[...] = value
-    down[...] = jnp.where(here == 1, value, raw[...])
-    up[...] = jnp.where(here == 2, value, raw[...])
-
-
-def early_kernel(raw, first, second, band, padded, spectra):
+def early_kernel(raw, first, first_other, second, band, padded, spectra):
     count, rows, columns = spectra.shape
     rim = (padded.shape[0] - count * rows) // 4
     edge = count * rows + rim
@@ -179,7 +182,7 @@
     padded[pl.ds(pl.multiple_of(last * rows + rim, rim), rows), :] = jnp.zeros((rows, columns), jnp.bfloat16)
     for place, value in (
         (lax.axis_index("chan"), raw),
-        (chosen(1, 3, 0, 2), first),
+        (chosen(1, 3, 0, 2), block_of(first, first_other)),
         (chosen(2, 0, 3, 1), second),
     ):
         padded[pl.ds(pl.multiple_of(place * rows + rim, rim), rows), :] = value[...]
@@ -189,13 +192,14 @@
         spectra[block] = whitened(band[block], window, padded[start + rim : start + rim + rows, :])
 
 
-def late_kernel(segments, scaling, slots, padded, early, third, fourth, band, out, left, result, sems):
+def late_kernel(segments, scaling, slots, padded, early, third, fourth, fourth_other, band, out, left, result, sems):
     count, rows, columns = early.shape
     width = band.shape[2]
     rim = (padded.shape[0] - count * rows) // 4
     here = lax.axis_index("chan")
     last = chosen(3, 2, 1, 0)
-    value = jnp.where(here <= 1, third[...], fourth[...])
+    inner = (here == 1) | (here == 2)
+    value = jnp.where(inner, third[...], block_of(fourth, fourth_other))
 
     start = pl.multiple_of(last * rows, rows)
     above = padded[pl.ds(start, rim), :]
@@ -211,8 +215,7 @@
     window = jnp.concatenate([value[rows - rim :], lower], axis=0)
     top = whitened(band[jnp.minimum(last + 1, count - 1), :rim, :LANES], window, lower[:rim])
 
-    def spectra_of(block):
-        known = jnp.where(block == last, arrived, early[block])
+    def mended(block, known):
         return jnp.concatenate(
             [
                 jnp.where(block == last + 1, top, known[:rim]),
@@ -222,7 +225,8 @@
             axis=0,
         )
 
-    pair_products(slots, spectra_of(here), spectra_of, segments, scaling, out, left, result, sems)
+    spectra_of = lambda block: mended(block, jnp.where(block == last, arrived, early[block]))
+    pair_products(slots, mended(here, early[here]), spectra_of, segments, scaling, out, left, result, sems)
 
 
 def local(tables, recording, trailing, whiten_filter, pair_list):
@@ -245,7 +249,7 @@
     if chain == 4:
         filters = [
             lax.ppermute(whiten_filter.T, "chan", [(i, i ^ step) for i in range(chain)])
-            for step in range(1, chain)
+            for step in (1, 3, 2)
         ]
     else:
         filters = [lax.all_gather(whiten_filter, ("chan", "freq"), axis=0, tiled=True)]
@@ -262,7 +266,7 @@
         scratch_shapes=[
             pltpu.VMEM(recording.shape, jnp.bfloat16),
             pltpu.VMEM(trailing.shape, jnp.bfloat16),
-            pltpu.SemaphoreType.DMA((3,)),
+            pltpu.SemaphoreType.DMA((4,)),
         ],
         compiler_params=small,
         name="begin_transform",
@@ -315,16 +319,8 @@
         across = [(2 * i + half, 2 * j + 1 - half) for i, j in route for half in range(2)]
         first_other = lax.ppermute(theirs, ("chan", "freq"), across)
         second = lax.ppermute(raw, "chan", [(1, 3), (3, 2), (2, 0), (0, 1)])
-        first, down, up = pl.pallas_call(
-            relay_kernel,
-            out_shape=[jax.ShapeDtypeStruct(total, jnp.bfloat16)] * 3,
-            in_specs=[in_vmem] * 3,
-            out_specs=[in_vmem] * 3,
-            compiler_params=small,
-            name="relay",
-        )(raw, first, first_other)
-        third = lax.ppermute(down, "chan", [(1, 0), (2, 1)])
-        fourth = lax.ppermute(up, "chan", [(2, 3), (1, 2)])
+        third = lax.ppermute(raw, "chan", [(1, 2), (2, 1)])
+        last = [lax.ppermute(value, "chan", [(1, 0), (2, 3)]) for value in (first, first_other)]
     else:
 
         def shifted(value, distance):
@@ -342,12 +338,12 @@
         operands = pl.pallas_call(
             early_kernel,
             out_shape=[jax.ShapeDtypeStruct(shape, jnp.bfloat16) for shape in (padded, spectra)],
-            in_specs=[in_vmem] * 4,
+            in_specs=[in_vmem] * 5,
             out_specs=[in_vmem] * 2,
             compiler_params=small,
             name="early_whitening",
-        )(raw, first, second, band)
-        operands = (*operands, third, fourth, band)
+        )(raw, first, first_other, second, band)
+        operands = (*operands, third, *last, band)
         kernel, scratch = late_kernel, []
     else:
         operands = (*blocks, band)
@@ -362,7 +358,7 @@
             *scratch,
             pltpu.VMEM((2 * block_rows, total[1]), jnp.bfloat16),
             pltpu.VMEM(out_shape, jnp.float32),
-            pltpu.SemaphoreType.DMA((SLOTS,)),
+            pltpu.SemaphoreType.DMA((SLOTS, 2)),
         ],
         compiler_params=pltpu.CompilerParams(vmem_limit_bytes=24 * 2**20),
         name="cross",

time: 35 us -> 35 us (level)
  starting transfers between devices: 13.6 us -> 14.2 us
  waiting for transfers between devices: 14.3 us -> 13.9 us
    ppermute x1, waiting for transfers between devices: 2.38 us -> 0.71 us  [local(): first_other = lax.ppermute(theirs, ('chan', 'freq'), across)]
    ppermute x2 -> x3, starting transfers between devices: 1.97 us -> 3.23 us  [the longest x2 2.56 us: local(): lax.ppermute(value, 'chan', [(1, 0), (2, 3)])]
    ppermute x1, waiting for transfers between devices: 2.21 us -> 3.2 us  [local(): second = lax.ppermute(raw, 'chan', [(1, 3), (3, 2), (2, 0), (0, 1)])]
    ppermute x1, starting transfers between devices: 1.54 us -> 0.73 us  [local(): second = lax.ppermute(raw, 'chan', [(1, 3), (3, 2), (2, 0), (0, 1)])]
    ppermute x1, starting transfers between devices: 0.31 us -> 1.12 us  [local(): first_other = lax.ppermute(theirs, ('chan', 'freq'), across)]
    ppermute x1, starting transfers between devices: 2.07 us -> 1.29 us  [local(): first = lax.ppermute(mine, 'chan', route)]
    ppermute x2 -> x3, waiting for transfers between devices: 4.69 us -> 4.68 us  [the longest x2 4.67 us: local(): lax.ppermute(value, 'chan', [(1, 0), (2, 3)])]
  transfers between devices with their start and end apart: 11 -> 12, of which waited for: 6 -> 7; matrix products, arithmetic and copies ran while one was open for 0% -> 0% of each run, Pallas kernels for 10% -> 10%
where the time goes in v5:
time: 35 us; the launch traced here: 34.8 us
  starting transfers between devices  14.2 us (41%)
  waiting for transfers between devices  13.9 us (40%)
  Pallas kernels  6.45 us (18%)
    ppermute x2, waiting for transfers between devices, local(): lax.ppermute(value, 'chan', [(1, 0), (2, 3)])  4.67 us
    ppermute x3, starting transfers between devices, local(): lax.ppermute(whiten_filter.T, 'chan', [(i, i ^ step) for i in range(chain)])  4.17 us
    ppermute x1, waiting for transfers between devices, local(): second = lax.ppermute(raw, 'chan', [(1, 3), (3, 2), (2, 0), (0, 1)])  3.2 us
    ppermute x1, starting transfers between devices, local(): lax.ppermute(recording, 'tm', [(i, (i + step) % spans) for i in range(spa...  2.94 us
    pallas_call x1, Pallas kernels, local(): pl.pallas_call(functools.partial(kernel, spans, 1.0 / math.sqrt(spans * b...  2.62 us
    ppermute x2, starting transfers between devices, local(): lax.ppermute(value, 'chan', [(1, 0), (2, 3)])  2.56 us
    ppermute x1, waiting for transfers between devices, local(): first = lax.ppermute(mine, 'chan', route)  2.5 us
    pallas_call x1, Pallas kernels, local(): pl.pallas_call(begin_kernel, out_shape=[jax.ShapeDtypeStruct((rows, halve...  2.2 us
  transfers between devices with their start and end apart: 12, of which 7 were waited for; matrix products, arithmetic and copies ran while one was open for 0% of the time, Pallas kernels for 10%

profile of v5, /device:TPU:0, one launch (start us, length us, event | category | flops | bytes accessed | tf_op | source)
XLA Modules:
  0.0 34.8 jit_solution(6190938321377585204)
XLA Ops:
  0.0 2.9 %collective-permute-start = (bf16[128,1024]{1,0:T(8,128)(2,1)}, bf16[128,1024]{1,0:T(8,128)(2,1)S(1)}, u32[]{:S(2)}, u32[]{:S(2)}) collective-permute-start(bf16[128,1024]{1,0:T(8,128)(2,1)} %recording.1), channel_id=1, source_target_pairs={{0,2},{2,0},{1,3},{3,1},{4,6},{6,4},{5,7},{7,5},{8,10},{10,8},{9,1... | collective-permute-start | bytes 786440 | tf_op jit(solution)/shard_map/ppermute | solution.py:246
  2.9 2.6 %collective-permute-start.3 = (bf16[64,128]{1,0:T(8,128)(2,1)}, bf16[64,128]{1,0:T(8,128)(2,1)S(1)}, u32[]{:S(2)}, u32[]{:S(2)}) collective-permute-start(bf16[64,128]{1,0:T(8,128)(2,1)} %bitcast.9), channel_id=1, source_target_pairs={{0,8},{4,12},{8,0},{12,4},{1,9},{5,13},{9,1},{13,5},{2,10},{6,14},... | collective-permute-start | bytes 49160 | tf_op jit(solution)/shard_map/ppermute | solution.py:251
  5.5 1.3 %collective-permute-start.2 = (bf16[64,128]{1,0:T(8,128)(2,1)}, bf16[64,128]{1,0:T(8,128)(2,1)S(1)}, u32[]{:S(2)}, u32[]{:S(2)}) collective-permute-start(bf16[64,128]{1,0:T(8,128)(2,1)} %bitcast.10), channel_id=1, source_target_pairs={{0,12},{4,8},{8,4},{12,0},{1,13},{5,9},{9,5},{13,1},{2,14},{6,10},... | collective-permute-start | bytes 49160 | tf_op jit(solution)/shard_map/ppermute | solution.py:251
  6.9 0.2 collective-permute-start.1
  7.1 2.2 %begin_transform.1 = (f32[128,1024]{1,0:T(8,128)S(1)}, bf16[2048,512]{1,0:T(8,128)(2,1)S(1)}) custom-call(bf16[128,1024]{1,0:T(8,128)(2,1)} %recording.1, bf16[128,1024]{1,0:T(8,128)(2,1)} %trailing.1, bf16[2,2048,512]{2,1,0:T(8,128)(2,1)} %constant.2.clone.tables), custom_call_target="tpu_custom_call" | custom-call | tf_op jit(solution)/shard_map/begin_transform/pallas_call | solution.py:258
  9.3 0.0 copy-start.1
  9.3 0.0 collective-permute-done.3
  9.3 1.9 %collective-permute-done.2 = bf16[64,128]{1,0:T(8,128)(2,1)S(1)} collective-permute-done((bf16[64,128]{1,0:T(8,128)(2,1)}, bf16[64,128]{1,0:T(8,128)(2,1)S(1)}, u32[]{:S(2)}, u32[]{:S(2)}) %collective-permute-start.2) | collective-permute-done | bytes 16416 | tf_op jit(solution)/shard_map/ppermute | solution.py:251
  11.3 0.0 collective-permute-done.1
  11.3 0.0 collective-permute-done.refs_0_
  11.3 0.5 %finish_transform.1 = (bf16[128,512]{1,0:T(8,128)(2,1)S(1)}, bf16[128,512]{1,0:T(8,128)(2,1)S(1)}) custom-call(bf16[128,1024]{1,0:T(8,128)(2,1)S(1)} %collective-permute-done.refs_0_, bf16[2048,512]{1,0:T(8,128)(2,1)S(1)} %get-tuple-element.18.refs_1_, f32[128,1024]{1,0:T(8,128)S(1)} %get-tuple-element.19.refs_2_), custom_call_target="tpu_custom_call" | custom-call | tf_op jit(solution)/shard_map/finish_transform/pallas_call | solution.py:281
  11.8 0.0 copy-start
  11.8 0.1 collective-permute-start.4
  11.9 1.3 %collective-permute-start.5 = (bf16[128,512]{1,0:T(8,128)(2,1)S(1)}, bf16[128,512]{1,0:T(8,128)(2,1)S(1)}, u32[]{:S(2)}, u32[]{:S(2)}) collective-permute-start(bf16[128,512]{1,0:T(8,128)(2,1)S(1)} %get-tuple-element.20.own), channel_id=1, source_target_pairs={{0,8},{8,12},{12,4},{4,0},{1,9},{9,13},{13,5},{5,1},{2,10},{10,14}... | collective-permute-start | bytes 393224 | tf_op jit(solution)/shard_map/ppermute | solution.py:318
  13.2 1.1 %collective-permute-start.6 = (bf16[128,512]{1,0:T(8,128)(2,1)S(1)}, bf16[128,512]{1,0:T(8,128)(2,1)S(1)}, u32[]{:S(2)}, u32[]{:S(2)}) collective-permute-start(bf16[128,512]{1,0:T(8,128)(2,1)S(1)} %get-tuple-element.21), channel_id=1, source_target_pairs={{0,9},{1,8},{8,13},{9,12},{12,5},{13,4},{4,1},{5,0},{2,11},{3,10},... | collective-permute-start | bytes 393224 | tf_op jit(solution)/shard_map/ppermute | solution.py:320
  14.3 0.0 collective-permute-done.4.other
  14.3 0.7 %collective-permute-start.7 = (bf16[256,512]{1,0:T(8,128)(2,1)S(1)}, bf16[256,512]{1,0:T(8,128)(2,1)S(1)}, u32[]{:S(2)}, u32[]{:S(2)}) collective-permute-start(bf16[256,512]{1,0:T(8,128)(2,1)S(1)} %block.1.raw), channel_id=1, source_target_pairs={{4,12},{12,8},{8,0},{0,4},{5,13},{13,9},{9,1},{1,5},{6,14},{14,10}... | collective-permute-start | bytes 786440 | tf_op jit(solution)/shard_map/ppermute | solution.py:321
  15.0 0.7 %collective-permute-start.9 = (bf16[256,512]{1,0:T(8,128)(2,1)S(1)}, bf16[256,512]{1,0:T(8,128)(2,1)S(1)}, u32[]{:S(2)}, u32[]{:S(2)}) collective-permute-start(bf16[256,512]{1,0:T(8,128)(2,1)S(1)} %block.1.raw), channel_id=1, source_target_pairs={{4,8},{8,4},{5,9},{9,5},{6,10},{10,6},{7,11},{11,7},{20,24},{24,20... | collective-permute-start | bytes 786440 | tf_op jit(solution)/shard_map/ppermute | solution.py:322
  15.7 2.5 %collective-permute-done.5.first = bf16[128,512]{1,0:T(8,128)(2,1)S(1)} collective-permute-done((bf16[128,512]{1,0:T(8,128)(2,1)S(1)}, bf16[128,512]{1,0:T(8,128)(2,1)S(1)}, u32[]{:S(2)}, u32[]{:S(2)}) %collective-permute-start.5) | collective-permute-done | bytes 131104 | tf_op jit(solution)/shard_map/ppermute | solution.py:318
  18.2 1.3 %collective-permute-start.10 = (bf16[128,512]{1,0:T(8,128)(2,1)S(1)}, bf16[128,512]{1,0:T(8,128)(2,1)S(1)}, u32[]{:S(2)}, u32[]{:S(2)}) collective-permute-start(bf16[128,512]{1,0:T(8,128)(2,1)S(1)} %collective-permute-done.5.first), channel_id=1, source_target_pairs={{4,0},{8,12},{5,1},{9,13},{6,2},{10,14},{7,3},{11,15},{20,16},{24,... | collective-permute-start | bytes 393224 | tf_op jit(solution)/shard_map/ppermute | solution.py:323
  19.5 0.7 %collective-permute-done.6.first_other = bf16[128,512]{1,0:T(8,128)(2,1)S(1)} collective-permute-done((bf16[128,512]{1,0:T(8,128)(2,1)S(1)}, bf16[128,512]{1,0:T(8,128)(2,1)S(1)}, u32[]{:S(2)}, u32[]{:S(2)}) %collective-permute-start.6) | collective-permute-done | bytes 131104 | tf_op jit(solution)/shard_map/ppermute | solution.py:320
  20.2 1.3 %collective-permute-start.11 = (bf16[128,512]{1,0:T(8,128)(2,1)S(1)}, bf16[128,512]{1,0:T(8,128)(2,1)S(1)}, u32[]{:S(2)}, u32[]{:S(2)}) collective-permute-start(bf16[128,512]{1,0:T(8,128)(2,1)S(1)} %collective-permute-done.6.first_other), channel_id=1, source_target_pairs={{4,0},{8,12},{5,1},{9,13},{6,2},{10,14},{7,3},{11,15},{20,16},{24,... | collective-permute-start | bytes 393224 | tf_op jit(solution)/shard_map/ppermute | solution.py:323
  21.5 0.0 copy-done.1
  21.5 0.7 %collective-permute-start.8 = (bf16[4,64,128]{2,1,0:T(8,128)(2,1)S(1)}, bf16[4,64,128]{2,1,0:T(8,128)(2,1)S(1)}, u32[]{:S(2)}, u32[]{:S(2)}) collective-permute-start(bf16[4,64,128]{2,1,0:T(8,128)(2,1)S(1)} %pad_maximum_fusion.refs_0_), channel_id=1, source_target_pairs={{0,1},{1,0},{2,3},{3,2},{4,5},{5,4},{6,7},{7,6},{8,9},{9,8},{10,11... | collective-permute-start | bytes 196616 | tf_op jit(solution)/shard_map/ppermute | solution.py:34
  22.2 0.9 %collective-permute-done.8.refs_1_ = bf16[4,64,128]{2,1,0:T(8,128)(2,1)S(1)} collective-permute-done((bf16[4,64,128]{2,1,0:T(8,128)(2,1)S(1)}, bf16[4,64,128]{2,1,0:T(8,128)(2,1)S(1)}, u32[]{:S(2)}, u32[]{:S(2)}) %collective-permute-start.8) | collective-permute-done | bytes 65568 | tf_op jit(solution)/shard_map/ppermute | solution.py:34
  23.1 0.3 band_matrix.1.band
  23.4 3.2 %collective-permute-done.7.second = bf16[256,512]{1,0:T(8,128)(2,1)S(1)} collective-permute-done((bf16[256,512]{1,0:T(8,128)(2,1)S(1)}, bf16[256,512]{1,0:T(8,128)(2,1)S(1)}, u32[]{:S(2)}, u32[]{:S(2)}) %collective-permute-start.7) | collective-permute-done | bytes 262176 | tf_op jit(solution)/shard_map/ppermute | solution.py:321
  26.6 0.8 %early_whitening.1 = (bf16[1152,512]{1,0:T(8,128)(2,1)S(1)}, bf16[4,256,512]{2,1,0:T(8,128)(2,1)S(1)}) custom-call(bf16[256,512]{1,0:T(8,128)(2,1)S(1)} %block.1.raw, bf16[128,512]{1,0:T(8,128)(2,1)S(1)} %collective-permute-done.5.first, bf16[128,512]{1,0:T(8,128)(2,1)S(1)} %collective-permute-done.6.first_other, ...), custom_call_target="tpu_custom_call" | custom-call | tf_op jit(solution)/shard_map/early_whitening/pallas_call | solution.py:338
  27.5 2.0 %collective-permute-done.10.fourth = bf16[128,512]{1,0:T(8,128)(2,1)S(1)} collective-permute-done((bf16[128,512]{1,0:T(8,128)(2,1)S(1)}, bf16[128,512]{1,0:T(8,128)(2,1)S(1)}, u32[]{:S(2)}, u32[]{:S(2)}) %collective-permute-start.10) | collective-permute-done | bytes 131104 | tf_op jit(solution)/shard_map/ppermute | solution.py:323
  29.4 2.7 %collective-permute-done.11.fourth_other = bf16[128,512]{1,0:T(8,128)(2,1)S(1)} collective-permute-done((bf16[128,512]{1,0:T(8,128)(2,1)S(1)}, bf16[128,512]{1,0:T(8,128)(2,1)S(1)}, u32[]{:S(2)}, u32[]{:S(2)}) %collective-permute-start.11) | collective-permute-done | bytes 131104 | tf_op jit(solution)/shard_map/ppermute | solution.py:323
  32.1 0.0 collective-permute-done.9.third
  32.1 0.0 copy-done
  32.2 2.6 %cross.1 = f32[4,2,256,256]{3,2,1,0:T(8,128)} custom-call(s32[1,4]{1,0:T(1,128)S(1)} %copy-done, bf16[1152,512]{1,0:T(8,128)(2,1)S(1)} %get-tuple-element.25.padded, bf16[4,256,512]{2,1,0:T(8,128)(2,1)S(1)} %get-tuple-element.26.early, bf16[256,512]{1,0:T(8,128)(2,1)S(1)} %collective-permute-done.9.third, ...), custom_call_target="tpu_custom_call" | custom-call | tf_op jit(solution)/shard_map/cross/pallas_call | solution.py:352
  (2 shorter events, 0.0 us)
Async XLA Ops:
  0.0 11.3 %collective-permute-start = (bf16[128,1024]{1,0:T(8,128)(2,1)}, bf16[128,1024]{1,0:T(8,128)(2,1)S(1)}, u32[]{:S(2)}, u32[]{:S(2)}) collective-permute-start(bf16[128,1024]{1,0:T(8,128)(2,1)} %recording.1), channel_id=1, source_target_pairs={{0,2},{2,0},{1,3},{3,1},{4,6},{6,4},{5,7},{7,5},{8,10},{10,8},{9,1... | collective-permute-start | bytes 786440 | tf_op jit(solution)/shard_map/ppermute | solution.py:246
  2.9 6.4 %collective-permute-start.3 = (bf16[64,128]{1,0:T(8,128)(2,1)}, bf16[64,128]{1,0:T(8,128)(2,1)S(1)}, u32[]{:S(2)}, u32[]{:S(2)}) collective-permute-start(bf16[64,128]{1,0:T(8,128)(2,1)} %bitcast.9), channel_id=1, source_target_pairs={{0,8},{4,12},{8,0},{12,4},{1,9},{5,13},{9,1},{13,5},{2,10},{6,14},... | collective-permute-start | bytes 49160 | tf_op jit(solution)/shard_map/ppermute | solution.py:251
  5.5 5.7 %collective-permute-start.2 = (bf16[64,128]{1,0:T(8,128)(2,1)}, bf16[64,128]{1,0:T(8,128)(2,1)S(1)}, u32[]{:S(2)}, u32[]{:S(2)}) collective-permute-start(bf16[64,128]{1,0:T(8,128)(2,1)} %bitcast.10), channel_id=1, source_target_pairs={{0,12},{4,8},{8,4},{12,0},{1,13},{5,9},{9,5},{13,1},{2,14},{6,10},... | collective-permute-start | bytes 49160 | tf_op jit(solution)/shard_map/ppermute | solution.py:251
  6.9 4.4 %collective-permute-start.1 = (bf16[64,128]{1,0:T(8,128)(2,1)}, bf16[64,128]{1,0:T(8,128)(2,1)S(1)}, u32[]{:S(2)}, u32[]{:S(2)}) collective-permute-start(bf16[64,128]{1,0:T(8,128)(2,1)} %bitcast.11), channel_id=1, source_target_pairs={{0,4},{4,0},{8,12},{12,8},{1,5},{5,1},{9,13},{13,9},{2,6},{6,2},{1... | collective-permute-start | bytes 49160 | tf_op jit(solution)/shard_map/ppermute | solution.py:251
  9.3 12.2 %copy-start.1 = (bf16[128,64]{0,1:T(8,128)(2,1)S(1)}, bf16[128,64]{0,1:T(8,128)(2,1)}, u32[]{:S(2)}) copy-start(bf16[128,64]{0,1:T(8,128)(2,1)} %param.7) | copy-start | bytes 49156
  11.8 20.4 %copy-start = (s32[1,4]{1,0:T(1,128)S(1)}, s32[1,4]{1,0:T(1,128)}, u32[]{:S(2)}) copy-start(s32[1,4]{1,0:T(1,128)} %slots.1) | copy-start | bytes 52
  11.8 2.5 %collective-permute-start.4 = (bf16[128,512]{1,0:T(8,128)(2,1)S(1)}, bf16[128,512]{1,0:T(8,128)(2,1)S(1)}, u32[]{:S(2)}, u32[]{:S(2)}) collective-permute-start(bf16[128,512]{1,0:T(8,128)(2,1)S(1)} %get-tuple-element.21), channel_id=1, source_target_pairs={{0,1},{1,0},{2,3},{3,2},{4,5},{5,4},{6,7},{7,6},{8,9},{9,8},{10,11... | collective-permute-start | bytes 393224 | tf_op jit(solution)/shard_map/ppermute | solution.py:34
  11.9 6.3 %collective-permute-start.5 = (bf16[128,512]{1,0:T(8,128)(2,1)S(1)}, bf16[128,512]{1,0:T(8,128)(2,1)S(1)}, u32[]{:S(2)}, u32[]{:S(2)}) collective-permute-start(bf16[128,512]{1,0:T(8,128)(2,1)S(1)} %get-tuple-element.20.own), channel_id=1, source_target_pairs={{0,8},{8,12},{12,4},{4,0},{1,9},{9,13},{13,5},{5,1},{2,10},{10,14}... | collective-permute-start | bytes 393224 | tf_op jit(solution)/shard_map/ppermute | solution.py:318
  13.2 7.1 %collective-permute-start.6 = (bf16[128,512]{1,0:T(8,128)(2,1)S(1)}, bf16[128,512]{1,0:T(8,128)(2,1)S(1)}, u32[]{:S(2)}, u32[]{:S(2)}) collective-permute-start(bf16[128,512]{1,0:T(8,128)(2,1)S(1)} %get-tuple-element.21), channel_id=1, source_target_pairs={{0,9},{1,8},{8,13},{9,12},{12,5},{13,4},{4,1},{5,0},{2,11},{3,10},... | collective-permute-start | bytes 393224 | tf_op jit(solution)/shard_map/ppermute | solution.py:320
  14.3 12.3 %collective-permute-start.7 = (bf16[256,512]{1,0:T(8,128)(2,1)S(1)}, bf16[256,512]{1,0:T(8,128)(2,1)S(1)}, u32[]{:S(2)}, u32[]{:S(2)}) collective-permute-start(bf16[256,512]{1,0:T(8,128)(2,1)S(1)} %block.1.raw), channel_id=1, source_target_pairs={{4,12},{12,8},{8,0},{0,4},{5,13},{13,9},{9,1},{1,5},{6,14},{14,10}... | collective-permute-start | bytes 786440 | tf_op jit(solution)/shard_map/ppermute | solution.py:321
  15.0 17.1 %collective-permute-start.9 = (bf16[256,512]{1,0:T(8,128)(2,1)S(1)}, bf16[256,512]{1,0:T(8,128)(2,1)S(1)}, u32[]{:S(2)}, u32[]{:S(2)}) collective-permute-start(bf16[256,512]{1,0:T(8,128)(2,1)S(1)} %block.1.raw), channel_id=1, source_target_pairs={{4,8},{8,4},{5,9},{9,5},{6,10},{10,6},{7,11},{11,7},{20,24},{24,20... | collective-permute-start | bytes 786440 | tf_op jit(solution)/shard_map/ppermute | solution.py:322
  18.2 11.2 %collective-permute-start.10 = (bf16[128,512]{1,0:T(8,128)(2,1)S(1)}, bf16[128,512]{1,0:T(8,128)(2,1)S(1)}, u32[]{:S(2)}, u32[]{:S(2)}) collective-permute-start(bf16[128,512]{1,0:T(8,128)(2,1)S(1)} %collective-permute-done.5.first), channel_id=1, source_target_pairs={{4,0},{8,12},{5,1},{9,13},{6,2},{10,14},{7,3},{11,15},{20,16},{24,... | collective-permute-start | bytes 393224 | tf_op jit(solution)/shard_map/ppermute | solution.py:323
  20.2 11.9 %collective-permute-start.11 = (bf16[128,512]{1,0:T(8,128)(2,1)S(1)}, bf16[128,512]{1,0:T(8,128)(2,1)S(1)}, u32[]{:S(2)}, u32[]{:S(2)}) collective-permute-start(bf16[128,512]{1,0:T(8,128)(2,1)S(1)} %collective-permute-done.6.first_other), channel_id=1, source_target_pairs={{4,0},{8,12},{5,1},{9,13},{6,2},{10,14},{7,3},{11,15},{20,16},{24,... | collective-permute-start | bytes 393224 | tf_op jit(solution)/shard_map/ppermute | solution.py:323
  21.5 1.6 %collective-permute-start.8 = (bf16[4,64,128]{2,1,0:T(8,128)(2,1)S(1)}, bf16[4,64,128]{2,1,0:T(8,128)(2,1)S(1)}, u32[]{:S(2)}, u32[]{:S(2)}) collective-permute-start(bf16[4,64,128]{2,1,0:T(8,128)(2,1)S(1)} %pad_maximum_fusion.refs_0_), channel_id=1, source_target_pairs={{0,1},{1,0},{2,3},{3,2},{4,5},{5,4},{6,7},{7,6},{8,9},{9,8},{10,11... | collective-permute-start | bytes 196616 | tf_op jit(solution)/shard_map/ppermute | solution.py:34

commit v6 on v5

--- a/solution.py
+++ b/solution.py
@@ -78,7 +78,8 @@
 
 
 def finish_kernel(spans, *refs):
-    hops, (table, begun, mine, theirs) = refs[: spans - 1], refs[spans - 1 :]
+    hops, (table, begun, mine, theirs, both) = refs[: spans - 1], refs[spans - 1 :]
+    rows = mine.shape[0]
     width = table.shape[1]
     part = width // 2
     low = lax.axis_index("freq") == 0
@@ -92,12 +93,16 @@
             value += more
         first, second = value[:, :part].astype(jnp.bfloat16), value[:, part:].astype(jnp.bfloat16)
         columns = slice(segment * part, (segment + 1) * part)
-        mine[:, columns] = jnp.where(low, first, second)
-        theirs[:, columns] = jnp.where(low, second, first)
+        mine[:, columns] = both[:rows, columns] = jnp.where(low, first, second)
+        theirs[:, columns] = both[rows:, columns] = jnp.where(low, second, first)
 
 
 def block_kernel(own, other, out):
     out[...] = block_of(own, other)
+
+
+def lower_kernel(value, out):
+    out[...] = value[out.shape[0] :, :]
 
 
 def band_kernel(chain, *refs):
@@ -172,7 +177,7 @@
     return jnp.where(here == 0, a, jnp.where(here == 1, b, jnp.where(here == 2, c, d)))
 
 
-def early_kernel(raw, first, first_other, second, band, padded, spectra):
+def early_kernel(raw, first, first_other, second, second_other, band, padded, spectra):
     count, rows, columns = spectra.shape
     rim = (padded.shape[0] - count * rows) // 4
     edge = count * rows + rim
@@ -183,7 +188,7 @@
     for place, value in (
         (lax.axis_index("chan"), raw),
         (chosen(1, 3, 0, 2), block_of(first, first_other)),
-        (chosen(2, 0, 3, 1), second),
+        (chosen(2, 0, 3, 1), block_of(second[: second_other.shape[0], :], second_other)),
     ):
         padded[pl.ds(pl.multiple_of(place * rows + rim, rim), rows), :] = value[...]
     for block in range(count):
@@ -278,11 +283,11 @@
     )
     received, filters, begun = lax.optimization_barrier((received, filters, begun))
     half_rows = (rows, total[1])
-    mine, theirs = pl.pallas_call(
+    mine, theirs, both = pl.pallas_call(
         functools.partial(finish_kernel, spans),
-        out_shape=[jax.ShapeDtypeStruct(half_rows, jnp.bfloat16)] * 2,
+        out_shape=[jax.ShapeDtypeStruct(shape, jnp.bfloat16) for shape in (half_rows, half_rows, total)],
         in_specs=[in_vmem] * (spans + 1),
-        out_specs=[in_vmem] * 2,
+        out_specs=[in_vmem] * 3,
         compiler_params=small,
         name="finish_transform",
     )(*received, table, begun)
@@ -318,7 +323,16 @@
         first = lax.ppermute(mine, "chan", route)
         across = [(2 * i + half, 2 * j + 1 - half) for i, j in route for half in range(2)]
         first_other = lax.ppermute(theirs, ("chan", "freq"), across)
-        second = lax.ppermute(raw, "chan", [(1, 3), (3, 2), (2, 0), (0, 1)])
+        second = lax.ppermute(both, "chan", [(1, 3), (3, 2), (2, 0), (0, 1)])
+        lower = pl.pallas_call(
+            lower_kernel,
+            out_shape=jax.ShapeDtypeStruct(half_rows, jnp.bfloat16),
+            in_specs=[in_vmem],
+            out_specs=in_vmem,
+            compiler_params=small,
+            name="lower_rows",
+        )(second)
+        second_other = swapped(lower, "freq")
         third = lax.ppermute(raw, "chan", [(1, 2), (2, 1)])
         last = [lax.ppermute(value, "chan", [(1, 0), (2, 3)]) for value in (first, first_other)]
     else:
@@ -338,11 +352,11 @@
         operands = pl.pallas_call(
             early_kernel,
             out_shape=[jax.ShapeDtypeStruct(shape, jnp.bfloat16) for shape in (padded, spectra)],
-            in_specs=[in_vmem] * 5,
+            in_specs=[in_vmem] * 6,
             out_specs=[in_vmem] * 2,
             compiler_params=small,
             name="early_whitening",
-        )(raw, first, first_other, second, band)
+        )(raw, first, first_other, second, second_other, band)
         operands = (*operands, third, *last, band)
         kernel, scratch = late_kernel, []
     else:

time: 35 us -> 34.9 us (level)
    ppermute x1, waiting for transfers between devices: 2.5 us -> 6.24 us  [local(): first = lax.ppermute(mine, 'chan', route)]
    ppermute x1, waiting for transfers between devices: 3.2 us -> 0.01 us  [local(): second = lax.ppermute(both, 'chan', [(1, 3), (3, 2), (2, 0), (0, 1)])]
    ppermute x1, starting transfers between devices: 1.29 us -> 2.84 us  [local(): first = lax.ppermute(mine, 'chan', route)]
    ppermute x2, waiting for transfers between devices: 4.67 us -> 3.37 us  [local(): lax.ppermute(value, 'chan', [(1, 0), (2, 3)])]
    ppermute x1, starting transfers between devices: 1.12 us -> 0.17 us  [local(): first_other = lax.ppermute(theirs, ('chan', 'freq'), across)]
    ppermute x1, waiting for transfers between devices: 0.71 us -> 1.49 us  [local(): first_other = lax.ppermute(theirs, ('chan', 'freq'), across)]
    ppermute x1, starting transfers between devices: 0.73 us -> 0.06 us  [local(): second = lax.ppermute(both, 'chan', [(1, 3), (3, 2), (2, 0), (0, 1)])]
    ppermute x2 -> x3, starting transfers between devices: 0.77 us -> 0.71 us  [swapped(): return lax.ppermute(value, axis, [(0, 1), (1, 0)])]
  transfers between devices with their start and end apart: 12 -> 13, of which waited for: 7 -> 6; matrix products, arithmetic and copies ran while one was open for 0% -> 0% of each run, Pallas kernels for 10% -> 10%
where the time goes in v6:
time: 34.9 us; the launch traced here: 34.7 us
  starting transfers between devices  14.1 us (40%)
  waiting for transfers between devices  14 us (40%)
  Pallas kernels  6.47 us (19%)
    ppermute x1, waiting for transfers between devices, local(): first = lax.ppermute(mine, 'chan', route)  6.24 us
    ppermute x3, starting transfers between devices, local(): lax.ppermute(whiten_filter.T, 'chan', [(i, i ^ step) for i in range(chain)])  4.17 us
    ppermute x2, waiting for transfers between devices, local(): lax.ppermute(value, 'chan', [(1, 0), (2, 3)])  3.37 us
    ppermute x1, starting transfers between devices, local(): lax.ppermute(recording, 'tm', [(i, (i + step) % spans) for i in range(spa...  2.94 us
    ppermute x1, starting transfers between devices, local(): first = lax.ppermute(mine, 'chan', route)  2.84 us
    pallas_call x1, Pallas kernels, local(): pl.pallas_call(functools.partial(kernel, spans, 1.0 / math.sqrt(spans * b...  2.62 us
    ppermute x2, starting transfers between devices, local(): lax.ppermute(value, 'chan', [(1, 0), (2, 3)])  2.56 us
    pallas_call x1, Pallas kernels, local(): pl.pallas_call(begin_kernel, out_shape=[jax.ShapeDtypeStruct((rows, halve...  2.2 us
  transfers between devices with their start and end apart: 13, of which 6 were waited for; matrix products, arithmetic and copies ran while one was open for 0% of the time, Pallas kernels for 10%

profile of v6, /device:TPU:0, one launch (start us, length us, event | category | flops | bytes accessed | tf_op | source)
XLA Modules:
  0.0 34.7 jit_solution(13885493554052058067)
XLA Ops:
  0.0 2.9 %collective-permute-start = (bf16[128,1024]{1,0:T(8,128)(2,1)}, bf16[128,1024]{1,0:T(8,128)(2,1)S(1)}, u32[]{:S(2)}, u32[]{:S(2)}) collective-permute-start(bf16[128,1024]{1,0:T(8,128)(2,1)} %recording.1), channel_id=1, source_target_pairs={{0,2},{2,0},{1,3},{3,1},{4,6},{6,4},{5,7},{7,5},{8,10},{10,8},{9,1... | collective-permute-start | bytes 786440 | tf_op jit(solution)/shard_map/ppermute | solution.py:251
  2.9 2.6 %collective-permute-start.3 = (bf16[64,128]{1,0:T(8,128)(2,1)}, bf16[64,128]{1,0:T(8,128)(2,1)S(1)}, u32[]{:S(2)}, u32[]{:S(2)}) collective-permute-start(bf16[64,128]{1,0:T(8,128)(2,1)} %bitcast.9), channel_id=1, source_target_pairs={{0,8},{4,12},{8,0},{12,4},{1,9},{5,13},{9,1},{13,5},{2,10},{6,14},... | collective-permute-start | bytes 49160 | tf_op jit(solution)/shard_map/ppermute | solution.py:256
  5.5 1.3 %collective-permute-start.2 = (bf16[64,128]{1,0:T(8,128)(2,1)}, bf16[64,128]{1,0:T(8,128)(2,1)S(1)}, u32[]{:S(2)}, u32[]{:S(2)}) collective-permute-start(bf16[64,128]{1,0:T(8,128)(2,1)} %bitcast.10), channel_id=1, source_target_pairs={{0,12},{4,8},{8,4},{12,0},{1,13},{5,9},{9,5},{13,1},{2,14},{6,10},... | collective-permute-start | bytes 49160 | tf_op jit(solution)/shard_map/ppermute | solution.py:256
  6.9 0.2 collective-permute-start.1
  7.1 2.2 %begin_transform.1 = (f32[128,1024]{1,0:T(8,128)S(1)}, bf16[2048,512]{1,0:T(8,128)(2,1)S(1)}) custom-call(bf16[128,1024]{1,0:T(8,128)(2,1)} %recording.1, bf16[128,1024]{1,0:T(8,128)(2,1)} %trailing.1, bf16[2,2048,512]{2,1,0:T(8,128)(2,1)} %constant.2.clone.tables), custom_call_target="tpu_custom_call" | custom-call | tf_op jit(solution)/shard_map/begin_transform/pallas_call | solution.py:263
  9.3 0.0 copy-start.1
  9.3 0.0 collective-permute-done.3
  9.3 1.9 %collective-permute-done.2 = bf16[64,128]{1,0:T(8,128)(2,1)S(1)} collective-permute-done((bf16[64,128]{1,0:T(8,128)(2,1)}, bf16[64,128]{1,0:T(8,128)(2,1)S(1)}, u32[]{:S(2)}, u32[]{:S(2)}) %collective-permute-start.2) | collective-permute-done | bytes 16416 | tf_op jit(solution)/shard_map/ppermute | solution.py:256
  11.3 0.0 collective-permute-done.1
  11.3 0.0 collective-permute-done.refs_0_
  11.3 0.5 %finish_transform.1 = (bf16[128,512]{1,0:T(8,128)(2,1)S(1)}, bf16[128,512]{1,0:T(8,128)(2,1)S(1)}, bf16[256,512]{1,0:T(8,128)(2,1)S(1)}) custom-call(bf16[128,1024]{1,0:T(8,128)(2,1)S(1)} %collective-permute-done.refs_0_, bf16[2048,512]{1,0:T(8,128)(2,1)S(1)} %get-tuple-element.19.refs_1_, f32[128,1024]{1,0:T(8,128)S(1)} %get-tuple-element.20.refs_2_), custom_call_target="tpu_custom_call" | custom-call | tf_op jit(solution)/shard_map/finish_transform/pallas_call | solution.py:286
  11.8 0.0 copy-start
  11.8 0.1 collective-permute-start.7
  11.9 0.1 collective-permute-start.4
  11.9 2.8 %collective-permute-start.5 = (bf16[128,512]{1,0:T(8,128)(2,1)S(1)}, bf16[128,512]{1,0:T(8,128)(2,1)S(1)}, u32[]{:S(2)}, u32[]{:S(2)}) collective-permute-start(bf16[128,512]{1,0:T(8,128)(2,1)S(1)} %get-tuple-element.21.own), channel_id=1, source_target_pairs={{0,8},{8,12},{12,4},{4,0},{1,9},{9,13},{13,5},{5,1},{2,10},{10,14}... | collective-permute-start | bytes 393224 | tf_op jit(solution)/shard_map/ppermute | solution.py:323
  14.8 0.2 collective-permute-start.6
  14.9 0.0 collective-permute-done.4.other
  15.0 0.7 %collective-permute-start.10 = (bf16[256,512]{1,0:T(8,128)(2,1)S(1)}, bf16[256,512]{1,0:T(8,128)(2,1)S(1)}, u32[]{:S(2)}, u32[]{:S(2)}) collective-permute-start(bf16[256,512]{1,0:T(8,128)(2,1)S(1)} %block.1.raw), channel_id=1, source_target_pairs={{4,8},{8,4},{5,9},{9,5},{6,10},{10,6},{7,11},{11,7},{20,24},{24,20... | collective-permute-start | bytes 786440 | tf_op jit(solution)/shard_map/ppermute | solution.py:336
  15.7 6.2 %collective-permute-done.5.first = bf16[128,512]{1,0:T(8,128)(2,1)S(1)} collective-permute-done((bf16[128,512]{1,0:T(8,128)(2,1)S(1)}, bf16[128,512]{1,0:T(8,128)(2,1)S(1)}, u32[]{:S(2)}, u32[]{:S(2)}) %collective-permute-start.5) | collective-permute-done | bytes 131104 | tf_op jit(solution)/shard_map/ppermute | solution.py:323
  21.9 1.3 %collective-permute-start.11 = (bf16[128,512]{1,0:T(8,128)(2,1)S(1)}, bf16[128,512]{1,0:T(8,128)(2,1)S(1)}, u32[]{:S(2)}, u32[]{:S(2)}) collective-permute-start(bf16[128,512]{1,0:T(8,128)(2,1)S(1)} %collective-permute-done.5.first), channel_id=1, source_target_pairs={{4,0},{8,12},{5,1},{9,13},{6,2},{10,14},{7,3},{11,15},{20,16},{24,... | collective-permute-start | bytes 393224 | tf_op jit(solution)/shard_map/ppermute | solution.py:337
  23.2 1.5 %collective-permute-done.6.first_other = bf16[128,512]{1,0:T(8,128)(2,1)S(1)} collective-permute-done((bf16[128,512]{1,0:T(8,128)(2,1)S(1)}, bf16[128,512]{1,0:T(8,128)(2,1)S(1)}, u32[]{:S(2)}, u32[]{:S(2)}) %collective-permute-start.6) | collective-permute-done | bytes 131104 | tf_op jit(solution)/shard_map/ppermute | solution.py:325
  24.7 1.3 %collective-permute-start.12 = (bf16[128,512]{1,0:T(8,128)(2,1)S(1)}, bf16[128,512]{1,0:T(8,128)(2,1)S(1)}, u32[]{:S(2)}, u32[]{:S(2)}) collective-permute-start(bf16[128,512]{1,0:T(8,128)(2,1)S(1)} %collective-permute-done.6.first_other), channel_id=1, source_target_pairs={{4,0},{8,12},{5,1},{9,13},{6,2},{10,14},{7,3},{11,15},{20,16},{24,... | collective-permute-start | bytes 393224 | tf_op jit(solution)/shard_map/ppermute | solution.py:337
  26.0 0.0 collective-permute-done.7.value.second
  26.0 0.2 collective-permute-start.8
  26.2 0.0 copy-done.1
  26.2 0.5 %collective-permute-start.9 = (bf16[4,64,128]{2,1,0:T(8,128)(2,1)S(1)}, bf16[4,64,128]{2,1,0:T(8,128)(2,1)S(1)}, u32[]{:S(2)}, u32[]{:S(2)}) collective-permute-start(bf16[4,64,128]{2,1,0:T(8,128)(2,1)S(1)} %pad_maximum_fusion.refs_0_), channel_id=1, source_target_pairs={{0,1},{1,0},{2,3},{3,2},{4,5},{5,4},{6,7},{7,6},{8,9},{9,8},{10,11... | collective-permute-start | bytes 196616 | tf_op jit(solution)/shard_map/ppermute | solution.py:34
  26.7 0.9 %collective-permute-done.9.refs_1_ = bf16[4,64,128]{2,1,0:T(8,128)(2,1)S(1)} collective-permute-done((bf16[4,64,128]{2,1,0:T(8,128)(2,1)S(1)}, bf16[4,64,128]{2,1,0:T(8,128)(2,1)S(1)}, u32[]{:S(2)}, u32[]{:S(2)}) %collective-permute-start.9) | collective-permute-done | bytes 65568 | tf_op jit(solution)/shard_map/ppermute | solution.py:34
  27.6 0.3 band_matrix.1.band
  27.9 0.0 collective-permute-done.8.second_other
  27.9 0.8 %early_whitening.1 = (bf16[1152,512]{1,0:T(8,128)(2,1)S(1)}, bf16[4,256,512]{2,1,0:T(8,128)(2,1)S(1)}) custom-call(bf16[256,512]{1,0:T(8,128)(2,1)S(1)} %block.1.raw, bf16[128,512]{1,0:T(8,128)(2,1)S(1)} %collective-permute-done.5.first, bf16[128,512]{1,0:T(8,128)(2,1)S(1)} %collective-permute-done.6.first_other, ...), custom_call_target="tpu_custom_call" | custom-call | tf_op jit(solution)/shard_map/early_whitening/pallas_call | solution.py:352
  28.7 0.6 %collective-permute-done.11.fourth = bf16[128,512]{1,0:T(8,128)(2,1)S(1)} collective-permute-done((bf16[128,512]{1,0:T(8,128)(2,1)S(1)}, bf16[128,512]{1,0:T(8,128)(2,1)S(1)}, u32[]{:S(2)}, u32[]{:S(2)}) %collective-permute-start.11) | collective-permute-done | bytes 131104 | tf_op jit(solution)/shard_map/ppermute | solution.py:337
  29.3 2.8 %collective-permute-done.12.fourth_other = bf16[128,512]{1,0:T(8,128)(2,1)S(1)} collective-permute-done((bf16[128,512]{1,0:T(8,128)(2,1)S(1)}, bf16[128,512]{1,0:T(8,128)(2,1)S(1)}, u32[]{:S(2)}, u32[]{:S(2)}) %collective-permute-start.12) | collective-permute-done | bytes 131104 | tf_op jit(solution)/shard_map/ppermute | solution.py:337
  32.1 0.0 collective-permute-done.10.third
  32.1 0.0 copy-done
  32.1 2.6 %cross.1 = f32[4,2,256,256]{3,2,1,0:T(8,128)} custom-call(s32[1,4]{1,0:T(1,128)S(1)} %copy-done, bf16[1152,512]{1,0:T(8,128)(2,1)S(1)} %get-tuple-element.27.padded, bf16[4,256,512]{2,1,0:T(8,128)(2,1)S(1)} %get-tuple-element.28.early, bf16[256,512]{1,0:T(8,128)(2,1)S(1)} %collective-permute-done.10.third, ...), custom_call_target="tpu_custom_call" | custom-call | tf_op jit(solution)/shard_map/cross/pallas_call | solution.py:366
  (3 shorter events, 0.0 us)
Async XLA Ops:
  0.0 11.3 %collective-permute-start = (bf16[128,1024]{1,0:T(8,128)(2,1)}, bf16[128,1024]{1,0:T(8,128)(2,1)S(1)}, u32[]{:S(2)}, u32[]{:S(2)}) collective-permute-start(bf16[128,1024]{1,0:T(8,128)(2,1)} %recording.1), channel_id=1, source_target_pairs={{0,2},{2,0},{1,3},{3,1},{4,6},{6,4},{5,7},{7,5},{8,10},{10,8},{9,1... | collective-permute-start | bytes 786440 | tf_op jit(solution)/shard_map/ppermute | solution.py:251
  2.9 6.4 %collective-permute-start.3 = (bf16[64,128]{1,0:T(8,128)(2,1)}, bf16[64,128]{1,0:T(8,128)(2,1)S(1)}, u32[]{:S(2)}, u32[]{:S(2)}) collective-permute-start(bf16[64,128]{1,0:T(8,128)(2,1)} %bitcast.9), channel_id=1, source_target_pairs={{0,8},{4,12},{8,0},{12,4},{1,9},{5,13},{9,1},{13,5},{2,10},{6,14},... | collective-permute-start | bytes 49160 | tf_op jit(solution)/shard_map/ppermute | solution.py:256
  5.5 5.7 %collective-permute-start.2 = (bf16[64,128]{1,0:T(8,128)(2,1)}, bf16[64,128]{1,0:T(8,128)(2,1)S(1)}, u32[]{:S(2)}, u32[]{:S(2)}) collective-permute-start(bf16[64,128]{1,0:T(8,128)(2,1)} %bitcast.10), channel_id=1, source_target_pairs={{0,12},{4,8},{8,4},{12,0},{1,13},{5,9},{9,5},{13,1},{2,14},{6,10},... | collective-permute-start | bytes 49160 | tf_op jit(solution)/shard_map/ppermute | solution.py:256
  6.9 4.4 %collective-permute-start.1 = (bf16[64,128]{1,0:T(8,128)(2,1)}, bf16[64,128]{1,0:T(8,128)(2,1)S(1)}, u32[]{:S(2)}, u32[]{:S(2)}) collective-permute-start(bf16[64,128]{1,0:T(8,128)(2,1)} %bitcast.11), channel_id=1, source_target_pairs={{0,4},{4,0},{8,12},{12,8},{1,5},{5,1},{9,13},{13,9},{2,6},{6,2},{1... | collective-permute-start | bytes 49160 | tf_op jit(solution)/shard_map/ppermute | solution.py:256
  9.3 16.9 %copy-start.1 = (bf16[128,64]{0,1:T(8,128)(2,1)S(1)}, bf16[128,64]{0,1:T(8,128)(2,1)}, u32[]{:S(2)}) copy-start(bf16[128,64]{0,1:T(8,128)(2,1)} %param.7) | copy-start | bytes 49156
  11.8 20.3 %copy-start = (s32[1,4]{1,0:T(1,128)S(1)}, s32[1,4]{1,0:T(1,128)}, u32[]{:S(2)}) copy-start(s32[1,4]{1,0:T(1,128)} %slots.1) | copy-start | bytes 52
  11.8 14.2 %collective-permute-start.7 = (bf16[256,512]{1,0:T(8,128)(2,1)S(1)}, bf16[256,512]{1,0:T(8,128)(2,1)S(1)}, u32[]{:S(2)}, u32[]{:S(2)}) collective-permute-start(bf16[256,512]{1,0:T(8,128)(2,1)S(1)} %get-tuple-element.23), channel_id=1, source_target_pairs={{4,12},{12,8},{8,0},{0,4},{5,13},{13,9},{9,1},{1,5},{6,14},{14,10}... | collective-permute-start | bytes 786440 | tf_op jit(solution)/shard_map/ppermute | solution.py:326
  11.9 3.1 %collective-permute-start.4 = (bf16[128,512]{1,0:T(8,128)(2,1)S(1)}, bf16[128,512]{1,0:T(8,128)(2,1)S(1)}, u32[]{:S(2)}, u32[]{:S(2)}) collective-permute-start(bf16[128,512]{1,0:T(8,128)(2,1)S(1)} %get-tuple-element.22), channel_id=1, source_target_pairs={{0,1},{1,0},{2,3},{3,2},{4,5},{5,4},{6,7},{7,6},{8,9},{9,8},{10,11... | collective-permute-start | bytes 393224 | tf_op jit(solution)/shard_map/ppermute | solution.py:34
  11.9 10.0 %collective-permute-start.5 = (bf16[128,512]{1,0:T(8,128)(2,1)S(1)}, bf16[128,512]{1,0:T(8,128)(2,1)S(1)}, u32[]{:S(2)}, u32[]{:S(2)}) collective-permute-start(bf16[128,512]{1,0:T(8,128)(2,1)S(1)} %get-tuple-element.21.own), channel_id=1, source_target_pairs={{0,8},{8,12},{12,4},{4,0},{1,9},{9,13},{13,5},{5,1},{2,10},{10,14}... | collective-permute-start | bytes 393224 | tf_op jit(solution)/shard_map/ppermute | solution.py:323
  14.8 9.9 %collective-permute-start.6 = (bf16[128,512]{1,0:T(8,128)(2,1)S(1)}, bf16[128,512]{1,0:T(8,128)(2,1)S(1)}, u32[]{:S(2)}, u32[]{:S(2)}) collective-permute-start(bf16[128,512]{1,0:T(8,128)(2,1)S(1)} %get-tuple-element.22), channel_id=1, source_target_pairs={{0,9},{1,8},{8,13},{9,12},{12,5},{13,4},{4,1},{5,0},{2,11},{3,10},... | collective-permute-start | bytes 393224 | tf_op jit(solution)/shard_map/ppermute | solution.py:325
  15.0 17.1 %collective-permute-start.10 = (bf16[256,512]{1,0:T(8,128)(2,1)S(1)}, bf16[256,512]{1,0:T(8,128)(2,1)S(1)}, u32[]{:S(2)}, u32[]{:S(2)}) collective-permute-start(bf16[256,512]{1,0:T(8,128)(2,1)S(1)} %block.1.raw), channel_id=1, source_target_pairs={{4,8},{8,4},{5,9},{9,5},{6,10},{10,6},{7,11},{11,7},{20,24},{24,20... | collective-permute-start | bytes 786440 | tf_op jit(solution)/shard_map/ppermute | solution.py:336
  21.9 7.4 %collective-permute-start.11 = (bf16[128,512]{1,0:T(8,128)(2,1)S(1)}, bf16[128,512]{1,0:T(8,128)(2,1)S(1)}, u32[]{:S(2)}, u32[]{:S(2)}) collective-permute-start(bf16[128,512]{1,0:T(8,128)(2,1)S(1)} %collective-permute-done.5.first), channel_id=1, source_target_pairs={{4,0},{8,12},{5,1},{9,13},{6,2},{10,14},{7,3},{11,15},{20,16},{24,... | collective-permute-start | bytes 393224 | tf_op jit(solution)/shard_map/ppermute | solution.py:337
  24.7 7.4 %collective-permute-start.12 = (bf16[128,512]{1,0:T(8,128)(2,1)S(1)}, bf16[128,512]{1,0:T(8,128)(2,1)S(1)}, u32[]{:S(2)}, u32[]{:S(2)}) collective-permute-start(bf16[128,512]{1,0:T(8,128)(2,1)S(1)} %collective-permute-done.6.first_other), channel_id=1, source_target_pairs={{4,0},{8,12},{5,1},{9,13},{6,2},{10,14},{7,3},{11,15},{20,16},{24,... | collective-permute-start | bytes 393224 | tf_op jit(solution)/shard_map/ppermute | solution.py:337
  26.0 1.9 %collective-permute-start.8 = (bf16[128,512]{1,0:T(8,128)(2,1)S(1)}, bf16[128,512]{1,0:T(8,128)(2,1)S(1)}, u32[]{:S(2)}, u32[]{:S(2)}) collective-permute-start(bf16[128,512]{1,0:T(8,128)(2,1)S(1)} %lower_rows.1), channel_id=1, source_target_pairs={{0,1},{1,0},{2,3},{3,2},{4,5},{5,4},{6,7},{7,6},{8,9},{9,8},{10,11... | collective-permute-start | bytes 393224 | tf_op jit(solution)/shard_map/ppermute | solution.py:34
  26.2 1.4 %collective-permute-start.9 = (bf16[4,64,128]{2,1,0:T(8,128)(2,1)S(1)}, bf16[4,64,128]{2,1,0:T(8,128)(2,1)S(1)}, u32[]{:S(2)}, u32[]{:S(2)}) collective-permute-start(bf16[4,64,128]{2,1,0:T(8,128)(2,1)S(1)} %pad_maximum_fusion.refs_0_), channel_id=1, source_target_pairs={{0,1},{1,0},{2,3},{3,2},{4,5},{5,4},{6,7},{7,6},{8,9},{9,8},{10,11... | collective-permute-start | bytes 196616 | tf_op jit(solution)/shard_map/ppermute | solution.py:34

commit v7 on v6

--- a/solution.py
+++ b/solution.py
@@ -177,7 +177,7 @@
     return jnp.where(here == 0, a, jnp.where(here == 1, b, jnp.where(here == 2, c, d)))
 
 
-def early_kernel(raw, first, first_other, second, second_other, band, padded, spectra):
+def early_kernel(raw, first, first_other, second, second_other, band, padded, spectra, beside, middle):
     count, rows, columns = spectra.shape
     rim = (padded.shape[0] - count * rows) // 4
     edge = count * rows + rim
@@ -196,8 +196,13 @@
         window = padded[start : start + band.shape[2], :]
         spectra[block] = whitened(band[block], window, padded[start + rim : start + rim + rows, :])
 
-
-def late_kernel(segments, scaling, slots, padded, early, third, fourth, fourth_other, band, out, left, result, sems):
+    window = padded[pl.ds(pl.multiple_of(last * rows, rows), band.shape[2]), :]
+    beside[...] = jnp.dot(band[last], window, preferred_element_type=jnp.float32)
+    wide = band[last].astype(jnp.float32)
+    middle[...] = pltpu.roll(wide, band.shape[2] - rim, 1)[:, :rows].astype(jnp.bfloat16)
+
+
+def late_kernel(segments, scaling, slots, padded, early, beside, middle, third, fourth, fourth_other, band, out, left, result, sems):
     count, rows, columns = early.shape
     width = band.shape[2]
     rim = (padded.shape[0] - count * rows) // 4
@@ -209,8 +214,8 @@
     start = pl.multiple_of(last * rows, rows)
     above = padded[pl.ds(start, rim), :]
     below = padded[pl.ds(start + rim + rows, width - rim - rows), :]
-    window = jnp.concatenate([above, value, below], axis=0)
-    arrived = whitened(band[last], window, value)
+    predicted = jnp.dot(middle[...], value, preferred_element_type=jnp.float32) + beside[...]
+    arrived = (value.astype(jnp.float32) - predicted).astype(jnp.bfloat16)
 
     half = rows // 2
     upper = padded[pl.ds(pl.multiple_of(jnp.maximum(start - half, 0), half), half + rim), :]
@@ -351,9 +356,14 @@
     if chain == 4:
         operands = pl.pallas_call(
             early_kernel,
-            out_shape=[jax.ShapeDtypeStruct(shape, jnp.bfloat16) for shape in (padded, spectra)],
+            out_shape=[
+                jax.ShapeDtypeStruct(padded, jnp.bfloat16),
+                jax.ShapeDtypeStruct(spectra, jnp.bfloat16),
+                jax.ShapeDtypeStruct(total, jnp.float32),
+                jax.ShapeDtypeStruct((block_rows, block_rows), jnp.bfloat16),
+            ],
             in_specs=[in_vmem] * 6,
-            out_specs=[in_vmem] * 2,
+            out_specs=[in_vmem] * 4,
             compiler_params=small,
             name="early_whitening",
         )(raw, first, first_other, second, second_other, band)

time: 34.9 us -> 34.8 us (level)
  no operation moved by 1% of the time
where the time goes in v7:
time: 34.8 us; the launch traced here: 34.6 us
  starting transfers between devices  14.1 us (41%)
  waiting for transfers between devices  13.8 us (40%)
  Pallas kernels  6.54 us (19%)
    ppermute x1, waiting for transfers between devices, local(): first = lax.ppermute(mine, 'chan', route)  6.24 us
    ppermute x3, starting transfers between devices, local(): lax.ppermute(whiten_filter.T, 'chan', [(i, i ^ step) for i in range(chain)])  4.17 us
    ppermute x2, waiting for transfers between devices, local(): lax.ppermute(value, 'chan', [(1, 0), (2, 3)])  3.23 us
    ppermute x1, starting transfers between devices, local(): lax.ppermute(recording, 'tm', [(i, (i + step) % spans) for i in range(spa...  2.94 us
    ppermute x1, starting transfers between devices, local(): first = lax.ppermute(mine, 'chan', route)  2.84 us
    ppermute x2, starting transfers between devices, local(): lax.ppermute(value, 'chan', [(1, 0), (2, 3)])  2.56 us
    pallas_call x1, Pallas kernels, local(): pl.pallas_call(functools.partial(kernel, spans, 1.0 / math.sqrt(spans * b...  2.54 us
    pallas_call x1, Pallas kernels, local(): pl.pallas_call(begin_kernel, out_shape=[jax.ShapeDtypeStruct((rows, halve...  2.2 us
  transfers between devices with their start and end apart: 13, of which 6 were waited for; matrix products, arithmetic and copies ran while one was open for 0% of the time, Pallas kernels for 10%

profile of v7, /device:TPU:0, one launch (start us, length us, event | category | flops | bytes accessed | tf_op | source)
XLA Modules:
  0.0 34.6 jit_solution(14030884379339423501)
XLA Ops:
  0.0 2.9 %collective-permute-start = (bf16[128,1024]{1,0:T(8,128)(2,1)}, bf16[128,1024]{1,0:T(8,128)(2,1)S(1)}, u32[]{:S(2)}, u32[]{:S(2)}) collective-permute-start(bf16[128,1024]{1,0:T(8,128)(2,1)} %recording.1), channel_id=1, source_target_pairs={{0,2},{2,0},{1,3},{3,1},{4,6},{6,4},{5,7},{7,5},{8,10},{10,8},{9,1... | collective-permute-start | bytes 786440 | tf_op jit(solution)/shard_map/ppermute | solution.py:256
  2.9 2.6 %collective-permute-start.3 = (bf16[64,128]{1,0:T(8,128)(2,1)}, bf16[64,128]{1,0:T(8,128)(2,1)S(1)}, u32[]{:S(2)}, u32[]{:S(2)}) collective-permute-start(bf16[64,128]{1,0:T(8,128)(2,1)} %bitcast.9), channel_id=1, source_target_pairs={{0,8},{4,12},{8,0},{12,4},{1,9},{5,13},{9,1},{13,5},{2,10},{6,14},... | collective-permute-start | bytes 49160 | tf_op jit(solution)/shard_map/ppermute | solution.py:261
  5.5 1.3 %collective-permute-start.2 = (bf16[64,128]{1,0:T(8,128)(2,1)}, bf16[64,128]{1,0:T(8,128)(2,1)S(1)}, u32[]{:S(2)}, u32[]{:S(2)}) collective-permute-start(bf16[64,128]{1,0:T(8,128)(2,1)} %bitcast.10), channel_id=1, source_target_pairs={{0,12},{4,8},{8,4},{12,0},{1,13},{5,9},{9,5},{13,1},{2,14},{6,10},... | collective-permute-start | bytes 49160 | tf_op jit(solution)/shard_map/ppermute | solution.py:261
  6.9 0.2 collective-permute-start.1
  7.1 2.2 %begin_transform.1 = (f32[128,1024]{1,0:T(8,128)S(1)}, bf16[2048,512]{1,0:T(8,128)(2,1)S(1)}) custom-call(bf16[128,1024]{1,0:T(8,128)(2,1)} %recording.1, bf16[128,1024]{1,0:T(8,128)(2,1)} %trailing.1, bf16[2,2048,512]{2,1,0:T(8,128)(2,1)} %constant.2.clone.tables), custom_call_target="tpu_custom_call" | custom-call | tf_op jit(solution)/shard_map/begin_transform/pallas_call | solution.py:268
  9.3 0.0 copy-start.1
  9.3 0.0 collective-permute-done.3
  9.3 1.9 %collective-permute-done.2 = bf16[64,128]{1,0:T(8,128)(2,1)S(1)} collective-permute-done((bf16[64,128]{1,0:T(8,128)(2,1)}, bf16[64,128]{1,0:T(8,128)(2,1)S(1)}, u32[]{:S(2)}, u32[]{:S(2)}) %collective-permute-start.2) | collective-permute-done | bytes 16416 | tf_op jit(solution)/shard_map/ppermute | solution.py:261
  11.3 0.0 collective-permute-done.1
  11.3 0.0 collective-permute-done.refs_0_
  11.3 0.5 %finish_transform.1 = (bf16[128,512]{1,0:T(8,128)(2,1)S(1)}, bf16[128,512]{1,0:T(8,128)(2,1)S(1)}, bf16[256,512]{1,0:T(8,128)(2,1)S(1)}) custom-call(bf16[128,1024]{1,0:T(8,128)(2,1)S(1)} %collective-permute-done.refs_0_, bf16[2048,512]{1,0:T(8,128)(2,1)S(1)} %get-tuple-element.21.refs_1_, f32[128,1024]{1,0:T(8,128)S(1)} %get-tuple-element.22.refs_2_), custom_call_target="tpu_custom_call" | custom-call | tf_op jit(solution)/shard_map/finish_transform/pallas_call | solution.py:291
  11.8 0.0 copy-start
  11.8 0.1 collective-permute-start.7
  11.9 0.1 collective-permute-start.4
  11.9 2.8 %collective-permute-start.5 = (bf16[128,512]{1,0:T(8,128)(2,1)S(1)}, bf16[128,512]{1,0:T(8,128)(2,1)S(1)}, u32[]{:S(2)}, u32[]{:S(2)}) collective-permute-start(bf16[128,512]{1,0:T(8,128)(2,1)S(1)} %get-tuple-element.23.own), channel_id=1, source_target_pairs={{0,8},{8,12},{12,4},{4,0},{1,9},{9,13},{13,5},{5,1},{2,10},{10,14}... | collective-permute-start | bytes 393224 | tf_op jit(solution)/shard_map/ppermute | solution.py:328
  14.8 0.2 collective-permute-start.6
  14.9 0.0 collective-permute-done.4.other
  15.0 0.7 %collective-permute-start.10 = (bf16[256,512]{1,0:T(8,128)(2,1)S(1)}, bf16[256,512]{1,0:T(8,128)(2,1)S(1)}, u32[]{:S(2)}, u32[]{:S(2)}) collective-permute-start(bf16[256,512]{1,0:T(8,128)(2,1)S(1)} %block.1.raw), channel_id=1, source_target_pairs={{4,8},{8,4},{5,9},{9,5},{6,10},{10,6},{7,11},{11,7},{20,24},{24,20... | collective-permute-start | bytes 786440 | tf_op jit(solution)/shard_map/ppermute | solution.py:341
  15.7 6.2 %collective-permute-done.5.first = bf16[128,512]{1,0:T(8,128)(2,1)S(1)} collective-permute-done((bf16[128,512]{1,0:T(8,128)(2,1)S(1)}, bf16[128,512]{1,0:T(8,128)(2,1)S(1)}, u32[]{:S(2)}, u32[]{:S(2)}) %collective-permute-start.5) | collective-permute-done | bytes 131104 | tf_op jit(solution)/shard_map/ppermute | solution.py:328
  21.9 1.3 %collective-permute-start.11 = (bf16[128,512]{1,0:T(8,128)(2,1)S(1)}, bf16[128,512]{1,0:T(8,128)(2,1)S(1)}, u32[]{:S(2)}, u32[]{:S(2)}) collective-permute-start(bf16[128,512]{1,0:T(8,128)(2,1)S(1)} %collective-permute-done.5.first), channel_id=1, source_target_pairs={{4,0},{8,12},{5,1},{9,13},{6,2},{10,14},{7,3},{11,15},{20,16},{24,... | collective-permute-start | bytes 393224 | tf_op jit(solution)/shard_map/ppermute | solution.py:342
  23.2 1.5 %collective-permute-done.6.first_other = bf16[128,512]{1,0:T(8,128)(2,1)S(1)} collective-permute-done((bf16[128,512]{1,0:T(8,128)(2,1)S(1)}, bf16[128,512]{1,0:T(8,128)(2,1)S(1)}, u32[]{:S(2)}, u32[]{:S(2)}) %collective-permute-start.6) | collective-permute-done | bytes 131104 | tf_op jit(solution)/shard_map/ppermute | solution.py:330
  24.7 1.3 %collective-permute-start.12 = (bf16[128,512]{1,0:T(8,128)(2,1)S(1)}, bf16[128,512]{1,0:T(8,128)(2,1)S(1)}, u32[]{:S(2)}, u32[]{:S(2)}) collective-permute-start(bf16[128,512]{1,0:T(8,128)(2,1)S(1)} %collective-permute-done.6.first_other), channel_id=1, source_target_pairs={{4,0},{8,12},{5,1},{9,13},{6,2},{10,14},{7,3},{11,15},{20,16},{24,... | collective-permute-start | bytes 393224 | tf_op jit(solution)/shard_map/ppermute | solution.py:342
  26.0 0.0 collective-permute-done.7.value.second
  26.0 0.2 collective-permute-start.8
  26.2 0.0 copy-done.1
  26.2 0.5 %collective-permute-start.9 = (bf16[4,64,128]{2,1,0:T(8,128)(2,1)S(1)}, bf16[4,64,128]{2,1,0:T(8,128)(2,1)S(1)}, u32[]{:S(2)}, u32[]{:S(2)}) collective-permute-start(bf16[4,64,128]{2,1,0:T(8,128)(2,1)S(1)} %pad_maximum_fusion.refs_0_), channel_id=1, source_target_pairs={{0,1},{1,0},{2,3},{3,2},{4,5},{5,4},{6,7},{7,6},{8,9},{9,8},{10,11... | collective-permute-start | bytes 196616 | tf_op jit(solution)/shard_map/ppermute | solution.py:34
  26.7 0.9 %collective-permute-done.9.refs_1_ = bf16[4,64,128]{2,1,0:T(8,128)(2,1)S(1)} collective-permute-done((bf16[4,64,128]{2,1,0:T(8,128)(2,1)S(1)}, bf16[4,64,128]{2,1,0:T(8,128)(2,1)S(1)}, u32[]{:S(2)}, u32[]{:S(2)}) %collective-permute-start.9) | collective-permute-done | bytes 65568 | tf_op jit(solution)/shard_map/ppermute | solution.py:34
  27.6 0.3 band_matrix.1.band
  27.9 0.0 collective-permute-done.8.second_other
  27.9 1.0 %early_whitening.1 = (bf16[1152,512]{1,0:T(8,128)(2,1)S(1)}, bf16[4,256,512]{2,1,0:T(8,128)(2,1)S(1)}, f32[256,512]{1,0:T(8,128)S(1)}, bf16[256,256]{1,0:T(8,128)(2,1)S(1)}) custom-call(bf16[256,512]{1,0:T(8,128)(2,1)S(1)} %block.1.raw, bf16[128,512]{1,0:T(8,128)(2,1)S(1)} %collective-permute-done.5.first, ...), custom_call_target="tpu_custom_call" | custom-call | tf_op jit(solution)/shard_map/early_whitening/pallas_call | solution.py:357
  28.9 0.4 %collective-permute-done.11.fourth = bf16[128,512]{1,0:T(8,128)(2,1)S(1)} collective-permute-done((bf16[128,512]{1,0:T(8,128)(2,1)S(1)}, bf16[128,512]{1,0:T(8,128)(2,1)S(1)}, u32[]{:S(2)}, u32[]{:S(2)}) %collective-permute-start.11) | collective-permute-done | bytes 131104 | tf_op jit(solution)/shard_map/ppermute | solution.py:342
  29.3 2.8 %collective-permute-done.12.fourth_other = bf16[128,512]{1,0:T(8,128)(2,1)S(1)} collective-permute-done((bf16[128,512]{1,0:T(8,128)(2,1)S(1)}, bf16[128,512]{1,0:T(8,128)(2,1)S(1)}, u32[]{:S(2)}, u32[]{:S(2)}) %collective-permute-start.12) | collective-permute-done | bytes 131104 | tf_op jit(solution)/shard_map/ppermute | solution.py:342
  32.1 0.0 collective-permute-done.10.third
  32.1 0.0 copy-done
  32.1 2.5 %cross.1 = f32[4,2,256,256]{3,2,1,0:T(8,128)} custom-call(s32[1,4]{1,0:T(1,128)S(1)} %copy-done, bf16[1152,512]{1,0:T(8,128)(2,1)S(1)} %get-tuple-element.29.padded, bf16[4,256,512]{2,1,0:T(8,128)(2,1)S(1)} %get-tuple-element.30.early, f32[256,512]{1,0:T(8,128)S(1)} %get-tuple-element.31.beside, bf16[256,256]{1,0:T(8,128)(2,1)S(1)} %get-tuple-element.32.middle, ...), custom_call_target="tpu_custom_call" | custom-call | tf_op jit(solution)/shard_map/cross/pallas_call | solution.py:376
  (3 shorter events, 0.0 us)
Async XLA Ops:
  0.0 11.3 %collective-permute-start = (bf16[128,1024]{1,0:T(8,128)(2,1)}, bf16[128,1024]{1,0:T(8,128)(2,1)S(1)}, u32[]{:S(2)}, u32[]{:S(2)}) collective-permute-start(bf16[128,1024]{1,0:T(8,128)(2,1)} %recording.1), channel_id=1, source_target_pairs={{0,2},{2,0},{1,3},{3,1},{4,6},{6,4},{5,7},{7,5},{8,10},{10,8},{9,1... | collective-permute-start | bytes 786440 | tf_op jit(solution)/shard_map/ppermute | solution.py:256
  2.9 6.4 %collective-permute-start.3 = (bf16[64,128]{1,0:T(8,128)(2,1)}, bf16[64,128]{1,0:T(8,128)(2,1)S(1)}, u32[]{:S(2)}, u32[]{:S(2)}) collective-permute-start(bf16[64,128]{1,0:T(8,128)(2,1)} %bitcast.9), channel_id=1, source_target_pairs={{0,8},{4,12},{8,0},{12,4},{1,9},{5,13},{9,1},{13,5},{2,10},{6,14},... | collective-permute-start | bytes 49160 | tf_op jit(solution)/shard_map/ppermute | solution.py:261
  5.5 5.7 %collective-permute-start.2 = (bf16[64,128]{1,0:T(8,128)(2,1)}, bf16[64,128]{1,0:T(8,128)(2,1)S(1)}, u32[]{:S(2)}, u32[]{:S(2)}) collective-permute-start(bf16[64,128]{1,0:T(8,128)(2,1)} %bitcast.10), channel_id=1, source_target_pairs={{0,12},{4,8},{8,4},{12,0},{1,13},{5,9},{9,5},{13,1},{2,14},{6,10},... | collective-permute-start | bytes 49160 | tf_op jit(solution)/shard_map/ppermute | solution.py:261
  6.9 4.4 %collective-permute-start.1 = (bf16[64,128]{1,0:T(8,128)(2,1)}, bf16[64,128]{1,0:T(8,128)(2,1)S(1)}, u32[]{:S(2)}, u32[]{:S(2)}) collective-permute-start(bf16[64,128]{1,0:T(8,128)(2,1)} %bitcast.11), channel_id=1, source_target_pairs={{0,4},{4,0},{8,12},{12,8},{1,5},{5,1},{9,13},{13,9},{2,6},{6,2},{1... | collective-permute-start | bytes 49160 | tf_op jit(solution)/shard_map/ppermute | solution.py:261
  9.3 16.9 %copy-start.1 = (bf16[128,64]{0,1:T(8,128)(2,1)S(1)}, bf16[128,64]{0,1:T(8,128)(2,1)}, u32[]{:S(2)}) copy-start(bf16[128,64]{0,1:T(8,128)(2,1)} %param.7) | copy-start | bytes 49156
  11.8 20.3 %copy-start = (s32[1,4]{1,0:T(1,128)S(1)}, s32[1,4]{1,0:T(1,128)}, u32[]{:S(2)}) copy-start(s32[1,4]{1,0:T(1,128)} %slots.1) | copy-start | bytes 52
  11.8 14.2 %collective-permute-start.7 = (bf16[256,512]{1,0:T(8,128)(2,1)S(1)}, bf16[256,512]{1,0:T(8,128)(2,1)S(1)}, u32[]{:S(2)}, u32[]{:S(2)}) collective-permute-start(bf16[256,512]{1,0:T(8,128)(2,1)S(1)} %get-tuple-element.25), channel_id=1, source_target_pairs={{4,12},{12,8},{8,0},{0,4},{5,13},{13,9},{9,1},{1,5},{6,14},{14,10}... | collective-permute-start | bytes 786440 | tf_op jit(solution)/shard_map/ppermute | solution.py:331
  11.9 3.1 %collective-permute-start.4 = (bf16[128,512]{1,0:T(8,128)(2,1)S(1)}, bf16[128,512]{1,0:T(8,128)(2,1)S(1)}, u32[]{:S(2)}, u32[]{:S(2)}) collective-permute-start(bf16[128,512]{1,0:T(8,128)(2,1)S(1)} %get-tuple-element.24), channel_id=1, source_target_pairs={{0,1},{1,0},{2,3},{3,2},{4,5},{5,4},{6,7},{7,6},{8,9},{9,8},{10,11... | collective-permute-start | bytes 393224 | tf_op jit(solution)/shard_map/ppermute | solution.py:34
  11.9 10.0 %collective-permute-start.5 = (bf16[128,512]{1,0:T(8,128)(2,1)S(1)}, bf16[128,512]{1,0:T(8,128)(2,1)S(1)}, u32[]{:S(2)}, u32[]{:S(2)}) collective-permute-start(bf16[128,512]{1,0:T(8,128)(2,1)S(1)} %get-tuple-element.23.own), channel_id=1, source_target_pairs={{0,8},{8,12},{12,4},{4,0},{1,9},{9,13},{13,5},{5,1},{2,10},{10,14}... | collective-permute-start | bytes 393224 | tf_op jit(solution)/shard_map/ppermute | solution.py:328
  14.8 9.9 %collective-permute-start.6 = (bf16[128,512]{1,0:T(8,128)(2,1)S(1)}, bf16[128,512]{1,0:T(8,128)(2,1)S(1)}, u32[]{:S(2)}, u32[]{:S(2)}) collective-permute-start(bf16[128,512]{1,0:T(8,128)(2,1)S(1)} %get-tuple-element.24), channel_id=1, source_target_pairs={{0,9},{1,8},{8,13},{9,12},{12,5},{13,4},{4,1},{5,0},{2,11},{3,10},... | collective-permute-start | bytes 393224 | tf_op jit(solution)/shard_map/ppermute | solution.py:330
  15.0 17.1 %collective-permute-start.10 = (bf16[256,512]{1,0:T(8,128)(2,1)S(1)}, bf16[256,512]{1,0:T(8,128)(2,1)S(1)}, u32[]{:S(2)}, u32[]{:S(2)}) collective-permute-start(bf16[256,512]{1,0:T(8,128)(2,1)S(1)} %block.1.raw), channel_id=1, source_target_pairs={{4,8},{8,4},{5,9},{9,5},{6,10},{10,6},{7,11},{11,7},{20,24},{24,20... | collective-permute-start | bytes 786440 | tf_op jit(solution)/shard_map/ppermute | solution.py:341
  21.9 7.4 %collective-permute-start.11 = (bf16[128,512]{1,0:T(8,128)(2,1)S(1)}, bf16[128,512]{1,0:T(8,128)(2,1)S(1)}, u32[]{:S(2)}, u32[]{:S(2)}) collective-permute-start(bf16[128,512]{1,0:T(8,128)(2,1)S(1)} %collective-permute-done.5.first), channel_id=1, source_target_pairs={{4,0},{8,12},{5,1},{9,13},{6,2},{10,14},{7,3},{11,15},{20,16},{24,... | collective-permute-start | bytes 393224 | tf_op jit(solution)/shard_map/ppermute | solution.py:342
  24.7 7.4 %collective-permute-start.12 = (bf16[128,512]{1,0:T(8,128)(2,1)S(1)}, bf16[128,512]{1,0:T(8,128)(2,1)S(1)}, u32[]{:S(2)}, u32[]{:S(2)}) collective-permute-start(bf16[128,512]{1,0:T(8,128)(2,1)S(1)} %collective-permute-done.6.first_other), channel_id=1, source_target_pairs={{4,0},{8,12},{5,1},{9,13},{6,2},{10,14},{7,3},{11,15},{20,16},{24,... | collective-permute-start | bytes 393224 | tf_op jit(solution)/shard_map/ppermute | solution.py:342
  26.0 1.9 %collective-permute-start.8 = (bf16[128,512]{1,0:T(8,128)(2,1)S(1)}, bf16[128,512]{1,0:T(8,128)(2,1)S(1)}, u32[]{:S(2)}, u32[]{:S(2)}) collective-permute-start(bf16[128,512]{1,0:T(8,128)(2,1)S(1)} %lower_rows.1), channel_id=1, source_target_pairs={{0,1},{1,0},{2,3},{3,2},{4,5},{5,4},{6,7},{7,6},{8,9},{9,8},{10,11... | collective-permute-start | bytes 393224 | tf_op jit(solution)/shard_map/ppermute | solution.py:34
  26.2 1.4 %collective-permute-start.9 = (bf16[4,64,128]{2,1,0:T(8,128)(2,1)S(1)}, bf16[4,64,128]{2,1,0:T(8,128)(2,1)S(1)}, u32[]{:S(2)}, u32[]{:S(2)}) collective-permute-start(bf16[4,64,128]{2,1,0:T(8,128)(2,1)S(1)} %pad_maximum_fusion.refs_0_), channel_id=1, source_target_pairs={{0,1},{1,0},{2,3},{3,2},{4,5},{5,4},{6,7},{7,6},{8,9},{9,8},{10,11... | collective-permute-start | bytes 196616 | tf_op jit(solution)/shard_map/ppermute | solution.py:34

commit v8 on v7

--- a/solution.py
+++ b/solution.py
@@ -144,7 +144,7 @@
         theirs = spectra_of(jnp.maximum(partner, 0))
         for part, lhs in enumerate((left[:rows, :], left[rows:, :])):
             value = lax.dot_general(lhs, theirs, contract, preferred_element_type=jnp.float32)
-            result[slot, part] = jnp.where(partner >= 0, value * scaling, 0.0)
+            result[slot, part] = value * jnp.where(partner >= 0, scaling, 0.0)
             pltpu.make_async_copy(result.at[slot, part], out.at[slot, part], sems.at[slot, part]).start()
     for slot in range(SLOTS):
         for part in range(2):

time: 34.8 us -> 34.8 us (level)
  no operation moved by 1% of the time
where the time goes in v8:
time: 34.8 us; the launch traced here: 34.6 us
  starting transfers between devices  14.1 us (41%)
  waiting for transfers between devices  13.8 us (40%)
  Pallas kernels  6.54 us (19%)
    ppermute x1, waiting for transfers between devices, local(): first = lax.ppermute(mine, 'chan', route)  6.24 us
    ppermute x3, starting transfers between devices, local(): lax.ppermute(whiten_filter.T, 'chan', [(i, i ^ step) for i in range(chain)])  4.17 us
    ppermute x2, waiting for transfers between devices, local(): lax.ppermute(value, 'chan', [(1, 0), (2, 3)])  3.23 us
    ppermute x1, starting transfers between devices, local(): lax.ppermute(recording, 'tm', [(i, (i + step) % spans) for i in range(spa...  2.94 us
    ppermute x1, starting transfers between devices, local(): first = lax.ppermute(mine, 'chan', route)  2.84 us
    ppermute x2, starting transfers between devices, local(): lax.ppermute(value, 'chan', [(1, 0), (2, 3)])  2.56 us
    pallas_call x1, Pallas kernels, local(): pl.pallas_call(functools.partial(kernel, spans, 1.0 / math.sqrt(spans * b...  2.54 us
    pallas_call x1, Pallas kernels, local(): pl.pallas_call(begin_kernel, out_shape=[jax.ShapeDtypeStruct((rows, halve...  2.2 us
  transfers between devices with their start and end apart: 13, of which 6 were waited for; matrix products, arithmetic and copies ran while one was open for 0% of the time, Pallas kernels for 10%

profile of v8, /device:TPU:0, one launch (start us, length us, event | category | flops | bytes accessed | tf_op | source)
XLA Modules:
  0.0 34.6 jit_solution(9946349585396597444)
XLA Ops:
  0.0 2.9 %collective-permute-start = (bf16[128,1024]{1,0:T(8,128)(2,1)}, bf16[128,1024]{1,0:T(8,128)(2,1)S(1)}, u32[]{:S(2)}, u32[]{:S(2)}) collective-permute-start(bf16[128,1024]{1,0:T(8,128)(2,1)} %recording.1), channel_id=1, source_target_pairs={{0,2},{2,0},{1,3},{3,1},{4,6},{6,4},{5,7},{7,5},{8,10},{10,8},{9,1... | collective-permute-start | bytes 786440 | tf_op jit(solution)/shard_map/ppermute | solution.py:256
  2.9 2.6 %collective-permute-start.3 = (bf16[64,128]{1,0:T(8,128)(2,1)}, bf16[64,128]{1,0:T(8,128)(2,1)S(1)}, u32[]{:S(2)}, u32[]{:S(2)}) collective-permute-start(bf16[64,128]{1,0:T(8,128)(2,1)} %bitcast.9), channel_id=1, source_target_pairs={{0,8},{4,12},{8,0},{12,4},{1,9},{5,13},{9,1},{13,5},{2,10},{6,14},... | collective-permute-start | bytes 49160 | tf_op jit(solution)/shard_map/ppermute | solution.py:261
  5.5 1.3 %collective-permute-start.2 = (bf16[64,128]{1,0:T(8,128)(2,1)}, bf16[64,128]{1,0:T(8,128)(2,1)S(1)}, u32[]{:S(2)}, u32[]{:S(2)}) collective-permute-start(bf16[64,128]{1,0:T(8,128)(2,1)} %bitcast.10), channel_id=1, source_target_pairs={{0,12},{4,8},{8,4},{12,0},{1,13},{5,9},{9,5},{13,1},{2,14},{6,10},... | collective-permute-start | bytes 49160 | tf_op jit(solution)/shard_map/ppermute | solution.py:261
  6.9 0.2 collective-permute-start.1
  7.1 2.2 %begin_transform.1 = (f32[128,1024]{1,0:T(8,128)S(1)}, bf16[2048,512]{1,0:T(8,128)(2,1)S(1)}) custom-call(bf16[128,1024]{1,0:T(8,128)(2,1)} %recording.1, bf16[128,1024]{1,0:T(8,128)(2,1)} %trailing.1, bf16[2,2048,512]{2,1,0:T(8,128)(2,1)} %constant.2.clone.tables), custom_call_target="tpu_custom_call" | custom-call | tf_op jit(solution)/shard_map/begin_transform/pallas_call | solution.py:268
  9.3 0.0 copy-start.1
  9.3 0.0 collective-permute-done.3
  9.3 1.9 %collective-permute-done.2 = bf16[64,128]{1,0:T(8,128)(2,1)S(1)} collective-permute-done((bf16[64,128]{1,0:T(8,128)(2,1)}, bf16[64,128]{1,0:T(8,128)(2,1)S(1)}, u32[]{:S(2)}, u32[]{:S(2)}) %collective-permute-start.2) | collective-permute-done | bytes 16416 | tf_op jit(solution)/shard_map/ppermute | solution.py:261
  11.3 0.0 collective-permute-done.1
  11.3 0.0 collective-permute-done.refs_0_
  11.3 0.5 %finish_transform.1 = (bf16[128,512]{1,0:T(8,128)(2,1)S(1)}, bf16[128,512]{1,0:T(8,128)(2,1)S(1)}, bf16[256,512]{1,0:T(8,128)(2,1)S(1)}) custom-call(bf16[128,1024]{1,0:T(8,128)(2,1)S(1)} %collective-permute-done.refs_0_, bf16[2048,512]{1,0:T(8,128)(2,1)S(1)} %get-tuple-element.21.refs_1_, f32[128,1024]{1,0:T(8,128)S(1)} %get-tuple-element.22.refs_2_), custom_call_target="tpu_custom_call" | custom-call | tf_op jit(solution)/shard_map/finish_transform/pallas_call | solution.py:291
  11.8 0.0 copy-start
  11.8 0.1 collective-permute-start.7
  11.9 0.1 collective-permute-start.4
  11.9 2.8 %collective-permute-start.5 = (bf16[128,512]{1,0:T(8,128)(2,1)S(1)}, bf16[128,512]{1,0:T(8,128)(2,1)S(1)}, u32[]{:S(2)}, u32[]{:S(2)}) collective-permute-start(bf16[128,512]{1,0:T(8,128)(2,1)S(1)} %get-tuple-element.23.own), channel_id=1, source_target_pairs={{0,8},{8,12},{12,4},{4,0},{1,9},{9,13},{13,5},{5,1},{2,10},{10,14}... | collective-permute-start | bytes 393224 | tf_op jit(solution)/shard_map/ppermute | solution.py:328
  14.8 0.2 collective-permute-start.6
  14.9 0.0 collective-permute-done.4.other
  15.0 0.7 %collective-permute-start.10 = (bf16[256,512]{1,0:T(8,128)(2,1)S(1)}, bf16[256,512]{1,0:T(8,128)(2,1)S(1)}, u32[]{:S(2)}, u32[]{:S(2)}) collective-permute-start(bf16[256,512]{1,0:T(8,128)(2,1)S(1)} %block.1.raw), channel_id=1, source_target_pairs={{4,8},{8,4},{5,9},{9,5},{6,10},{10,6},{7,11},{11,7},{20,24},{24,20... | collective-permute-start | bytes 786440 | tf_op jit(solution)/shard_map/ppermute | solution.py:341
  15.7 6.2 %collective-permute-done.5.first = bf16[128,512]{1,0:T(8,128)(2,1)S(1)} collective-permute-done((bf16[128,512]{1,0:T(8,128)(2,1)S(1)}, bf16[128,512]{1,0:T(8,128)(2,1)S(1)}, u32[]{:S(2)}, u32[]{:S(2)}) %collective-permute-start.5) | collective-permute-done | bytes 131104 | tf_op jit(solution)/shard_map/ppermute | solution.py:328
  21.9 1.3 %collective-permute-start.11 = (bf16[128,512]{1,0:T(8,128)(2,1)S(1)}, bf16[128,512]{1,0:T(8,128)(2,1)S(1)}, u32[]{:S(2)}, u32[]{:S(2)}) collective-permute-start(bf16[128,512]{1,0:T(8,128)(2,1)S(1)} %collective-permute-done.5.first), channel_id=1, source_target_pairs={{4,0},{8,12},{5,1},{9,13},{6,2},{10,14},{7,3},{11,15},{20,16},{24,... | collective-permute-start | bytes 393224 | tf_op jit(solution)/shard_map/ppermute | solution.py:342
  23.2 1.5 %collective-permute-done.6.first_other = bf16[128,512]{1,0:T(8,128)(2,1)S(1)} collective-permute-done((bf16[128,512]{1,0:T(8,128)(2,1)S(1)}, bf16[128,512]{1,0:T(8,128)(2,1)S(1)}, u32[]{:S(2)}, u32[]{:S(2)}) %collective-permute-start.6) | collective-permute-done | bytes 131104 | tf_op jit(solution)/shard_map/ppermute | solution.py:330
  24.7 1.3 %collective-permute-start.12 = (bf16[128,512]{1,0:T(8,128)(2,1)S(1)}, bf16[128,512]{1,0:T(8,128)(2,1)S(1)}, u32[]{:S(2)}, u32[]{:S(2)}) collective-permute-start(bf16[128,512]{1,0:T(8,128)(2,1)S(1)} %collective-permute-done.6.first_other), channel_id=1, source_target_pairs={{4,0},{8,12},{5,1},{9,13},{6,2},{10,14},{7,3},{11,15},{20,16},{24,... | collective-permute-start | bytes 393224 | tf_op jit(solution)/shard_map/ppermute | solution.py:342
  26.0 0.0 collective-permute-done.7.value.second
  26.0 0.2 collective-permute-start.8
  26.2 0.0 copy-done.1
  26.2 0.5 %collective-permute-start.9 = (bf16[4,64,128]{2,1,0:T(8,128)(2,1)S(1)}, bf16[4,64,128]{2,1,0:T(8,128)(2,1)S(1)}, u32[]{:S(2)}, u32[]{:S(2)}) collective-permute-start(bf16[4,64,128]{2,1,0:T(8,128)(2,1)S(1)} %pad_maximum_fusion.refs_0_), channel_id=1, source_target_pairs={{0,1},{1,0},{2,3},{3,2},{4,5},{5,4},{6,7},{7,6},{8,9},{9,8},{10,11... | collective-permute-start | bytes 196616 | tf_op jit(solution)/shard_map/ppermute | solution.py:34
  26.7 0.9 %collective-permute-done.9.refs_1_ = bf16[4,64,128]{2,1,0:T(8,128)(2,1)S(1)} collective-permute-done((bf16[4,64,128]{2,1,0:T(8,128)(2,1)S(1)}, bf16[4,64,128]{2,1,0:T(8,128)(2,1)S(1)}, u32[]{:S(2)}, u32[]{:S(2)}) %collective-permute-start.9) | collective-permute-done | bytes 65568 | tf_op jit(solution)/shard_map/ppermute | solution.py:34
  27.6 0.3 band_matrix.1.band
  27.9 0.0 collective-permute-done.8.second_other
  27.9 1.0 %early_whitening.1 = (bf16[1152,512]{1,0:T(8,128)(2,1)S(1)}, bf16[4,256,512]{2,1,0:T(8,128)(2,1)S(1)}, f32[256,512]{1,0:T(8,128)S(1)}, bf16[256,256]{1,0:T(8,128)(2,1)S(1)}) custom-call(bf16[256,512]{1,0:T(8,128)(2,1)S(1)} %block.1.raw, bf16[128,512]{1,0:T(8,128)(2,1)S(1)} %collective-permute-done.5.first, ...), custom_call_target="tpu_custom_call" | custom-call | tf_op jit(solution)/shard_map/early_whitening/pallas_call | solution.py:357
  28.9 0.4 %collective-permute-done.11.fourth = bf16[128,512]{1,0:T(8,128)(2,1)S(1)} collective-permute-done((bf16[128,512]{1,0:T(8,128)(2,1)S(1)}, bf16[128,512]{1,0:T(8,128)(2,1)S(1)}, u32[]{:S(2)}, u32[]{:S(2)}) %collective-permute-start.11) | collective-permute-done | bytes 131104 | tf_op jit(solution)/shard_map/ppermute | solution.py:342
  29.3 2.8 %collective-permute-done.12.fourth_other = bf16[128,512]{1,0:T(8,128)(2,1)S(1)} collective-permute-done((bf16[128,512]{1,0:T(8,128)(2,1)S(1)}, bf16[128,512]{1,0:T(8,128)(2,1)S(1)}, u32[]{:S(2)}, u32[]{:S(2)}) %collective-permute-start.12) | collective-permute-done | bytes 131104 | tf_op jit(solution)/shard_map/ppermute | solution.py:342
  32.1 0.0 collective-permute-done.10.third
  32.1 0.0 copy-done
  32.1 2.5 %cross.1 = f32[4,2,256,256]{3,2,1,0:T(8,128)} custom-call(s32[1,4]{1,0:T(1,128)S(1)} %copy-done, bf16[1152,512]{1,0:T(8,128)(2,1)S(1)} %get-tuple-element.29.padded, bf16[4,256,512]{2,1,0:T(8,128)(2,1)S(1)} %get-tuple-element.30.early, f32[256,512]{1,0:T(8,128)S(1)} %get-tuple-element.31.beside, bf16[256,256]{1,0:T(8,128)(2,1)S(1)} %get-tuple-element.32.middle, ...), custom_call_target="tpu_custom_call" | custom-call | tf_op jit(solution)/shard_map/cross/pallas_call | solution.py:376
  (3 shorter events, 0.0 us)
Async XLA Ops:
  0.0 11.3 %collective-permute-start = (bf16[128,1024]{1,0:T(8,128)(2,1)}, bf16[128,1024]{1,0:T(8,128)(2,1)S(1)}, u32[]{:S(2)}, u32[]{:S(2)}) collective-permute-start(bf16[128,1024]{1,0:T(8,128)(2,1)} %recording.1), channel_id=1, source_target_pairs={{0,2},{2,0},{1,3},{3,1},{4,6},{6,4},{5,7},{7,5},{8,10},{10,8},{9,1... | collective-permute-start | bytes 786440 | tf_op jit(solution)/shard_map/ppermute | solution.py:256
  2.9 6.4 %collective-permute-start.3 = (bf16[64,128]{1,0:T(8,128)(2,1)}, bf16[64,128]{1,0:T(8,128)(2,1)S(1)}, u32[]{:S(2)}, u32[]{:S(2)}) collective-permute-start(bf16[64,128]{1,0:T(8,128)(2,1)} %bitcast.9), channel_id=1, source_target_pairs={{0,8},{4,12},{8,0},{12,4},{1,9},{5,13},{9,1},{13,5},{2,10},{6,14},... | collective-permute-start | bytes 49160 | tf_op jit(solution)/shard_map/ppermute | solution.py:261
  5.5 5.7 %collective-permute-start.2 = (bf16[64,128]{1,0:T(8,128)(2,1)}, bf16[64,128]{1,0:T(8,128)(2,1)S(1)}, u32[]{:S(2)}, u32[]{:S(2)}) collective-permute-start(bf16[64,128]{1,0:T(8,128)(2,1)} %bitcast.10), channel_id=1, source_target_pairs={{0,12},{4,8},{8,4},{12,0},{1,13},{5,9},{9,5},{13,1},{2,14},{6,10},... | collective-permute-start | bytes 49160 | tf_op jit(solution)/shard_map/ppermute | solution.py:261
  6.9 4.4 %collective-permute-start.1 = (bf16[64,128]{1,0:T(8,128)(2,1)}, bf16[64,128]{1,0:T(8,128)(2,1)S(1)}, u32[]{:S(2)}, u32[]{:S(2)}) collective-permute-start(bf16[64,128]{1,0:T(8,128)(2,1)} %bitcast.11), channel_id=1, source_target_pairs={{0,4},{4,0},{8,12},{12,8},{1,5},{5,1},{9,13},{13,9},{2,6},{6,2},{1... | collective-permute-start | bytes 49160 | tf_op jit(solution)/shard_map/ppermute | solution.py:261
  9.3 16.9 %copy-start.1 = (bf16[128,64]{0,1:T(8,128)(2,1)S(1)}, bf16[128,64]{0,1:T(8,128)(2,1)}, u32[]{:S(2)}) copy-start(bf16[128,64]{0,1:T(8,128)(2,1)} %param.7) | copy-start | bytes 49156
  11.8 20.3 %copy-start = (s32[1,4]{1,0:T(1,128)S(1)}, s32[1,4]{1,0:T(1,128)}, u32[]{:S(2)}) copy-start(s32[1,4]{1,0:T(1,128)} %slots.1) | copy-start | bytes 52
  11.8 14.2 %collective-permute-start.7 = (bf16[256,512]{1,0:T(8,128)(2,1)S(1)}, bf16[256,512]{1,0:T(8,128)(2,1)S(1)}, u32[]{:S(2)}, u32[]{:S(2)}) collective-permute-start(bf16[256,512]{1,0:T(8,128)(2,1)S(1)} %get-tuple-element.25), channel_id=1, source_target_pairs={{4,12},{12,8},{8,0},{0,4},{5,13},{13,9},{9,1},{1,5},{6,14},{14,10}... | collective-permute-start | bytes 786440 | tf_op jit(solution)/shard_map/ppermute | solution.py:331
  11.9 3.1 %collective-permute-start.4 = (bf16[128,512]{1,0:T(8,128)(2,1)S(1)}, bf16[128,512]{1,0:T(8,128)(2,1)S(1)}, u32[]{:S(2)}, u32[]{:S(2)}) collective-permute-start(bf16[128,512]{1,0:T(8,128)(2,1)S(1)} %get-tuple-element.24), channel_id=1, source_target_pairs={{0,1},{1,0},{2,3},{3,2},{4,5},{5,4},{6,7},{7,6},{8,9},{9,8},{10,11... | collective-permute-start | bytes 393224 | tf_op jit(solution)/shard_map/ppermute | solution.py:34
  11.9 10.0 %collective-permute-start.5 = (bf16[128,512]{1,0:T(8,128)(2,1)S(1)}, bf16[128,512]{1,0:T(8,128)(2,1)S(1)}, u32[]{:S(2)}, u32[]{:S(2)}) collective-permute-start(bf16[128,512]{1,0:T(8,128)(2,1)S(1)} %get-tuple-element.23.own), channel_id=1, source_target_pairs={{0,8},{8,12},{12,4},{4,0},{1,9},{9,13},{13,5},{5,1},{2,10},{10,14}... | collective-permute-start | bytes 393224 | tf_op jit(solution)/shard_map/ppermute | solution.py:328
  14.8 9.9 %collective-permute-start.6 = (bf16[128,512]{1,0:T(8,128)(2,1)S(1)}, bf16[128,512]{1,0:T(8,128)(2,1)S(1)}, u32[]{:S(2)}, u32[]{:S(2)}) collective-permute-start(bf16[128,512]{1,0:T(8,128)(2,1)S(1)} %get-tuple-element.24), channel_id=1, source_target_pairs={{0,9},{1,8},{8,13},{9,12},{12,5},{13,4},{4,1},{5,0},{2,11},{3,10},... | collective-permute-start | bytes 393224 | tf_op jit(solution)/shard_map/ppermute | solution.py:330
  15.0 17.1 %collective-permute-start.10 = (bf16[256,512]{1,0:T(8,128)(2,1)S(1)}, bf16[256,512]{1,0:T(8,128)(2,1)S(1)}, u32[]{:S(2)}, u32[]{:S(2)}) collective-permute-start(bf16[256,512]{1,0:T(8,128)(2,1)S(1)} %block.1.raw), channel_id=1, source_target_pairs={{4,8},{8,4},{5,9},{9,5},{6,10},{10,6},{7,11},{11,7},{20,24},{24,20... | collective-permute-start | bytes 786440 | tf_op jit(solution)/shard_map/ppermute | solution.py:341
  21.9 7.4 %collective-permute-start.11 = (bf16[128,512]{1,0:T(8,128)(2,1)S(1)}, bf16[128,512]{1,0:T(8,128)(2,1)S(1)}, u32[]{:S(2)}, u32[]{:S(2)}) collective-permute-start(bf16[128,512]{1,0:T(8,128)(2,1)S(1)} %collective-permute-done.5.first), channel_id=1, source_target_pairs={{4,0},{8,12},{5,1},{9,13},{6,2},{10,14},{7,3},{11,15},{20,16},{24,... | collective-permute-start | bytes 393224 | tf_op jit(solution)/shard_map/ppermute | solution.py:342
  24.7 7.4 %collective-permute-start.12 = (bf16[128,512]{1,0:T(8,128)(2,1)S(1)}, bf16[128,512]{1,0:T(8,128)(2,1)S(1)}, u32[]{:S(2)}, u32[]{:S(2)}) collective-permute-start(bf16[128,512]{1,0:T(8,128)(2,1)S(1)} %collective-permute-done.6.first_other), channel_id=1, source_target_pairs={{4,0},{8,12},{5,1},{9,13},{6,2},{10,14},{7,3},{11,15},{20,16},{24,... | collective-permute-start | bytes 393224 | tf_op jit(solution)/shard_map/ppermute | solution.py:342
  26.0 1.9 %collective-permute-start.8 = (bf16[128,512]{1,0:T(8,128)(2,1)S(1)}, bf16[128,512]{1,0:T(8,128)(2,1)S(1)}, u32[]{:S(2)}, u32[]{:S(2)}) collective-permute-start(bf16[128,512]{1,0:T(8,128)(2,1)S(1)} %lower_rows.1), channel_id=1, source_target_pairs={{0,1},{1,0},{2,3},{3,2},{4,5},{5,4},{6,7},{7,6},{8,9},{9,8},{10,11... | collective-permute-start | bytes 393224 | tf_op jit(solution)/shard_map/ppermute | solution.py:34
  26.2 1.4 %collective-permute-start.9 = (bf16[4,64,128]{2,1,0:T(8,128)(2,1)S(1)}, bf16[4,64,128]{2,1,0:T(8,128)(2,1)S(1)}, u32[]{:S(2)}, u32[]{:S(2)}) collective-permute-start(bf16[4,64,128]{2,1,0:T(8,128)(2,1)S(1)} %pad_maximum_fusion.refs_0_), channel_id=1, source_target_pairs={{0,1},{1,0},{2,3},{3,2},{4,5},{5,4},{6,7},{7,6},{8,9},{9,8},{10,11... | collective-permute-start | bytes 196616 | tf_op jit(solution)/shard_map/ppermute | solution.py:34

commit v9 on v7

--- a/solution.py
+++ b/solution.py
@@ -325,9 +325,9 @@
 
     if chain == 4:
         route = [(0, 2), (2, 3), (3, 1), (1, 0)]
-        first = lax.ppermute(mine, "chan", route)
         across = [(2 * i + half, 2 * j + 1 - half) for i, j in route for half in range(2)]
         first_other = lax.ppermute(theirs, ("chan", "freq"), across)
+        first = lax.ppermute(mine, "chan", route)
         second = lax.ppermute(both, "chan", [(1, 3), (3, 2), (2, 0), (0, 1)])
         lower = pl.pallas_call(
             lower_kernel,

time: 34.8 us -> 34.8 us (level)
  no operation moved by 1% of the time
where the time goes in v9:
time: 34.8 us; the launch traced here: 34.6 us
  starting transfers between devices  14.1 us (41%)
  waiting for transfers between devices  13.8 us (40%)
  Pallas kernels  6.54 us (19%)
    ppermute x1, waiting for transfers between devices, local(): first = lax.ppermute(mine, 'chan', route)  6.24 us
    ppermute x3, starting transfers between devices, local(): lax.ppermute(whiten_filter.T, 'chan', [(i, i ^ step) for i in range(chain)])  4.17 us
    ppermute x2, waiting for transfers between devices, local(): lax.ppermute(value, 'chan', [(1, 0), (2, 3)])  3.23 us
    ppermute x1, starting transfers between devices, local(): lax.ppermute(recording, 'tm', [(i, (i + step) % spans) for i in range(spa...  2.94 us
    ppermute x1, starting transfers between devices, local(): first = lax.ppermute(mine, 'chan', route)  2.84 us
    ppermute x2, starting transfers between devices, local(): lax.ppermute(value, 'chan', [(1, 0), (2, 3)])  2.56 us
    pallas_call x1, Pallas kernels, local(): pl.pallas_call(functools.partial(kernel, spans, 1.0 / math.sqrt(spans * b...  2.54 us
    pallas_call x1, Pallas kernels, local(): pl.pallas_call(begin_kernel, out_shape=[jax.ShapeDtypeStruct((rows, halve...  2.2 us
  transfers between devices with their start and end apart: 13, of which 6 were waited for; matrix products, arithmetic and copies ran while one was open for 0% of the time, Pallas kernels for 10%

profile of v9, /device:TPU:0, one launch (start us, length us, event | category | flops | bytes accessed | tf_op | source)
XLA Modules:
  0.0 34.6 jit_solution(14030884379339423501)
XLA Ops:
  0.0 2.9 %collective-permute-start = (bf16[128,1024]{1,0:T(8,128)(2,1)}, bf16[128,1024]{1,0:T(8,128)(2,1)S(1)}, u32[]{:S(2)}, u32[]{:S(2)}) collective-permute-start(bf16[128,1024]{1,0:T(8,128)(2,1)} %recording.1), channel_id=1, source_target_pairs={{0,2},{2,0},{1,3},{3,1},{4,6},{6,4},{5,7},{7,5},{8,10},{10,8},{9,1... | collective-permute-start | bytes 786440 | tf_op jit(solution)/shard_map/ppermute | solution.py:256
  2.9 2.6 %collective-permute-start.3 = (bf16[64,128]{1,0:T(8,128)(2,1)}, bf16[64,128]{1,0:T(8,128)(2,1)S(1)}, u32[]{:S(2)}, u32[]{:S(2)}) collective-permute-start(bf16[64,128]{1,0:T(8,128)(2,1)} %bitcast.9), channel_id=1, source_target_pairs={{0,8},{4,12},{8,0},{12,4},{1,9},{5,13},{9,1},{13,5},{2,10},{6,14},... | collective-permute-start | bytes 49160 | tf_op jit(solution)/shard_map/ppermute | solution.py:261
  5.5 1.3 %collective-permute-start.2 = (bf16[64,128]{1,0:T(8,128)(2,1)}, bf16[64,128]{1,0:T(8,128)(2,1)S(1)}, u32[]{:S(2)}, u32[]{:S(2)}) collective-permute-start(bf16[64,128]{1,0:T(8,128)(2,1)} %bitcast.10), channel_id=1, source_target_pairs={{0,12},{4,8},{8,4},{12,0},{1,13},{5,9},{9,5},{13,1},{2,14},{6,10},... | collective-permute-start | bytes 49160 | tf_op jit(solution)/shard_map/ppermute | solution.py:261
  6.9 0.2 collective-permute-start.1
  7.1 2.2 %begin_transform.1 = (f32[128,1024]{1,0:T(8,128)S(1)}, bf16[2048,512]{1,0:T(8,128)(2,1)S(1)}) custom-call(bf16[128,1024]{1,0:T(8,128)(2,1)} %recording.1, bf16[128,1024]{1,0:T(8,128)(2,1)} %trailing.1, bf16[2,2048,512]{2,1,0:T(8,128)(2,1)} %constant.2.clone.tables), custom_call_target="tpu_custom_call" | custom-call | tf_op jit(solution)/shard_map/begin_transform/pallas_call | solution.py:268
  9.3 0.0 copy-start.1
  9.3 0.0 collective-permute-done.3
  9.3 1.9 %collective-permute-done.2 = bf16[64,128]{1,0:T(8,128)(2,1)S(1)} collective-permute-done((bf16[64,128]{1,0:T(8,128)(2,1)}, bf16[64,128]{1,0:T(8,128)(2,1)S(1)}, u32[]{:S(2)}, u32[]{:S(2)}) %collective-permute-start.2) | collective-permute-done | bytes 16416 | tf_op jit(solution)/shard_map/ppermute | solution.py:261
  11.3 0.0 collective-permute-done.1
  11.3 0.0 collective-permute-done.refs_0_
  11.3 0.5 %finish_transform.1 = (bf16[128,512]{1,0:T(8,128)(2,1)S(1)}, bf16[128,512]{1,0:T(8,128)(2,1)S(1)}, bf16[256,512]{1,0:T(8,128)(2,1)S(1)}) custom-call(bf16[128,1024]{1,0:T(8,128)(2,1)S(1)} %collective-permute-done.refs_0_, bf16[2048,512]{1,0:T(8,128)(2,1)S(1)} %get-tuple-element.21.refs_1_, f32[128,1024]{1,0:T(8,128)S(1)} %get-tuple-element.22.refs_2_), custom_call_target="tpu_custom_call" | custom-call | tf_op jit(solution)/shard_map/finish_transform/pallas_call | solution.py:291
  11.8 0.0 copy-start
  11.8 0.1 collective-permute-start.7
  11.9 0.1 collective-permute-start.4
  11.9 2.8 %collective-permute-start.5 = (bf16[128,512]{1,0:T(8,128)(2,1)S(1)}, bf16[128,512]{1,0:T(8,128)(2,1)S(1)}, u32[]{:S(2)}, u32[]{:S(2)}) collective-permute-start(bf16[128,512]{1,0:T(8,128)(2,1)S(1)} %get-tuple-element.23.own), channel_id=1, source_target_pairs={{0,8},{8,12},{12,4},{4,0},{1,9},{9,13},{13,5},{5,1},{2,10},{10,14}... | collective-permute-start | bytes 393224 | tf_op jit(solution)/shard_map/ppermute | solution.py:330
  14.8 0.2 collective-permute-start.6
  14.9 0.0 collective-permute-done.4.other
  15.0 0.7 %collective-permute-start.10 = (bf16[256,512]{1,0:T(8,128)(2,1)S(1)}, bf16[256,512]{1,0:T(8,128)(2,1)S(1)}, u32[]{:S(2)}, u32[]{:S(2)}) collective-permute-start(bf16[256,512]{1,0:T(8,128)(2,1)S(1)} %block.1.raw), channel_id=1, source_target_pairs={{4,8},{8,4},{5,9},{9,5},{6,10},{10,6},{7,11},{11,7},{20,24},{24,20... | collective-permute-start | bytes 786440 | tf_op jit(solution)/shard_map/ppermute | solution.py:341
  15.7 6.2 %collective-permute-done.5.first = bf16[128,512]{1,0:T(8,128)(2,1)S(1)} collective-permute-done((bf16[128,512]{1,0:T(8,128)(2,1)S(1)}, bf16[128,512]{1,0:T(8,128)(2,1)S(1)}, u32[]{:S(2)}, u32[]{:S(2)}) %collective-permute-start.5) | collective-permute-done | bytes 131104 | tf_op jit(solution)/shard_map/ppermute | solution.py:330
  21.9 1.3 %collective-permute-start.11 = (bf16[128,512]{1,0:T(8,128)(2,1)S(1)}, bf16[128,512]{1,0:T(8,128)(2,1)S(1)}, u32[]{:S(2)}, u32[]{:S(2)}) collective-permute-start(bf16[128,512]{1,0:T(8,128)(2,1)S(1)} %collective-permute-done.5.first), channel_id=1, source_target_pairs={{4,0},{8,12},{5,1},{9,13},{6,2},{10,14},{7,3},{11,15},{20,16},{24,... | collective-permute-start | bytes 393224 | tf_op jit(solution)/shard_map/ppermute | solution.py:342
  23.2 1.5 %collective-permute-done.6.first_other = bf16[128,512]{1,0:T(8,128)(2,1)S(1)} collective-permute-done((bf16[128,512]{1,0:T(8,128)(2,1)S(1)}, bf16[128,512]{1,0:T(8,128)(2,1)S(1)}, u32[]{:S(2)}, u32[]{:S(2)}) %collective-permute-start.6) | collective-permute-done | bytes 131104 | tf_op jit(solution)/shard_map/ppermute | solution.py:329
  24.7 1.3 %collective-permute-start.12 = (bf16[128,512]{1,0:T(8,128)(2,1)S(1)}, bf16[128,512]{1,0:T(8,128)(2,1)S(1)}, u32[]{:S(2)}, u32[]{:S(2)}) collective-permute-start(bf16[128,512]{1,0:T(8,128)(2,1)S(1)} %collective-permute-done.6.first_other), channel_id=1, source_target_pairs={{4,0},{8,12},{5,1},{9,13},{6,2},{10,14},{7,3},{11,15},{20,16},{24,... | collective-permute-start | bytes 393224 | tf_op jit(solution)/shard_map/ppermute | solution.py:342
  26.0 0.0 collective-permute-done.7.value.second
  26.0 0.2 collective-permute-start.8
  26.2 0.0 copy-done.1
  26.2 0.5 %collective-permute-start.9 = (bf16[4,64,128]{2,1,0:T(8,128)(2,1)S(1)}, bf16[4,64,128]{2,1,0:T(8,128)(2,1)S(1)}, u32[]{:S(2)}, u32[]{:S(2)}) collective-permute-start(bf16[4,64,128]{2,1,0:T(8,128)(2,1)S(1)} %pad_maximum_fusion.refs_0_), channel_id=1, source_target_pairs={{0,1},{1,0},{2,3},{3,2},{4,5},{5,4},{6,7},{7,6},{8,9},{9,8},{10,11... | collective-permute-start | bytes 196616 | tf_op jit(solution)/shard_map/ppermute | solution.py:34
  26.7 0.9 %collective-permute-done.9.refs_1_ = bf16[4,64,128]{2,1,0:T(8,128)(2,1)S(1)} collective-permute-done((bf16[4,64,128]{2,1,0:T(8,128)(2,1)S(1)}, bf16[4,64,128]{2,1,0:T(8,128)(2,1)S(1)}, u32[]{:S(2)}, u32[]{:S(2)}) %collective-permute-start.9) | collective-permute-done | bytes 65568 | tf_op jit(solution)/shard_map/ppermute | solution.py:34
  27.6 0.3 band_matrix.1.band
  27.9 0.0 collective-permute-done.8.second_other
  27.9 1.0 %early_whitening.1 = (bf16[1152,512]{1,0:T(8,128)(2,1)S(1)}, bf16[4,256,512]{2,1,0:T(8,128)(2,1)S(1)}, f32[256,512]{1,0:T(8,128)S(1)}, bf16[256,256]{1,0:T(8,128)(2,1)S(1)}) custom-call(bf16[256,512]{1,0:T(8,128)(2,1)S(1)} %block.1.raw, bf16[128,512]{1,0:T(8,128)(2,1)S(1)} %collective-permute-done.5.first, ...), custom_call_target="tpu_custom_call" | custom-call | tf_op jit(solution)/shard_map/early_whitening/pallas_call | solution.py:357
  28.9 0.4 %collective-permute-done.11.fourth = bf16[128,512]{1,0:T(8,128)(2,1)S(1)} collective-permute-done((bf16[128,512]{1,0:T(8,128)(2,1)S(1)}, bf16[128,512]{1,0:T(8,128)(2,1)S(1)}, u32[]{:S(2)}, u32[]{:S(2)}) %collective-permute-start.11) | collective-permute-done | bytes 131104 | tf_op jit(solution)/shard_map/ppermute | solution.py:342
  29.3 2.8 %collective-permute-done.12.fourth_other = bf16[128,512]{1,0:T(8,128)(2,1)S(1)} collective-permute-done((bf16[128,512]{1,0:T(8,128)(2,1)S(1)}, bf16[128,512]{1,0:T(8,128)(2,1)S(1)}, u32[]{:S(2)}, u32[]{:S(2)}) %collective-permute-start.12) | collective-permute-done | bytes 131104 | tf_op jit(solution)/shard_map/ppermute | solution.py:342
  32.1 0.0 collective-permute-done.10.third
  32.1 0.0 copy-done
  32.1 2.5 %cross.1 = f32[4,2,256,256]{3,2,1,0:T(8,128)} custom-call(s32[1,4]{1,0:T(1,128)S(1)} %copy-done, bf16[1152,512]{1,0:T(8,128)(2,1)S(1)} %get-tuple-element.29.padded, bf16[4,256,512]{2,1,0:T(8,128)(2,1)S(1)} %get-tuple-element.30.early, f32[256,512]{1,0:T(8,128)S(1)} %get-tuple-element.31.beside, bf16[256,256]{1,0:T(8,128)(2,1)S(1)} %get-tuple-element.32.middle, ...), custom_call_target="tpu_custom_call" | custom-call | tf_op jit(solution)/shard_map/cross/pallas_call | solution.py:376
  (3 shorter events, 0.0 us)
Async XLA Ops:
  0.0 11.3 %collective-permute-start = (bf16[128,1024]{1,0:T(8,128)(2,1)}, bf16[128,1024]{1,0:T(8,128)(2,1)S(1)}, u32[]{:S(2)}, u32[]{:S(2)}) collective-permute-start(bf16[128,1024]{1,0:T(8,128)(2,1)} %recording.1), channel_id=1, source_target_pairs={{0,2},{2,0},{1,3},{3,1},{4,6},{6,4},{5,7},{7,5},{8,10},{10,8},{9,1... | collective-permute-start | bytes 786440 | tf_op jit(solution)/shard_map/ppermute | solution.py:256
  2.9 6.4 %collective-permute-start.3 = (bf16[64,128]{1,0:T(8,128)(2,1)}, bf16[64,128]{1,0:T(8,128)(2,1)S(1)}, u32[]{:S(2)}, u32[]{:S(2)}) collective-permute-start(bf16[64,128]{1,0:T(8,128)(2,1)} %bitcast.9), channel_id=1, source_target_pairs={{0,8},{4,12},{8,0},{12,4},{1,9},{5,13},{9,1},{13,5},{2,10},{6,14},... | collective-permute-start | bytes 49160 | tf_op jit(solution)/shard_map/ppermute | solution.py:261
  5.5 5.7 %collective-permute-start.2 = (bf16[64,128]{1,0:T(8,128)(2,1)}, bf16[64,128]{1,0:T(8,128)(2,1)S(1)}, u32[]{:S(2)}, u32[]{:S(2)}) collective-permute-start(bf16[64,128]{1,0:T(8,128)(2,1)} %bitcast.10), channel_id=1, source_target_pairs={{0,12},{4,8},{8,4},{12,0},{1,13},{5,9},{9,5},{13,1},{2,14},{6,10},... | collective-permute-start | bytes 49160 | tf_op jit(solution)/shard_map/ppermute | solution.py:261
  6.9 4.4 %collective-permute-start.1 = (bf16[64,128]{1,0:T(8,128)(2,1)}, bf16[64,128]{1,0:T(8,128)(2,1)S(1)}, u32[]{:S(2)}, u32[]{:S(2)}) collective-permute-start(bf16[64,128]{1,0:T(8,128)(2,1)} %bitcast.11), channel_id=1, source_target_pairs={{0,4},{4,0},{8,12},{12,8},{1,5},{5,1},{9,13},{13,9},{2,6},{6,2},{1... | collective-permute-start | bytes 49160 | tf_op jit(solution)/shard_map/ppermute | solution.py:261
  9.3 16.9 %copy-start.1 = (bf16[128,64]{0,1:T(8,128)(2,1)S(1)}, bf16[128,64]{0,1:T(8,128)(2,1)}, u32[]{:S(2)}) copy-start(bf16[128,64]{0,1:T(8,128)(2,1)} %param.7) | copy-start | bytes 49156
  11.8 20.3 %copy-start = (s32[1,4]{1,0:T(1,128)S(1)}, s32[1,4]{1,0:T(1,128)}, u32[]{:S(2)}) copy-start(s32[1,4]{1,0:T(1,128)} %slots.1) | copy-start | bytes 52
  11.8 14.2 %collective-permute-start.7 = (bf16[256,512]{1,0:T(8,128)(2,1)S(1)}, bf16[256,512]{1,0:T(8,128)(2,1)S(1)}, u32[]{:S(2)}, u32[]{:S(2)}) collective-permute-start(bf16[256,512]{1,0:T(8,128)(2,1)S(1)} %get-tuple-element.25), channel_id=1, source_target_pairs={{4,12},{12,8},{8,0},{0,4},{5,13},{13,9},{9,1},{1,5},{6,14},{14,10}... | collective-permute-start | bytes 786440 | tf_op jit(solution)/shard_map/ppermute | solution.py:331
  11.9 3.1 %collective-permute-start.4 = (bf16[128,512]{1,0:T(8,128)(2,1)S(1)}, bf16[128,512]{1,0:T(8,128)(2,1)S(1)}, u32[]{:S(2)}, u32[]{:S(2)}) collective-permute-start(bf16[128,512]{1,0:T(8,128)(2,1)S(1)} %get-tuple-element.24), channel_id=1, source_target_pairs={{0,1},{1,0},{2,3},{3,2},{4,5},{5,4},{6,7},{7,6},{8,9},{9,8},{10,11... | collective-permute-start | bytes 393224 | tf_op jit(solution)/shard_map/ppermute | solution.py:34
  11.9 10.0 %collective-permute-start.5 = (bf16[128,512]{1,0:T(8,128)(2,1)S(1)}, bf16[128,512]{1,0:T(8,128)(2,1)S(1)}, u32[]{:S(2)}, u32[]{:S(2)}) collective-permute-start(bf16[128,512]{1,0:T(8,128)(2,1)S(1)} %get-tuple-element.23.own), channel_id=1, source_target_pairs={{0,8},{8,12},{12,4},{4,0},{1,9},{9,13},{13,5},{5,1},{2,10},{10,14}... | collective-permute-start | bytes 393224 | tf_op jit(solution)/shard_map/ppermute | solution.py:330
  14.8 9.9 %collective-permute-start.6 = (bf16[128,512]{1,0:T(8,128)(2,1)S(1)}, bf16[128,512]{1,0:T(8,128)(2,1)S(1)}, u32[]{:S(2)}, u32[]{:S(2)}) collective-permute-start(bf16[128,512]{1,0:T(8,128)(2,1)S(1)} %get-tuple-element.24), channel_id=1, source_target_pairs={{0,9},{1,8},{8,13},{9,12},{12,5},{13,4},{4,1},{5,0},{2,11},{3,10},... | collective-permute-start | bytes 393224 | tf_op jit(solution)/shard_map/ppermute | solution.py:329
  15.0 17.1 %collective-permute-start.10 = (bf16[256,512]{1,0:T(8,128)(2,1)S(1)}, bf16[256,512]{1,0:T(8,128)(2,1)S(1)}, u32[]{:S(2)}, u32[]{:S(2)}) collective-permute-start(bf16[256,512]{1,0:T(8,128)(2,1)S(1)} %block.1.raw), channel_id=1, source_target_pairs={{4,8},{8,4},{5,9},{9,5},{6,10},{10,6},{7,11},{11,7},{20,24},{24,20... | collective-permute-start | bytes 786440 | tf_op jit(solution)/shard_map/ppermute | solution.py:341
  21.9 7.4 %collective-permute-start.11 = (bf16[128,512]{1,0:T(8,128)(2,1)S(1)}, bf16[128,512]{1,0:T(8,128)(2,1)S(1)}, u32[]{:S(2)}, u32[]{:S(2)}) collective-permute-start(bf16[128,512]{1,0:T(8,128)(2,1)S(1)} %collective-permute-done.5.first), channel_id=1, source_target_pairs={{4,0},{8,12},{5,1},{9,13},{6,2},{10,14},{7,3},{11,15},{20,16},{24,... | collective-permute-start | bytes 393224 | tf_op jit(solution)/shard_map/ppermute | solution.py:342
  24.7 7.4 %collective-permute-start.12 = (bf16[128,512]{1,0:T(8,128)(2,1)S(1)}, bf16[128,512]{1,0:T(8,128)(2,1)S(1)}, u32[]{:S(2)}, u32[]{:S(2)}) collective-permute-start(bf16[128,512]{1,0:T(8,128)(2,1)S(1)} %collective-permute-done.6.first_other), channel_id=1, source_target_pairs={{4,0},{8,12},{5,1},{9,13},{6,2},{10,14},{7,3},{11,15},{20,16},{24,... | collective-permute-start | bytes 393224 | tf_op jit(solution)/shard_map/ppermute | solution.py:342
  26.0 1.9 %collective-permute-start.8 = (bf16[128,512]{1,0:T(8,128)(2,1)S(1)}, bf16[128,512]{1,0:T(8,128)(2,1)S(1)}, u32[]{:S(2)}, u32[]{:S(2)}) collective-permute-start(bf16[128,512]{1,0:T(8,128)(2,1)S(1)} %lower_rows.1), channel_id=1, source_target_pairs={{0,1},{1,0},{2,3},{3,2},{4,5},{5,4},{6,7},{7,6},{8,9},{9,8},{10,11... | collective-permute-start | bytes 393224 | tf_op jit(solution)/shard_map/ppermute | solution.py:34
  26.2 1.4 %collective-permute-start.9 = (bf16[4,64,128]{2,1,0:T(8,128)(2,1)S(1)}, bf16[4,64,128]{2,1,0:T(8,128)(2,1)S(1)}, u32[]{:S(2)}, u32[]{:S(2)}) collective-permute-start(bf16[4,64,128]{2,1,0:T(8,128)(2,1)S(1)} %pad_maximum_fusion.refs_0_), channel_id=1, source_target_pairs={{0,1},{1,0},{2,3},{3,2},{4,5},{5,4},{6,7},{7,6},{8,9},{9,8},{10,11... | collective-permute-start | bytes 196616 | tf_op jit(solution)/shard_map/ppermute | solution.py:34
